TPU v7x, 256 devices: a whole 4x4x8 slice. The times are simulated.
256 devices in a mesh: blk: 64 (over x, z, y_hi), rows: 4 (over y_lo, core).
Axes of the slice: x: 4, y: 4 (y_hi: 2, y_lo: 2; y = y_hi * 2 + y_lo), z: 8, core: 2. Of those that a mesh axis runs over, the one named last changes fastest.
Arguments:
- features: bfloat16 [65536, 2048], P(('blk', 'rows')), may hold values from -24 to 24
- head_weight: bfloat16 [2048, 768], replicated, may hold values from -0.0048828125 to 0.0048828125
- labels: int32 [65536], P(('blk', 'rows')), may hold values from 0 to 11317
- pos_index: int32 [65536, 3], P(('blk', 'rows')), may hold values from 0 to 1023
- pair_mask: int32 [64, 3], P('blk'), may hold values from 0 to 1, as said below
- loss_weight: float32 [65536], P(('blk', 'rows')), may hold values from 0.25 to 1
Outputs:
- anchor_loss: float32 [65536], P(('blk', 'rows'))
- weight_grad: float32 [2048, 768], P(('blk', 'rows'))
Inputs may be any that keep to these rules, and one draw needn't show every extreme that they name: `pair_mask`: entry [t, s] is 1 where anchor tile t scores the rows of tile (t - s) mod 64, else 0. The rows of tiles 0 to 2 and of tile 64 - 1 are all ones.
All inputs are finite; a program needn't handle non-finite values.
Results may differ from a plain program's by a relative error of at most 0.0034.
Values may be sent and summed in bfloat16 or wider, within the bound.
No kernel may reach another device: no remote copies, remote signals or barrier semaphores. Data moves between devices by JAX's collectives and lax.ppermute only.
A program may use at most 128 MiB of HBM per device.

v0:
```python
import jax
import jax.numpy as jnp
from jax import lax
from jax.sharding import PartitionSpec as P

SMOOTHING_SCALE = 16.0
SLACK_GAP = 0.1


def passed_along(block, axis, distance):
    devices = range(lax.axis_size(axis))
    route = [((i - distance) % len(devices), i) for i in devices]
    return lax.ppermute(block, axis, route)


def score_tile(
    anchors, anchor_sq, anchor_labels, matching_separation, weights, tile_rows, tile_labels, listed
):
    matching_samples = matching_separation.shape[1]
    block_tally = tile_rows.shape[0]
    anchor_count = anchors.shape[0]

    def compute(unused):
        products = lax.dot_general(
            anchors, tile_rows, (((1,), (1,)), ((), ())), preferred_element_type=jnp.float32
        )
        widened = tile_rows.astype(jnp.float32)
        tile_sq = jnp.sum(widened * widened, axis=1)
        couple_separation = anchor_sq[:, None] + tile_sq[None, :] - 2.0 * products
        valid = (anchor_labels[:, None] != tile_labels[None, :]).astype(jnp.float32)
        weighting = weights / (matching_samples * block_tally)
        objective_accrued = jnp.zeros((anchor_count,), jnp.float32)
        coefficient = jnp.zeros((anchor_count, block_tally), jnp.float32)
        totals = []
        for target_slot in range(matching_samples):
            slack_excess = SMOOTHING_SCALE * (
                matching_separation[:, target_slot : target_slot + 1]
                - couple_separation
                + SLACK_GAP
            )
            objective_accrued = objective_accrued + jnp.sum(
                valid * jax.nn.softplus(slack_excess), axis=1
            )
            sigmoids = valid * jax.nn.sigmoid(slack_excess)
            coefficient = coefficient + sigmoids
            totals.append(jnp.sum(sigmoids, axis=1))
        objective_accrued = objective_accrued / (SMOOTHING_SCALE * matching_samples * block_tally)
        coefficient = coefficient * weighting[:, None]
        pos_coef = jnp.stack(totals, axis=1) * weighting[:, None]
        coef_low = coefficient.astype(jnp.bfloat16)
        anchor_grad = 2.0 * jnp.dot(coef_low, tile_rows, preferred_element_type=jnp.float32)
        pulled = lax.dot_general(
            coef_low, anchors, (((0,), (0,)), ((), ())), preferred_element_type=jnp.float32
        )
        col_sums = jnp.sum(coefficient, axis=0)
        tile_grad = 2.0 * (pulled - col_sums[:, None] * widened)
        return (objective_accrued, pos_coef, anchor_grad, tile_grad, coef_low, col_sums)

    def skip(unused):
        return (
            jnp.zeros((anchor_count,), jnp.float32),
            jnp.zeros((anchor_count, matching_samples), jnp.float32),
            jnp.zeros((anchor_count, anchors.shape[1]), jnp.float32),
            jnp.zeros((block_tally, anchors.shape[1]), jnp.float32),
            jnp.zeros((anchor_count, block_tally), jnp.bfloat16),
            jnp.zeros((block_tally,), jnp.float32),
        )

    return lax.cond(listed, compute, skip, 0)


def local(features, head_weight, labels, pos_index, pair_mask, loss_weight):
    embedded = jnp.dot(features, head_weight, preferred_element_type=jnp.float32).astype(
        jnp.bfloat16
    )
    widened = embedded.astype(jnp.float32)
    anchor_sq = jnp.sum(widened * widened, axis=1)
    tile_rows, tile_labels = (
        lax.all_gather(embedded, "rows", axis=0, tiled=True),
        lax.all_gather(labels, "rows", axis=0, tiled=True),
    )
    pos_rows = tile_rows[pos_index]
    pos_wide = pos_rows.astype(jnp.float32)
    pos_sq = jnp.sum(pos_wide * pos_wide, axis=2)
    matching_separation = (
        anchor_sq[:, None]
        + pos_sq
        - 2.0 * jnp.einsum("ad,akd->ak", embedded, pos_rows, preferred_element_type=jnp.float32)
    )
    offsets = pair_mask.shape[1]
    loss_total, coef_total, grad_total, own_term, first_low, first_sums = score_tile(
        embedded,
        anchor_sq,
        labels,
        matching_separation,
        loss_weight,
        tile_rows,
        tile_labels,
        pair_mask[0, 0] > 0,
    )
    received = jnp.zeros_like(own_term)
    walk_rows, walk_labels = (tile_rows, tile_labels)
    for offset in range(1, offsets):
        walk_rows, walk_labels = passed_along((walk_rows, walk_labels), "blk", 1)
        loss_part, coef_part, grad_part, term_part, low_part, sums_part = score_tile(
            embedded,
            anchor_sq,
            labels,
            matching_separation,
            loss_weight,
            walk_rows,
            walk_labels,
            pair_mask[0, offset] > 0,
        )
        loss_total = loss_total + loss_part
        coef_total = coef_total + coef_part
        grad_total = grad_total + grad_part
        received = received + passed_along(term_part.astype(jnp.bfloat16), "blk", -offset).astype(
            term_part.dtype
        )
    grad_total = grad_total - 2.0 * jnp.sum(coef_total[:, :, None] * pos_wide, axis=1)
    pushed = 2.0 * coef_total[:, :, None] * (pos_wide - widened[:, None, :])
    own_term = own_term.at[pos_index.reshape(-1)].add(pushed.reshape(-1, pushed.shape[2]))
    quarter_sum = lax.psum_scatter(own_term + received, "rows", scatter_dimension=0, tiled=True)
    emb_grad = grad_total + quarter_sum
    grad_low = emb_grad.astype(jnp.bfloat16)
    weight_grad = lax.psum_scatter(
        lax.dot_general(
            features, grad_low, (((0,), (0,)), ((), ())), preferred_element_type=jnp.float32
        ),
        ("blk", "rows"),
        scatter_dimension=0,
        tiled=True,
    )
    return (loss_total, weight_grad)


def solution(mesh):
    return jax.shard_map(
        local,
        mesh=mesh,
        in_specs=(
            P(("blk", "rows"), None),
            P(),
            P(("blk", "rows")),
            P(("blk", "rows"), None),
            P("blk", None),
            P(("blk", "rows")),
        ),
        out_specs=(P(("blk", "rows")), P(("blk", "rows"), None)),
        check_vma=False,
    )
```

profile of v0, /device:TPU:8, one launch (start us, length us, event | category | flops | bytes accessed | tf_op | source)
XLA Modules:
  0.0 712.5 jit_solution(14131492475354479606)
XLA Ops:
  7.3 1.8 copy-done
  9.1 3.5 multiply_reduce_fusion
  12.7 28.8 %all-gather.3.cloned.1.call-done = bf16[1024,768]{1,0:T(8,128)(2,1)} async-done(((bf16[256,768]{1,0:T(8,128)(2,1)}), bf16[1024,768]{1,0:T(8,128)(2,1)}) %all-gather.3.cloned.1.call-update) | async-done | bytes 1572880 | tf_op jit(solution)/shard_map/all_gather | solution.py:79
  41.5 2.9 collective-permute-start.1
  44.4 40.1 %collective-permute-done.1 = bf16[1024,768]{1,0:T(8,128)(2,1)} collective-permute-done((bf16[1024,768]{1,0:T(8,128)(2,1)}, bf16[1024,768]{1,0:T(8,128)(2,1)}, u32[]{:S(2)}, u32[]{:S(2)}) %collective-permute-start.1) | collective-permute-done | bytes 1572896 | tf_op jit(solution)/shard_map/ppermute | solution.py:13
  84.5 37.1 %all-gather = s32[4,1,256]{2,1,0:T(1,128)S(1)} all-gather(s32[1,1,256]{2,1,0:T(1,128)S(1)} %bitcast.56), channel_id=1, replica_groups=mesh['blk'=64,'rows'=4] {'rows'}, dimensions={0}, use_global_device_ids=true | all-gather | bytes 5120 | tf_op jit(solution)/shard_map/all_gather | solution.py:80
  123.8 7.2 %collective-permute-done = s32[1024]{0:T(1024)} collective-permute-done((s32[1024]{0:T(1024)S(1)}, s32[1024]{0:T(1024)}, u32[]{:S(2)}, u32[]{:S(2)}) %collective-permute-start) | collective-permute-done | bytes 4128 | tf_op jit(solution)/shard_map/ppermute | solution.py:13
  131.0 5.6 gather_fusion
  136.6 3.8 reshape.82
  140.4 3.7 fusion.41
  145.0 3.0 fusion.36
  149.7 13.6 %conditional.4 = (f32[256]{0:T(256)S(1)}, f32[256,3]{0,1:T(4,128)S(1)}, f32[256,768]{1,0:T(8,128)S(1)}, bf16[1024,768]{1,0:T(8,128)(2,1)}) conditional(s32[]{:T(128)} %bitcast.23, () %tuple.34, (s32[256]{0:T(256)}, s32[1024]{0:T(1024)}, f32[256,3]{0,1:T(4,128)S(1)}, f32[256]{0:T(256)}, bf16[1024,768]{1,0:T(8,128)(2,1)}, ...), branch_computations={%region_12.13_spmd, %region_13.22_spmd} | conditional | flops 1229389568 | bytes 11062304 | solution.py:69
  152.4 5.6 fusion.48
  158.0 2.0 convolution_multiply_fusion.3
  160.0 3.3 fusion.14
  163.3 7.7 %collective-permute-start.4 = (bf16[1024,768]{1,0:T(8,128)(2,1)}, bf16[1024,768]{1,0:T(8,128)(2,1)}, u32[]{:S(2)}, u32[]{:S(2)}) collective-permute-start(bf16[1024,768]{1,0:T(8,128)(2,1)} %get-tuple-element.87), channel_id=1, source_target_pairs={{4,0},{8,4},{12,8},{16,12},{20,16},{24,20},{28,24},{32,28},{36,32}... | collective-permute-start | bytes 4718600 | tf_op jit(solution)/shard_map/ppermute | solution.py:13
  171.1 15.4 %conditional.5 = (f32[256]{0:T(256)}, f32[256,3]{0,1:T(4,128)S(1)}, f32[256,768]{1,0:T(8,128)}, bf16[1024,768]{1,0:T(8,128)(2,1)}) conditional(s32[]{:T(128)} %bitcast.24, () %tuple.36, (s32[256]{0:T(256)}, s32[1024]{0:T(1024)}, f32[256,3]{0,1:T(4,128)S(1)}, f32[256]{0:T(256)}, bf16[1024,768]{1,0:T(8,128)(2,1)}, ...), branch_computations={%region_22.23_spmd, %region_23.32_spmd} | conditional | flops 1229389568 | bytes 11062304 | solution.py:69
  174.1 5.6 fusion.49
  180.2 2.9 convolution_multiply_fusion.5
  183.1 3.4 fusion.26
  190.6 12.4 %conditional.3 = (f32[256]{0:T(256)S(1)}, f32[256,3]{0,1:T(4,128)S(1)}, f32[256,768]{1,0:T(8,128)}, f32[1024,768]{1,0:T(8,128)}) conditional(s32[]{:T(128)} %bitcast.18, () %tuple.32, (s32[256]{0:T(256)}, s32[1024]{0:T(1024)}, f32[256,3]{0,1:T(4,128)S(1)}, f32[256]{0:T(256)}, bf16[1024,768]{1,0:T(8,128)(2,1)}, ...), branch_computations={%region_2.0_spmd, %region_3.12_spmd} | conditional | flops 1228603136 | bytes 18926652 | solution.py:69
  193.3 5.7 fusion.47
  200.5 2.4 fusion.2
  203.8 5.7 fusion.37
  209.5 4.6 sub.130
  214.5 23.3 %collective-permute-done.5 = bf16[1024,768]{1,0:T(8,128)(2,1)} collective-permute-done((bf16[1024,768]{1,0:T(8,128)(2,1)}, bf16[1024,768]{1,0:T(8,128)(2,1)}, u32[]{:S(2)}, u32[]{:S(2)}) %collective-permute-start.5) | collective-permute-done | bytes 1572896 | tf_op jit(solution)/shard_map/ppermute | solution.py:13
  237.8 5.0 add_add_fusion
  242.7 13.6 %scatter_custom_fusion = f32[1024,768]{1,0:T(8,128)} fusion(f32[1024,768]{1,0:T(8,128)} %add_add_fusion, s32[768]{0:T(1024)} %fusion.45, f32[768,768]{1,0:T(8,128)} %sub.130, f32[768]{0:T(1024)S(1)} %mul.236), kind=kCustom, calls=%fused_computation.105 | custom fusion | flops 1179648 | bytes 5508096 | tf_op jit(solution)/shard_map/scatter-add | solution.py:123
  256.5 35.2 %reduce-scatter.5.cloned.1.call-done = f32[256,768]{1,0:T(8,128)} async-done(((f32[1024,768]{1,0:T(8,128)}), f32[256,768]{1,0:T(8,128)}) %reduce-scatter.5.cloned.1.call-update) | async-done | bytes 786448 | tf_op jit(solution)/shard_map/reduce_scatter | solution.py:124
  291.6 6.2 convolution_bitcast_fusion
  297.8 6.5 copy.34
  306.3 399.5 %reduce-scatter.7.cloned.1.call-done = f32[8,768]{1,0:T(8,128)} async-done(((f32[2048,768]{1,0:T(8,128)}), f32[8,768]{1,0:T(8,128)}) %reduce-scatter.7.cloned.1.call-update) | async-done | bytes 24592
  (69 shorter events, 19.8 us)
Async XLA Ops:
  7.2 1.9 copy-start
  7.2 77.3 %copy-start.7 = (s32[256]{0:T(256)S(1)}, s32[256]{0:T(256)}, u32[]{:S(2)}) copy-start(s32[256]{0:T(256)} %param.14) | copy-start | bytes 3076
  7.2 114.3 %copy-start.4 = (s32[256,3]{0,1:T(4,128)S(1)}, s32[256,3]{0,1:T(4,128)}, u32[]{:S(2)}) copy-start(s32[256,3]{0,1:T(4,128)} %param.15) | copy-start | bytes 9220
  7.2 114.7 %copy-start.5 = (s32[1,3]{1,0:T(1,128)S(1)}, s32[1,3]{1,0:T(1,128)}, u32[]{:S(2)}) copy-start(s32[1,3]{1,0:T(1,128)} %param.16) | copy-start | bytes 40
  7.2 34.3 %all-gather.3.cloned.1.call-start = ((), (), s32[]{:S(2)}) async-start(), calls=%async_computation.2 | async-start | bytes 1966080 | tf_op jit(solution)/shard_map/all_gather | solution.py:79
  12.6 279.0 %reduce-scatter.5.cloned.1.call-start = ((), (), s32[]{:S(2)}) async-start(), calls=%async_computation.3 | async-start | bytes 3932160 | tf_op jit(solution)/shard_map/reduce_scatter | solution.py:124
  41.5 43.0 %collective-permute-start.1 = (bf16[1024,768]{1,0:T(8,128)(2,1)}, bf16[1024,768]{1,0:T(8,128)(2,1)}, u32[]{:S(2)}, u32[]{:S(2)}) collective-permute-start(bf16[1024,768]{1,0:T(8,128)(2,1)} %all-gather.3.cloned.1.call-done), channel_id=1, source_target_pairs={{252,0},{0,4},{4,8},{8,12},{12,16},{16,20},{20,24},{24,28},{28,32}... | collective-permute-start | bytes 4718600 | tf_op jit(solution)/shard_map/ppermute | solution.py:13
  84.5 86.6 %collective-permute-start.3 = (bf16[1024,768]{1,0:T(8,128)(2,1)}, bf16[1024,768]{1,0:T(8,128)(2,1)}, u32[]{:S(2)}, u32[]{:S(2)}) collective-permute-start(bf16[1024,768]{1,0:T(8,128)(2,1)} %collective-permute-done.1), channel_id=1, source_target_pairs={{252,0},{0,4},{4,8},{8,12},{12,16},{16,20},{20,24},{24,28},{28,32}... | collective-permute-start | bytes 4718600 | tf_op jit(solution)/shard_map/ppermute | solution.py:13
  121.5 9.4 %copy-start.6 = (s32[4,1,256]{2,1,0:T(1,128)}, s32[4,1,256]{2,1,0:T(1,128)S(1)}, u32[]{:S(2)}) copy-start(s32[4,1,256]{2,1,0:T(1,128)S(1)} %all-gather) | copy-start | bytes 12292
  121.5 9.4 %collective-permute-start = (s32[1024]{0:T(1024)S(1)}, s32[1024]{0:T(1024)}, u32[]{:S(2)}, u32[]{:S(2)}) collective-permute-start(s32[1024]{0:T(1024)S(1)} %bitcast.54), channel_id=1, source_target_pairs={{252,0},{0,4},{4,8},{8,12},{12,16},{16,20},{20,24},{24,28},{28,32}... | collective-permute-start | bytes 12296 | tf_op jit(solution)/shard_map/ppermute | solution.py:13
  131.0 40.1 %collective-permute-start.2 = (s32[1024]{0:T(1024)}, s32[1024]{0:T(1024)}, u32[]{:S(2)}, u32[]{:S(2)}) collective-permute-start(s32[1024]{0:T(1024)} %collective-permute-done), channel_id=1, source_target_pairs={{252,0},{0,4},{4,8},{8,12},{12,16},{16,20},{20,24},{24,28},{28,32}... | collective-permute-start | bytes 12296 | tf_op jit(solution)/shard_map/ppermute | solution.py:13
  136.6 3.8 copy-start.3
  163.3 7.8 %copy-start.8 = (f32[256]{0:T(256)}, f32[256]{0:T(256)S(1)}, u32[]{:S(2)}) copy-start(f32[256]{0:T(256)S(1)} %get-tuple-element.78) | copy-start | bytes 3076
  163.3 7.8 %copy-start.2 = (f32[256,768]{1,0:T(8,128)}, f32[256,768]{1,0:T(8,128)S(1)}, u32[]{:S(2)}) copy-start(f32[256,768]{1,0:T(8,128)S(1)} %get-tuple-element.81) | copy-start | bytes 2359300
  163.3 51.2 %collective-permute-start.4 = (bf16[1024,768]{1,0:T(8,128)(2,1)}, bf16[1024,768]{1,0:T(8,128)(2,1)}, u32[]{:S(2)}, u32[]{:S(2)}) collective-permute-start(bf16[1024,768]{1,0:T(8,128)(2,1)} %get-tuple-element.87), channel_id=1, source_target_pairs={{4,0},{8,4},{12,8},{16,12},{20,16},{24,20},{28,24},{32,28},{36,32}... | collective-permute-start | bytes 4718600 | tf_op jit(solution)/shard_map/ppermute | solution.py:13
  186.5 51.3 %collective-permute-start.5 = (bf16[1024,768]{1,0:T(8,128)(2,1)}, bf16[1024,768]{1,0:T(8,128)(2,1)}, u32[]{:S(2)}, u32[]{:S(2)}) collective-permute-start(bf16[1024,768]{1,0:T(8,128)(2,1)} %get-tuple-element.88), channel_id=1, source_target_pairs={{8,0},{12,4},{16,8},{20,12},{24,16},{28,20},{32,24},{36,28},{40,32... | collective-permute-start | bytes 4718600 | tf_op jit(solution)/shard_map/ppermute | solution.py:13
  193.3 5.7 copy-start.1
  203.1 0.6 copy-start.10
  256.4 449.3 %reduce-scatter.7.cloned.1.call-start = ((), (), s32[]{:S(2)}) async-start(), calls=%async_computation.4 | async-start | bytes 6316032
  304.4 0.7 copy-start.9
  304.4 0.7 copy-start.11
Sparse Core Ops, SparseCore 0:
  12.7 28.7 all-gather.2
  256.5 35.0 reduce-scatter.4
  304.5 401.1 reduce-scatter.6
where the time goes:
time: 719 us; the launch traced here: 713 us
  waiting for transfers between devices  534 us (74%)
  matrix products  45.6 us (6%)
  other arithmetic  38.9 us (5%)
  blocking collectives  37.1 us (5%)
  local copies, waits for them, and re-layouts  28.9 us (4%)
  between operations  16 us (2%)
  starting transfers between devices  10.8 us (2%)
    unnamed x4, waiting for transfers between devices  400 us
    ppermute x6, waiting for transfers between devices, passed_along(): return lax.ppermute(block, axis, route)  70.6 us
    all_gather x1, blocking collectives, local(): lax.all_gather(labels, 'rows', axis=0, tiled=True)  37.1 us
    reduce_scatter x1, waiting for transfers between devices, local(): lax.psum_scatter(own_term + received, 'rows', scatter_dimension=0, tiled=...  35.2 us
    all_gather x1, waiting for transfers between devices, local(): lax.all_gather(embedded, 'rows', axis=0, tiled=True)  28.8 us
    dot_general x3, matrix products, compute(): lax.dot_general(anchors, tile_rows, (((1,), (1,)), ((), ())), preferred_e...  16.8 us
  transfers between devices with their start and end apart: 9, of which 6 were waited for; matrix products, arithmetic and copies ran while one was open for 11% of the time, Pallas kernels for 0%

commit v1 on v0

v1 whole, which is shorter than its diff:
```python
import functools

import jax
import jax.numpy as jnp
from jax import lax
from jax.experimental import pallas as pl
from jax.experimental.pallas import tpu as pltpu
from jax.sharding import PartitionSpec as P

SMOOTHING_SCALE = 16.0
SLACK_GAP = 0.1
LN2 = 0.6931471805599453
BASE2 = SMOOTHING_SCALE / LN2
MASKED = 1e30
META = 16
CHUNK = 16
f32 = jnp.float32
bf16 = jnp.bfloat16

VMEM = pl.BlockSpec(memory_space=pltpu.VMEM)
SMEM = pl.BlockSpec(memory_space=pltpu.SMEM)


def call(kernel, inputs, outs, scratch=(), flops=0, name=None):
    moved = sum(x.size * x.dtype.itemsize for x in inputs)
    moved += sum(x.size * x.dtype.itemsize for x in outs)
    return pl.pallas_call(
        kernel,
        out_shape=outs,
        in_specs=[SMEM if x.ndim == 1 else VMEM for x in inputs],
        out_specs=[VMEM] * len(outs),
        scratch_shapes=list(scratch),
        compiler_params=pltpu.CompilerParams(vmem_limit_bytes=40 << 20),
        cost_estimate=pl.CostEstimate(flops=flops, bytes_accessed=moved, transcendentals=0),
        name=name,
    )(*inputs)


def shape(*dims, dtype=f32):
    return jax.ShapeDtypeStruct(dims, dtype)


def nn(a, b):
    return jnp.dot(a, b, preferred_element_type=f32)


def nt(a, b):
    return lax.dot_general(a, b, (((1,), (1,)), ((), ())), preferred_element_type=f32)


def tn(a, b):
    return lax.dot_general(a, b, (((0,), (0,)), ((), ())), preferred_element_type=f32)


def embed_kernel(features_ref, weight_ref, meta_ref, out_ref):
    rows = features_ref.shape[0]
    out_ref[:rows, :] = nn(features_ref[...], weight_ref[...]).astype(bf16)
    out_ref[rows:, :] = meta_ref[...]


def score_block(
    rows_n, listed, tile, anchors_ref, labels_n, products_ref, coef_ref, lanes_ref, sq_ref, sums_ref
):
    n = rows_n.shape[0]
    wide = rows_n.astype(f32)
    squares = jnp.sum(wide * wide, axis=1, keepdims=True) * BASE2
    sq_ref[...] = jnp.broadcast_to(jnp.where(listed, squares, MASKED), sq_ref.shape)
    lanes_ref[...] = jnp.zeros_like(lanes_ref)
    for i, part in enumerate(tile):
        lanes = slice(i * n, (i + 1) * n)
        products_ref[...] = nt(rows_n, part) * (2.0 * BASE2)
        base = [anchors_ref[k : k + 1, lanes] for k in range(3)]
        weight = anchors_ref[6:7, lanes]
        labels_a = anchors_ref[7:8, lanes]

        def step(c, carry, lanes=lanes, base=base, weight=weight, labels_a=labels_a):
            at = pl.multiple_of(c * CHUNK, CHUNK)
            rows = pl.ds(at, CHUNK)
            q = sq_ref[rows, :1] - products_ref[rows, :]
            q = jnp.where(labels_n[rows, :1] == labels_a, MASKED, q)
            y = [b - q for b in base]
            e = [jnp.exp2(-jnp.abs(v)) for v in y]
            a = [1.0 + v for v in e]
            a01 = a[0] * a[1]
            excess = e[0] + e[1] * a[0] + e[2] * a01
            total = 1.0 + excess
            inverse = 1.0 / total
            log_sum = jnp.log(total) + (excess - (total - 1.0))
            tops = jnp.maximum(y[0], 0.0) + jnp.maximum(y[1], 0.0) + jnp.maximum(y[2], 0.0)
            loss = tops * LN2 + log_sum
            inv2 = inverse * a[2]
            s = [inv2 * a[1], inv2 * a[0], inverse * a01]
            s = [v * jnp.where(w >= 0.0, 1.0, x) for v, w, x in zip(s, y, e)]
            coef = (s[0] + s[1] + s[2]) * weight
            coef_ref[rows, lanes] = coef.astype(bf16)
            folded = coef[:, :128]
            for j in range(128, n, 128):
                folded = folded + coef[:, j : j + 128]
            lanes_ref[rows, :] += folded
            fold = lambda v: jnp.sum(v.reshape(CHUNK // 8, 8, n), axis=0)
            return tuple(x + fold(v) for x, v in zip(carry, (*s, loss)))

        zero = jnp.zeros((8, n), f32)
        sums = lax.fori_loop(0, n // CHUNK, step, (zero,) * 4)
        for k, v in enumerate(sums):
            sums_ref[k : k + 1, lanes] += jnp.sum(v, axis=0, keepdims=True)


def negative_grad(rows_n, tile, coef_ref, lanes_ref):
    n = rows_n.shape[0]
    pulled = sum(nn(coef_ref[:, i * n : (i + 1) * n], part) for i, part in enumerate(tile))
    col_sums = jnp.sum(lanes_ref[...], axis=1, keepdims=True)
    return 2.0 * (pulled - col_sums * rows_n.astype(f32))


def column(row):
    n = row.shape[1]
    eye = lax.broadcasted_iota(jnp.int32, (n, n), 0) == lax.broadcasted_iota(jnp.int32, (n, n), 1)
    return jnp.sum(jnp.where(eye, jnp.broadcast_to(row, (n, n)), 0.0), axis=1, keepdims=True)


def meta_row(ref, n, i):
    return ref[n : n + META, :n].astype(f32)[i : i + 1, :]


def own_kernel(
    scal_ref, p0, p1, p2, p3, anchors_ref, coef_ref, sums_ref, grad_ref,
    products_ref, lanes_ref, sq_ref, label_ref,
):
    blocks = (p0, p1, p2, p3)
    n = p0.shape[0] - META
    me = scal_ref[0]
    scale = 1.0 / (3 * 4 * n)
    tile = [p[:n, :] for p in blocks]
    squares = []
    for part in tile:
        wide = part.astype(f32)
        squares.append(jnp.sum(wide * wide, axis=1, keepdims=True))
    for i, p in enumerate(blocks):
        lanes = slice(i * n, (i + 1) * n)
        meta = p[n : n + META, :n].astype(f32)
        where = []
        for k in range(3):
            holder = meta[2 + k : 3 + k, :].astype(jnp.int32) ^ me
            where.append(holder * n + meta[5 + k : 6 + k, :].astype(jnp.int32))
        found = [jnp.zeros((1, n), f32) for _ in range(3)]
        for j, part in enumerate(tile):
            apart = squares[j] - 2.0 * nt(part, tile[i])
            index = lax.broadcasted_iota(jnp.int32, (n, n), 0) + j * n
            for k in range(3):
                picked = jnp.where(index == where[k], apart, 0.0)
                found[k] = found[k] + jnp.sum(picked, axis=0, keepdims=True)
        for k in range(3):
            anchors_ref[k : k + 1, lanes] = (found[k] + SLACK_GAP) * BASE2
            anchors_ref[3 + k : 4 + k, lanes] = where[k].astype(f32)
        weight = meta[8:9, :] + meta[9:10, :] + meta[10:11, :]
        anchors_ref[6:7, lanes] = weight * scale
        anchors_ref[7:8, lanes] = meta[0:1, :] * 128.0 + meta[1:2, :]
    label_ref[...] = jnp.broadcast_to(column(anchors_ref[7:8, :n]), label_ref.shape)
    sums_ref[...] = jnp.zeros_like(sums_ref)
    score_block(
        tile[0], scal_ref[1] > 0, tile, anchors_ref, label_ref, products_ref, coef_ref, lanes_ref,
        sq_ref, sums_ref,
    )
    grad_ref[...] = negative_grad(tile[0], tile, coef_ref, lanes_ref)


def earlier_kernel(
    scal_ref, n1, n2, p0, p1, p2, p3, anchors_ref, before_ref, coef1, coef2, sums_ref, grad1, grad2,
    products_ref, lanes_ref, sq_ref, label_ref,
):
    n = p0.shape[0] - META
    tile = [p[:n, :] for p in (p0, p1, p2, p3)]
    sums_ref[...] = before_ref[...]
    for s, (p, coef_ref, grad_ref) in enumerate(((n1, coef1, grad1), (n2, coef2, grad2))):
        labels = meta_row(p, n, 0) * 128.0 + meta_row(p, n, 1)
        label_ref[...] = jnp.broadcast_to(column(labels), label_ref.shape)
        rows_n = p[:n, :]
        score_block(
            rows_n, scal_ref[2 + s] > 0, tile, anchors_ref, label_ref, products_ref, coef_ref,
            lanes_ref, sq_ref, sums_ref,
        )
        grad_ref[...] = negative_grad(rows_n, tile, coef_ref, lanes_ref).astype(bf16)
    weight = anchors_ref[6:7, :]
    for k in range(3):
        sums_ref[k : k + 1, :] = sums_ref[k : k + 1, :] * weight


def anchor_kernel(c0, c1, c2, n0, n1, n2, keep_ref, send_ref):
    n = n0.shape[0] - META
    for i, (ref, j) in enumerate(((keep_ref, 0), (send_ref, 0), (keep_ref, 1), (send_ref, 1))):
        lanes = slice(i * n, (i + 1) * n)
        total = tn(c0[:, lanes], n0[:n, :])
        total = total + tn(c1[:, lanes], n1[:n, :]) + tn(c2[:, lanes], n2[:n, :])
        ref[j * n : (j + 1) * n, :] = 2.0 * total


def listed_kernel(anchors_ref, coef_ref, own_where, own_coef, p0, p1, p2, p3, base_ref, out_ref):
    n = p0.shape[0] - META
    tile = [p[:n, :] for p in (p0, p1, p2, p3)]
    total = jnp.zeros(out_ref.shape, f32)
    pushed = jnp.zeros((n, 1), f32)
    for i, part in enumerate(tile):
        lanes = slice(i * n, (i + 1) * n)
        mine = lax.broadcasted_iota(jnp.int32, (n, n), 0).astype(f32)
        others = (lax.broadcasted_iota(jnp.int32, (n, n), 1) + i * n).astype(f32)
        matrix = jnp.zeros((n, n), f32)
        for k in range(3):
            hit = anchors_ref[3 + k : 4 + k, lanes] == mine
            matrix = matrix + jnp.where(hit, coef_ref[k : k + 1, lanes], 0.0)
        pushed = pushed + jnp.sum(matrix, axis=1, keepdims=True)
        for k in range(3):
            hit = own_where[:, k : k + 1] == others
            matrix = matrix + jnp.where(hit, own_coef[:, k : k + 1], 0.0)
        high = matrix.astype(bf16)
        low = (matrix - high.astype(f32)).astype(bf16)
        total = total + nn(high, part) + nn(low, part)
    out_ref[...] = base_ref[...] + 2.0 * (pushed * tile[0].astype(f32) - total)


def head_kernel(f0, f2, f13, g0, g1, g2, g3, out_ref):
    m = f0.shape[0]
    total = nn(f0[...], g0[...]) + nn(f13[:m, :], g1[...])
    total = total + nn(f2[...], g2[...]) + nn(f13[m:, :], g3[...])
    out_ref[...] = total.astype(bf16)


def local(features, head_weight, labels, pos_index, pair_mask, loss_weight):
    blks, rows_n = lax.axis_size("blk"), lax.axis_size("rows")
    me = lax.axis_index("rows")
    n, depth = features.shape
    wide = head_weight.shape[1]
    slice_rows = depth // (blks * rows_n)

    def over_rows(x, flip):
        return lax.ppermute(x, "rows", [(i, i ^ flip) for i in range(rows_n)])

    def over_blk(x, by):
        return lax.ppermute(x, "blk", [(i, (i + by) % blks) for i in range(blks)])

    pos = pos_index.T
    w_hi = loss_weight.astype(bf16).astype(f32)
    w_mid = (loss_weight - w_hi).astype(bf16).astype(f32)
    meta = jnp.concatenate(
        [
            (labels >> 7)[None].astype(bf16),
            (labels & 127)[None].astype(bf16),
            (pos // n).astype(bf16),
            (pos % n).astype(bf16),
            w_hi[None].astype(bf16),
            w_mid[None].astype(bf16),
            (loss_weight - w_hi - w_mid)[None].astype(bf16),
        ]
    )
    meta = jnp.pad(meta, ((0, META - meta.shape[0]), (0, wide - n)))
    (p0,) = call(
        embed_kernel,
        (features, head_weight, meta),
        [shape(n + META, wide, dtype=bf16)],
        flops=2 * n * depth * wide,
        name="embed",
    )
    p2 = over_rows(p0, 2)
    n1, n2 = over_blk(p0, 1), over_blk(p0, 2)
    p1 = over_rows(p0, 1)
    p3 = over_rows(p2, 1)

    turned = features.T.reshape(blks, rows_n, slice_rows, n)
    turned = [
        lax.dynamic_index_in_dim(turned, me ^ j, 1, keepdims=False).reshape(blks * slice_rows, n)
        for j in range(4)
    ]
    f2 = over_rows(jnp.concatenate(turned[2:]), 2)
    m = blks * slice_rows
    f13 = over_rows(jnp.concatenate([turned[1], f2[m:]]), 1)
    f2 = f2[:m]

    scal = jnp.concatenate([me[None].astype(jnp.int32), pair_mask[0]])
    scratch = [
        pltpu.VMEM((n, n), f32),
        pltpu.VMEM((n, 128), f32),
        pltpu.VMEM((n, 128), f32),
        pltpu.VMEM((n, 128), f32),
    ]
    tile = (p0, p1, p2, p3)
    anchors, c0, sums, own_grad = call(
        own_kernel,
        (scal, *tile),
        [shape(8, 4 * n), shape(n, 4 * n, dtype=bf16), shape(8, 4 * n), shape(n, wide)],
        scratch,
        flops=2 * n * n * wide * 40,
        name="own_block",
    )
    c1, c2, sums, grad1, grad2 = call(
        earlier_kernel,
        (scal, n1, n2, *tile, anchors, sums),
        [
            shape(n, 4 * n, dtype=bf16),
            shape(n, 4 * n, dtype=bf16),
            shape(8, 4 * n),
            shape(n, wide, dtype=bf16),
            shape(n, wide, dtype=bf16),
        ],
        scratch,
        flops=2 * n * n * wide * 40,
        name="earlier_blocks",
    )
    grad1, grad2 = over_blk(grad1, -1), over_blk(grad2, -2)
    keep, send = call(
        anchor_kernel,
        (c0, c1, c2, p0, n1, n2),
        [shape(2 * n, wide), shape(2 * n, wide)],
        flops=2 * n * n * wide * 12,
        name="anchor_grad",
    )
    half = keep + over_rows(send, 1)
    from_y = over_rows(half[n:].astype(bf16), 2)

    other = over_rows(sums, 1).reshape(8, 2, 2, n)[:, :, ::-1].reshape(8, 4 * n)
    sums = sums + other
    other = over_rows(sums, 2).reshape(8, 2, 2 * n)[:, ::-1].reshape(8, 4 * n)
    sums = sums + other
    anchor_loss = sums[3, :n] / (SMOOTHING_SCALE * 3 * 4 * n)
    own_where = (((pos_index // n) ^ me) * n + pos_index % n).astype(f32)
    (base,) = call(
        listed_kernel,
        (anchors, sums, own_where, sums[:, :n].T, *tile, half[:n] + own_grad),
        [shape(n, wide)],
        flops=2 * n * n * wide * 8,
        name="listed",
    )
    total = base + from_y.astype(f32) + grad1.astype(f32) + grad2.astype(f32)
    g0 = total.astype(bf16)
    g2 = over_rows(g0, 2)
    g1 = over_rows(g0, 1)
    g3 = over_rows(g2, 1)
    (part,) = call(
        head_kernel,
        (turned[0], f2, f13, g0, g1, g2, g3),
        [shape(m, wide, dtype=bf16)],
        flops=2 * m * 4 * n * wide,
        name="head_grad",
    )
    parts = lax.all_to_all(part, "blk", split_axis=0, concat_axis=0, tiled=True)
    weight_grad = jnp.sum(parts.reshape(blks, slice_rows, wide).astype(f32), axis=0)
    return anchor_loss, weight_grad


def solution(mesh):
    return jax.shard_map(
        local,
        mesh=mesh,
        in_specs=(
            P(("blk", "rows"), None),
            P(),
            P(("blk", "rows")),
            P(("blk", "rows"), None),
            P("blk", None),
            P(("blk", "rows")),
        ),
        out_specs=(P(("blk", "rows")), P(("blk", "rows"), None)),
        check_vma=False,
    )
```

time: 719 us -> 169 us (0.24)
  waiting for transfers between devices: 534 us -> 66.9 us
  matrix products: 45.6 us -> 0 us
  Pallas kernels: 0 us -> 37.2 us
  blocking collectives: 37.1 us -> 0 us
  other arithmetic: 38.9 us -> 12.3 us
  starting transfers between devices: 10.8 us -> 34.1 us
  between operations: 16 us -> 0.9 us
  local copies, waits for them, and re-layouts: 28.9 us -> 16.6 us
    unnamed x4 -> x0, waiting for transfers between devices: 400 us -> none
    dot_general x12 -> x0, matrix products: 45.6 us -> none  [the longest x3 16.8 us: compute(): lax.dot_general(anchors, tile_rows, (((1,), (1,)), ((), ())), preferred_e...]
    pallas_call x0 -> x6, Pallas kernels: none -> 37.2 us  [call(): pl.pallas_call(kernel, out_shape=outs, in_specs=[SMEM if x.ndim == 1 else...]
    all_gather x1 -> x0, blocking collectives: 37.1 us -> none  [local(): lax.all_gather(labels, 'rows', axis=0, tiled=True)]
    reduce_scatter x1 -> x0, waiting for transfers between devices: 35.2 us -> none  [local(): lax.psum_scatter(own_term + received, 'rows', scatter_dimension=0, tiled=...]
    all_gather x1 -> x0, waiting for transfers between devices: 28.8 us -> none  [local(): lax.all_gather(embedded, 'rows', axis=0, tiled=True)]
    ppermute x6 -> x16, waiting for transfers between devices: 70.6 us -> 43.3 us  [the longest x12 39 us: over_rows(): return lax.ppermute(x, 'rows', [(i, i ^ flip) for i in range(rows_n)])]
    all_to_all x0 -> x1, waiting for transfers between devices: none -> 23.6 us  [local(): parts = lax.all_to_all(part, 'blk', split_axis=0, concat_axis=0, tiled=True)]
  transfers between devices with their start and end apart: 9 -> 17, of which waited for: 6 -> 8; matrix products, arithmetic and copies ran while one was open for 11% -> 11% of each run, Pallas kernels for 0% -> 7%
where the time goes in v1:
time: 169 us; the launch traced here: 168 us
  waiting for transfers between devices  66.9 us (40%)
  Pallas kernels  37.2 us (22%)
  starting transfers between devices  34.1 us (20%)
  local copies, waits for them, and re-layouts  16.6 us (10%)
  other arithmetic  12.3 us (7%)
    ppermute x12, waiting for transfers between devices, over_rows(): return lax.ppermute(x, 'rows', [(i, i ^ flip) for i in range(rows_n)])  39 us
    pallas_call x6, Pallas kernels, call(): pl.pallas_call(kernel, out_shape=outs, in_specs=[SMEM if x.ndim == 1 else...  37.2 us
    all_to_all x1, waiting for transfers between devices, local(): parts = lax.all_to_all(part, 'blk', split_axis=0, concat_axis=0, tiled=True)  23.6 us
    ppermute x4, starting transfers between devices, over_blk(): return lax.ppermute(x, 'blk', [(i, (i + by) % blks) for i in range(blks)])  16.4 us
    all_to_all x1, starting transfers between devices, local(): parts = lax.all_to_all(part, 'blk', split_axis=0, concat_axis=0, tiled=True)  9.69 us
    unnamed x44, local copies, waits for them, and re-layouts  9.01 us
    ppermute x12, starting transfers between devices, over_rows(): return lax.ppermute(x, 'rows', [(i, i ^ flip) for i in range(rows_n)])  7.98 us
    ppermute x4, waiting for transfers between devices, over_blk(): return lax.ppermute(x, 'blk', [(i, (i + by) % blks) for i in range(blks)])  4.37 us
  transfers between devices with their start and end apart: 17, of which 8 were waited for; matrix products, arithmetic and copies ran while one was open for 11% of the time, Pallas kernels for 7%

profile of v1, /device:TPU:8, one launch (start us, length us, event | category | flops | bytes accessed | tf_op | source)
XLA Modules:
  0.0 168.0 jit_solution(10478920685657335396)
XLA Ops:
  2.9 1.2 copy-done
  4.1 1.9 %copy-done.2 = bf16[2048,768]{1,0:T(8,128)(2,1)S(1)} copy-done((bf16[2048,768]{1,0:T(8,128)(2,1)S(1)}, bf16[2048,768]{1,0:T(8,128)(2,1)}, u32[]{:S(2)}) %copy-start.2) | copy-done | bytes 3145752
  7.0 2.3 %collective-permute-start.3 = (bf16[272,768]{1,0:T(8,128)(2,1)S(1)}, bf16[272,768]{1,0:T(8,128)(2,1)S(1)}, u32[]{:S(2)}, u32[]{:S(2)}) collective-permute-start(bf16[272,768]{1,0:T(8,128)(2,1)S(1)} %embed.1.p0.n0), channel_id=1, source_target_pairs={{0,2},{1,3},{2,0},{3,1},{4,6},{5,7},{6,4},{7,5},{8,10},{9,11},{10,... | collective-permute-start | bytes 1253384 | tf_op jit(solution)/shard_map/ppermute | solution.py:236
  9.3 9.2 %collective-permute-done.3.p2 = bf16[272,768]{1,0:T(8,128)(2,1)S(1)} collective-permute-done((bf16[272,768]{1,0:T(8,128)(2,1)S(1)}, bf16[272,768]{1,0:T(8,128)(2,1)S(1)}, u32[]{:S(2)}, u32[]{:S(2)}) %collective-permute-start.3) | collective-permute-done | bytes 417824 | tf_op jit(solution)/shard_map/ppermute | solution.py:236
  18.5 2.3 %collective-permute-start = (bf16[272,768]{1,0:T(8,128)(2,1)S(1)}, bf16[272,768]{1,0:T(8,128)(2,1)S(1)}, u32[]{:S(2)}, u32[]{:S(2)}) collective-permute-start(bf16[272,768]{1,0:T(8,128)(2,1)S(1)} %embed.1.p0.n0), channel_id=1, source_target_pairs={{0,4},{4,8},{8,12},{12,16},{16,20},{20,24},{24,28},{28,32},{32,36}... | collective-permute-start | bytes 1253384 | tf_op jit(solution)/shard_map/ppermute | solution.py:239
  20.7 1.9 %collective-permute-start.1 = (bf16[272,768]{1,0:T(8,128)(2,1)S(1)}, bf16[272,768]{1,0:T(8,128)(2,1)S(1)}, u32[]{:S(2)}, u32[]{:S(2)}) collective-permute-start(bf16[272,768]{1,0:T(8,128)(2,1)S(1)} %embed.1.p0.n0), channel_id=1, source_target_pairs={{0,8},{4,12},{8,16},{12,20},{16,24},{20,28},{24,32},{28,36},{32,40... | collective-permute-start | bytes 1253384 | tf_op jit(solution)/shard_map/ppermute | solution.py:239
  22.8 10.8 %own_block.1 = (f32[8,1024]{1,0:T(8,128)S(1)}, bf16[256,1024]{1,0:T(8,128)(2,1)S(1)}, f32[8,1024]{1,0:T(8,128)S(1)}, f32[256,768]{1,0:T(8,128)S(1)}) custom-call(s32[4]{0:T(128)S(1)} %pad_add_fusion.scal_ref, bf16[272,768]{1,0:T(8,128)(2,1)S(1)} %embed.1.p0.n0, bf16[272,768]{1,0:T(8,128)(2,1)S(1)} %collective-permute-done.2.p1, ...), custom_call_target="tpu_custom_call" | custom-call | flops 4026531840 | bytes 3047440 | tf_op jit(solution)/shard_map/own_block/pallas_call | solution.py:27
  34.5 4.3 %collective-permute-done.n1 = bf16[272,768]{1,0:T(8,128)(2,1)S(1)} collective-permute-done((bf16[272,768]{1,0:T(8,128)(2,1)S(1)}, bf16[272,768]{1,0:T(8,128)(2,1)S(1)}, u32[]{:S(2)}, u32[]{:S(2)}) %collective-permute-start) | collective-permute-done | bytes 417824 | tf_op jit(solution)/shard_map/ppermute | solution.py:239
  38.8 19.6 %earlier_blocks.1 = (bf16[256,1024]{1,0:T(8,128)(2,1)S(1)}, bf16[256,1024]{1,0:T(8,128)(2,1)S(1)}, f32[8,1024]{1,0:T(8,128)S(1)}, bf16[256,768]{1,0:T(8,128)(2,1)}, bf16[256,768]{1,0:T(8,128)(2,1)}) custom-call(s32[4]{0:T(128)S(1)} %pad_add_fusion.scal_ref, bf16[272,768]{1,0:T(8,128)(2,1)S(1)} %collective-permute-done.n1, ...), custom_call_target="tpu_custom_call" | custom-call | flops 4026531840 | bytes 4440080 | tf_op jit(solution)/shard_map/earlier_blocks/pallas_call | solution.py:27
  60.4 2.6 %anchor_grad.1 = (f32[512,768]{1,0:T(8,128)S(1)}, f32[512,768]{1,0:T(8,128)}) custom-call(bf16[256,1024]{1,0:T(8,128)(2,1)S(1)} %get-tuple-element.16.c0, bf16[256,1024]{1,0:T(8,128)(2,1)S(1)} %get-tuple-element.17.c1, bf16[256,1024]{1,0:T(8,128)(2,1)S(1)} %get-tuple-element.18.c2, bf16[272,768]{1,0:T(8,128)(2,1)S(1)} %embed.1.p0.n0, ...), custom_call_target="tpu_custom_call" | custom-call | flops 1207959552 | bytes 5971968 | tf_op jit(solution)/shard_map/anchor_grad/pallas_call | solution.py:27
  63.1 1.3 copy.35
  64.4 2.0 %dynamic-slice_bitcast_fusion = (bf16[512,256]{1,0:T(8,128)(2,1)}, bf16[512,256]{1,0:T(8,128)(2,1)S(1)}, bf16[512,256]{1,0:T(8,128)(2,1)S(1)}, bf16[512,256]{1,0:T(8,128)(2,1)S(1)}) fusion(bf16[64,4,8,256]{3,2,1,0:T(8,128)(2,1)} %bitcast.44, s32[]{:T(128)S(6)} %select_n.41, s32[]{:T(128)S(6)} %select_n.40, s32[]{:T(128)S(6)} %select_n.39, s32[]{:T(128)S(6)} %select_n.38), kind=kLoop, calls=%fused_computation.8 | loop fusion | bytes 2097168 | tf_op jit(solution)/shard_map/reshape | solution.py:270
  67.2 1.3 collective-permute-start.7
  71.1 1.1 bitcast_add_fusion.1
  74.0 11.2 %collective-permute-start.11 = (bf16[256,768]{1,0:T(8,128)(2,1)}, bf16[256,768]{1,0:T(8,128)(2,1)}, u32[]{:S(2)}, u32[]{:S(2)}) collective-permute-start(bf16[256,768]{1,0:T(8,128)(2,1)} %get-tuple-element.22), channel_id=1, source_target_pairs={{0,252},{4,0},{8,4},{12,8},{16,12},{20,16},{24,20},{28,24},{32,28}... | collective-permute-start | bytes 1179656 | tf_op jit(solution)/shard_map/ppermute | solution.py:239
  86.2 15.3 %collective-permute-done.6 = f32[8,1024]{0,1:T(8,128)S(1)} collective-permute-done((f32[8,1024]{0,1:T(8,128)S(1)}, f32[8,1024]{0,1:T(8,128)S(1)}, u32[]{:S(2)}, u32[]{:S(2)}) %collective-permute-start.6) | collective-permute-done | bytes 32800 | tf_op jit(solution)/shard_map/ppermute | solution.py:236
  102.2 1.1 rev.7
  103.4 1.8 %add.62 = f32[512,768]{1,0:T(8,128)S(1)} add(f32[512,768]{1,0:T(8,128)S(1)} %get-tuple-element.19, f32[512,768]{1,0:T(8,128)} %collective-permute-done.9) | non-fusion elementwise | flops 393216 | bytes 4718592 | tf_op jit(solution)/shard_map/add | solution.py:316
  106.1 1.3 collective-permute-start.10
  107.4 1.2 copy.44.coef_ref
  108.6 1.3 slice_add_fusion.base_ref
  109.9 1.4 listed.1
  111.4 5.9 %collective-permute-done.10 = bf16[256,768]{1,0:T(8,128)(2,1)} collective-permute-done((bf16[256,768]{1,0:T(8,128)(2,1)}, bf16[256,768]{1,0:T(8,128)(2,1)}, u32[]{:S(2)}, u32[]{:S(2)}) %collective-permute-start.10) | collective-permute-done | bytes 393248 | tf_op jit(solution)/shard_map/ppermute | solution.py:236
  117.2 1.5 add_convert_fusion.g0
  118.7 1.4 collective-permute-start.14
  120.1 1.1 fusion.14
  121.8 6.9 %collective-permute-done.14.g2 = bf16[256,768]{1,0:T(8,128)(2,1)S(1)} collective-permute-done((bf16[256,768]{1,0:T(8,128)(2,1)S(1)}, bf16[256,768]{1,0:T(8,128)(2,1)S(1)}, u32[]{:S(2)}, u32[]{:S(2)}) %collective-permute-start.14) | collective-permute-done | bytes 393248 | tf_op jit(solution)/shard_map/ppermute | solution.py:236
  128.8 1.7 %collective-permute-done.15.g3 = bf16[256,768]{1,0:T(8,128)(2,1)S(1)} collective-permute-done((bf16[256,768]{1,0:T(8,128)(2,1)S(1)}, bf16[256,768]{1,0:T(8,128)(2,1)S(1)}, u32[]{:S(2)}, u32[]{:S(2)}) %collective-permute-start.15) | collective-permute-done | bytes 393248 | tf_op jit(solution)/shard_map/ppermute | solution.py:236
  130.5 1.9 %head_grad.1 = bf16[512,768]{1,0:T(8,128)(2,1)} custom-call(bf16[512,256]{1,0:T(8,128)(2,1)S(1)} %get-tuple-element.27.f0, bf16[512,256]{1,0:T(8,128)(2,1)S(1)} %get-tuple-element.29.f2, bf16[1024,256]{1,0:T(8,128)(2,1)S(1)} %collective-permute-done.8.f13, bf16[256,768]{1,0:T(8,128)(2,1)S(1)} %add_convert_fusion.g0, ...), custom_call_target="tpu_custom_call" | custom-call | flops 805306368 | bytes 3407872 | tf_op jit(solution)/shard_map/head_grad/pallas_call | solution.py:27
  132.3 9.7 %all-to-all-start = ((bf16[64,8,768]{2,1,0:T(8,128)(2,1)}), bf16[64,8,768]{2,1,0:T(8,128)(2,1)S(1)}, u32[]{:S(2)}, u32[]{:S(2)}) async-start(bf16[64,8,768]{2,1,0:T(8,128)(2,1)} %bitcast.15), calls=%async_computation | async-start | bytes 1572864 | tf_op jit(solution)/shard_map/all_to_all | solution.py:344
  142.0 1.7 fusion.4
  143.7 23.6 %all-to-all-done = bf16[64,8,768]{2,1,0:T(8,128)(2,1)S(1)} async-done(((bf16[64,8,768]{2,1,0:T(8,128)(2,1)}), bf16[64,8,768]{2,1,0:T(8,128)(2,1)S(1)}, u32[]{:S(2)}, u32[]{:S(2)}) %all-to-all-start) | async-done | bytes 786464 | tf_op jit(solution)/shard_map/all_to_all | solution.py:344
  (84 shorter events, 15.5 us)
Async XLA Ops:
  6.0 16.7 %copy-start.20 = (s32[1,3]{1,0:T(1,128)S(1)}, s32[1,3]{1,0:T(1,128)}, u32[]{:S(2)}) copy-start(s32[1,3]{1,0:T(1,128)} %param.10) | copy-start | bytes 40
  7.0 11.5 %collective-permute-start.3 = (bf16[272,768]{1,0:T(8,128)(2,1)S(1)}, bf16[272,768]{1,0:T(8,128)(2,1)S(1)}, u32[]{:S(2)}, u32[]{:S(2)}) collective-permute-start(bf16[272,768]{1,0:T(8,128)(2,1)S(1)} %embed.1.p0.n0), channel_id=1, source_target_pairs={{0,2},{1,3},{2,0},{3,1},{4,6},{5,7},{6,4},{7,5},{8,10},{9,11},{10,... | collective-permute-start | bytes 1253384 | tf_op jit(solution)/shard_map/ppermute | solution.py:236
  9.2 13.5 %collective-permute-start.2 = (bf16[272,768]{1,0:T(8,128)(2,1)S(1)}, bf16[272,768]{1,0:T(8,128)(2,1)S(1)}, u32[]{:S(2)}, u32[]{:S(2)}) collective-permute-start(bf16[272,768]{1,0:T(8,128)(2,1)S(1)} %embed.1.p0.n0), channel_id=1, source_target_pairs={{0,1},{1,0},{2,3},{3,2},{4,5},{5,4},{6,7},{7,6},{8,9},{9,8},{10,11... | collective-permute-start | bytes 1253384 | tf_op jit(solution)/shard_map/ppermute | solution.py:236
  18.4 20.4 %copy-start.5 = (bf16[272,768]{1,0:T(8,128)(2,1)}, bf16[272,768]{1,0:T(8,128)(2,1)S(1)}, u32[]{:S(2)}) copy-start(bf16[272,768]{1,0:T(8,128)(2,1)S(1)} %collective-permute-done.3.p2) | copy-start | bytes 1253380
  18.4 4.3 %collective-permute-start.4 = (bf16[272,768]{1,0:T(8,128)(2,1)S(1)}, bf16[272,768]{1,0:T(8,128)(2,1)S(1)}, u32[]{:S(2)}, u32[]{:S(2)}) collective-permute-start(bf16[272,768]{1,0:T(8,128)(2,1)S(1)} %collective-permute-done.3.p2), channel_id=1, source_target_pairs={{0,1},{1,0},{2,3},{3,2},{4,5},{5,4},{6,7},{7,6},{8,9},{9,8},{10,11... | collective-permute-start | bytes 1253384 | tf_op jit(solution)/shard_map/ppermute | solution.py:236
  18.5 20.3 %collective-permute-start = (bf16[272,768]{1,0:T(8,128)(2,1)S(1)}, bf16[272,768]{1,0:T(8,128)(2,1)S(1)}, u32[]{:S(2)}, u32[]{:S(2)}) collective-permute-start(bf16[272,768]{1,0:T(8,128)(2,1)S(1)} %embed.1.p0.n0), channel_id=1, source_target_pairs={{0,4},{4,8},{8,12},{12,16},{16,20},{20,24},{24,28},{28,32},{32,36}... | collective-permute-start | bytes 1253384 | tf_op jit(solution)/shard_map/ppermute | solution.py:239
  20.7 18.1 %collective-permute-start.1 = (bf16[272,768]{1,0:T(8,128)(2,1)S(1)}, bf16[272,768]{1,0:T(8,128)(2,1)S(1)}, u32[]{:S(2)}, u32[]{:S(2)}) collective-permute-start(bf16[272,768]{1,0:T(8,128)(2,1)S(1)} %embed.1.p0.n0), channel_id=1, source_target_pairs={{0,8},{4,12},{8,16},{12,20},{16,24},{20,28},{24,32},{28,36},{32,40... | collective-permute-start | bytes 1253384 | tf_op jit(solution)/shard_map/ppermute | solution.py:239
  22.7 16.1 %copy-start.7 = (bf16[272,768]{1,0:T(8,128)(2,1)}, bf16[272,768]{1,0:T(8,128)(2,1)S(1)}, u32[]{:S(2)}) copy-start(bf16[272,768]{1,0:T(8,128)(2,1)S(1)} %collective-permute-done.2.p1) | copy-start | bytes 1253380
  22.8 16.1 %copy-start.9 = (bf16[272,768]{1,0:T(8,128)(2,1)}, bf16[272,768]{1,0:T(8,128)(2,1)S(1)}, u32[]{:S(2)}) copy-start(bf16[272,768]{1,0:T(8,128)(2,1)S(1)} %collective-permute-done.4.p3) | copy-start | bytes 1253380
  38.7 19.7 %copy-start.11 = (bf16[272,768]{1,0:T(8,128)(2,1)}, bf16[272,768]{1,0:T(8,128)(2,1)S(1)}, u32[]{:S(2)}) copy-start(bf16[272,768]{1,0:T(8,128)(2,1)S(1)} %collective-permute-done.n1) | copy-start | bytes 1253380
  38.8 19.6 %copy-start.13 = (bf16[272,768]{1,0:T(8,128)(2,1)}, bf16[272,768]{1,0:T(8,128)(2,1)S(1)}, u32[]{:S(2)}) copy-start(bf16[272,768]{1,0:T(8,128)(2,1)S(1)} %collective-permute-done.1.n2) | copy-start | bytes 1253380
  60.4 2.6 %copy-start.1 = (bf16[256,2048]{1,0:T(8,128)(2,1)S(1)}, bf16[256,2048]{1,0:T(8,128)(2,1)}, u32[]{:S(2)}) copy-start(bf16[256,2048]{1,0:T(8,128)(2,1)} %features_ref.1) | copy-start | bytes 3145732
  63.1 40.3 %collective-permute-start.9 = (f32[512,768]{1,0:T(8,128)}, f32[512,768]{1,0:T(8,128)}, u32[]{:S(2)}, u32[]{:S(2)}) collective-permute-start(f32[512,768]{1,0:T(8,128)} %get-tuple-element.20), channel_id=1, source_target_pairs={{0,1},{1,0},{2,3},{3,2},{4,5},{5,4},{6,7},{7,6},{8,9},{9,8},{10,11... | collective-permute-start | bytes 4718600 | tf_op jit(solution)/shard_map/ppermute | solution.py:236
  64.4 4.4 %copy-start.19 = (s32[256,3]{0,1:T(4,128)S(1)}, s32[256,3]{0,1:T(4,128)}, u32[]{:S(2)}) copy-start(s32[256,3]{0,1:T(4,128)} %param.9) | copy-start | bytes 9220
  67.2 52.9 %collective-permute-start.7 = (bf16[1024,256]{1,0:T(8,128)(2,1)}, bf16[1024,256]{1,0:T(8,128)(2,1)}, u32[]{:S(2)}, u32[]{:S(2)}) collective-permute-start(bf16[1024,256]{1,0:T(8,128)(2,1)} %pad_maximum_fusion), channel_id=1, source_target_pairs={{0,2},{1,3},{2,0},{3,1},{4,6},{5,7},{6,4},{7,5},{8,10},{9,11},{10,... | collective-permute-start | bytes 1572872 | tf_op jit(solution)/shard_map/ppermute | solution.py:236
  68.6 1.4 collective-permute-start.5
  72.2 29.2 %collective-permute-start.6 = (f32[8,1024]{0,1:T(8,128)S(1)}, f32[8,1024]{0,1:T(8,128)S(1)}, u32[]{:S(2)}, u32[]{:S(2)}) collective-permute-start(f32[8,1024]{0,1:T(8,128)S(1)} %bitcast_add_fusion.1), channel_id=1, source_target_pairs={{0,2},{1,3},{2,0},{3,1},{4,6},{5,7},{6,4},{7,5},{8,10},{9,11},{10,... | collective-permute-start | bytes 98312 | tf_op jit(solution)/shard_map/ppermute | solution.py:236
  74.0 37.3 %collective-permute-start.11 = (bf16[256,768]{1,0:T(8,128)(2,1)}, bf16[256,768]{1,0:T(8,128)(2,1)}, u32[]{:S(2)}, u32[]{:S(2)}) collective-permute-start(bf16[256,768]{1,0:T(8,128)(2,1)} %get-tuple-element.22), channel_id=1, source_target_pairs={{0,252},{4,0},{8,4},{12,8},{16,12},{20,16},{24,20},{28,24},{32,28}... | collective-permute-start | bytes 1179656 | tf_op jit(solution)/shard_map/ppermute | solution.py:239
  85.2 26.2 %collective-permute-start.12 = (bf16[256,768]{1,0:T(8,128)(2,1)}, bf16[256,768]{1,0:T(8,128)(2,1)}, u32[]{:S(2)}, u32[]{:S(2)}) collective-permute-start(bf16[256,768]{1,0:T(8,128)(2,1)} %get-tuple-element.23), channel_id=1, source_target_pairs={{0,248},{4,252},{8,0},{12,4},{16,8},{20,12},{24,16},{28,20},{32,24... | collective-permute-start | bytes 1179656 | tf_op jit(solution)/shard_map/ppermute | solution.py:239
  103.4 4.0 %copy-start.16 = (f32[8,1024]{0,1:T(8,128)}, f32[8,1024]{0,1:T(8,128)S(1)}, u32[]{:S(2)}) copy-start(f32[8,1024]{0,1:T(8,128)S(1)} %bitcast_add_fusion) | copy-start | bytes 98308
  105.2 2.2 %copy-start.15 = (f32[512,768]{1,0:T(8,128)}, f32[512,768]{1,0:T(8,128)S(1)}, u32[]{:S(2)}) copy-start(f32[512,768]{1,0:T(8,128)S(1)} %add.62) | copy-start | bytes 4718596
  105.2 3.4 %copy-start.4 = (f32[256,768]{1,0:T(8,128)S(1)}, f32[256,768]{1,0:T(8,128)}, u32[]{:S(2)}) copy-start(f32[256,768]{1,0:T(8,128)} %copy-done.3) | copy-start | bytes 2359300
  106.0 3.8 %copy-start.6 = (bf16[272,768]{1,0:T(8,128)(2,1)S(1)}, bf16[272,768]{1,0:T(8,128)(2,1)}, u32[]{:S(2)}) copy-start(bf16[272,768]{1,0:T(8,128)(2,1)} %copy-done.5) | copy-start | bytes 1253380
  106.0 3.8 %copy-start.8 = (bf16[272,768]{1,0:T(8,128)(2,1)S(1)}, bf16[272,768]{1,0:T(8,128)(2,1)}, u32[]{:S(2)}) copy-start(bf16[272,768]{1,0:T(8,128)(2,1)} %copy-done.7) | copy-start | bytes 1253380
  106.0 3.9 %copy-start.10 = (bf16[272,768]{1,0:T(8,128)(2,1)S(1)}, bf16[272,768]{1,0:T(8,128)(2,1)}, u32[]{:S(2)}) copy-start(bf16[272,768]{1,0:T(8,128)(2,1)} %copy-done.9) | copy-start | bytes 1253380
  106.1 11.2 %collective-permute-start.10 = (bf16[256,768]{1,0:T(8,128)(2,1)}, bf16[256,768]{1,0:T(8,128)(2,1)}, u32[]{:S(2)}, u32[]{:S(2)}) collective-permute-start(bf16[256,768]{1,0:T(8,128)(2,1)} %slice.37), channel_id=1, source_target_pairs={{0,2},{1,3},{2,0},{3,1},{4,6},{5,7},{6,4},{7,5},{8,10},{9,11},{10,... | collective-permute-start | bytes 1179656 | tf_op jit(solution)/shard_map/ppermute | solution.py:236
  111.3 9.8 %copy-start.17 = (bf16[512,256]{1,0:T(8,128)(2,1)S(1)}, bf16[512,256]{1,0:T(8,128)(2,1)}, u32[]{:S(2)}) copy-start(bf16[512,256]{1,0:T(8,128)(2,1)} %get-tuple-element.24) | copy-start | bytes 786436
  118.7 10.1 %collective-permute-start.14 = (bf16[256,768]{1,0:T(8,128)(2,1)S(1)}, bf16[256,768]{1,0:T(8,128)(2,1)S(1)}, u32[]{:S(2)}, u32[]{:S(2)}) collective-permute-start(bf16[256,768]{1,0:T(8,128)(2,1)S(1)} %add_convert_fusion.g0), channel_id=1, source_target_pairs={{0,2},{1,3},{2,0},{3,1},{4,6},{5,7},{6,4},{7,5},{8,10},{9,11},{10,... | collective-permute-start | bytes 1179656 | tf_op jit(solution)/shard_map/ppermute | solution.py:236
  121.2 7.5 %collective-permute-start.8 = (bf16[1024,256]{1,0:T(8,128)(2,1)S(1)}, bf16[1024,256]{1,0:T(8,128)(2,1)S(1)}, u32[]{:S(2)}, u32[]{:S(2)}) collective-permute-start(bf16[1024,256]{1,0:T(8,128)(2,1)S(1)} %pad_maximum_fusion.1), channel_id=1, source_target_pairs={{0,1},{1,0},{2,3},{3,2},{4,5},{5,4},{6,7},{7,6},{8,9},{9,8},{10,11... | collective-permute-start | bytes 1572872 | tf_op jit(solution)/shard_map/ppermute | solution.py:236
  121.3 7.4 %collective-permute-start.13 = (bf16[256,768]{1,0:T(8,128)(2,1)S(1)}, bf16[256,768]{1,0:T(8,128)(2,1)S(1)}, u32[]{:S(2)}, u32[]{:S(2)}) collective-permute-start(bf16[256,768]{1,0:T(8,128)(2,1)S(1)} %add_convert_fusion.g0), channel_id=1, source_target_pairs={{0,1},{1,0},{2,3},{3,2},{4,5},{5,4},{6,7},{7,6},{8,9},{9,8},{10,11... | collective-permute-start | bytes 1179656 | tf_op jit(solution)/shard_map/ppermute | solution.py:236
  128.7 1.7 %collective-permute-start.15 = (bf16[256,768]{1,0:T(8,128)(2,1)S(1)}, bf16[256,768]{1,0:T(8,128)(2,1)S(1)}, u32[]{:S(2)}, u32[]{:S(2)}) collective-permute-start(bf16[256,768]{1,0:T(8,128)(2,1)S(1)} %collective-permute-done.14.g2), channel_id=1, source_target_pairs={{0,1},{1,0},{2,3},{3,2},{4,5},{5,4},{6,7},{7,6},{8,9},{9,8},{10,11... | collective-permute-start | bytes 1179656 | tf_op jit(solution)/shard_map/ppermute | solution.py:236
  132.3 34.9 %all-to-all-start = ((bf16[64,8,768]{2,1,0:T(8,128)(2,1)}), bf16[64,8,768]{2,1,0:T(8,128)(2,1)S(1)}, u32[]{:S(2)}, u32[]{:S(2)}) async-start(bf16[64,8,768]{2,1,0:T(8,128)(2,1)} %bitcast.15), calls=%async_computation | async-start | bytes 1572864 | tf_op jit(solution)/shard_map/all_to_all | solution.py:344
  (6 other events, 6.8 us)

commit v2 on v1

--- a/solution.py
+++ b/solution.py
@@ -13,6 +13,7 @@
 BASE2 = SMOOTHING_SCALE / LN2
 MASKED = 1e30
 META = 16
+OWN_US = 3.0
 CHUNK = 16
 f32 = jnp.float32
 bf16 = jnp.bfloat16
@@ -21,17 +22,17 @@
 SMEM = pl.BlockSpec(memory_space=pltpu.SMEM)
 
 
-def call(kernel, inputs, outs, scratch=(), flops=0, name=None):
-    moved = sum(x.size * x.dtype.itemsize for x in inputs)
-    moved += sum(x.size * x.dtype.itemsize for x in outs)
+def call(kernel, inputs, outs, scratch=(), micros=0.0, name=None):
     return pl.pallas_call(
         kernel,
         out_shape=outs,
         in_specs=[SMEM if x.ndim == 1 else VMEM for x in inputs],
         out_specs=[VMEM] * len(outs),
         scratch_shapes=list(scratch),
-        compiler_params=pltpu.CompilerParams(vmem_limit_bytes=40 << 20),
-        cost_estimate=pl.CostEstimate(flops=flops, bytes_accessed=moved, transcendentals=0),
+        compiler_params=pltpu.CompilerParams(vmem_limit_bytes=16 << 20),
+        cost_estimate=pl.CostEstimate(
+            flops=int(micros * 1.15e9), bytes_accessed=1024, transcendentals=0
+        ),
         name=name,
     )(*inputs)
 
@@ -52,14 +53,50 @@
     return lax.dot_general(a, b, (((0,), (0,)), ((), ())), preferred_element_type=f32)
 
 
-def embed_kernel(features_ref, weight_ref, meta_ref, out_ref):
-    rows = features_ref.shape[0]
-    out_ref[:rows, :] = nn(features_ref[...], weight_ref[...]).astype(bf16)
-    out_ref[rows:, :] = meta_ref[...]
+def embed_kernel(features_ref, weight_ref, labels_ref, pos_ref, loss_weight_ref, out_ref):
+    n, width = features_ref.shape[0], weight_ref.shape[1]
+    out_ref[:n, :] = nn(features_ref[...], weight_ref[...]).astype(bf16)
+    out_ref[n:, :] = jnp.zeros((META, width), bf16)
+
+    @pl.when(pl.program_id(0) == 0)
+    def _():
+        labels, pos, weight = labels_ref[...], pos_ref[...], loss_weight_ref[...]
+        high = weight.astype(bf16).astype(f32)
+        middle = (weight - high).astype(bf16).astype(f32)
+        rows = [labels >> 7, labels & 127, pos // n, pos % n]
+        rows = [x.astype(f32) for x in rows] + [high, middle, weight - high - middle]
+        rows.append(jnp.zeros((META - 11, n), f32))
+        out_ref[n:, :n] = jnp.concatenate(rows, axis=0).astype(bf16)
+
+
+def embed(features, head_weight, labels, pos, loss_weight):
+    n, depth = features.shape
+    wide, step = head_weight.shape[1], n
+    return pl.pallas_call(
+        embed_kernel,
+        grid=(wide // step,),
+        out_shape=shape(n + META, wide, dtype=bf16),
+        in_specs=[
+            pl.BlockSpec((n, depth), lambda i: (0, 0)),
+            pl.BlockSpec((depth, step), lambda i: (0, i)),
+            pl.BlockSpec((1, n), lambda i: (0, 0)),
+            pl.BlockSpec((3, n), lambda i: (0, 0)),
+            pl.BlockSpec((1, n), lambda i: (0, 0)),
+        ],
+        out_specs=pl.BlockSpec((n + META, step), lambda i: (0, i)),
+        compiler_params=pltpu.CompilerParams(vmem_limit_bytes=56 << 20),
+        cost_estimate=pl.CostEstimate(flops=1 << 30, bytes_accessed=1 << 22, transcendentals=0),
+        name="embed",
+    )(features, head_weight, labels, pos, loss_weight)
+
+
+def across(x, width):
+    return jnp.concatenate([x] * (width // x.shape[1]), axis=1)
 
 
 def score_block(
-    rows_n, listed, tile, anchors_ref, labels_n, products_ref, coef_ref, lanes_ref, sq_ref, sums_ref
+    rows_n, listed, tile, anchors_ref, labels_n, products_ref, coef_ref, lanes_ref, sq_ref,
+    sums_ref,
 ):
     n = rows_n.shape[0]
     wide = rows_n.astype(f32)
@@ -76,8 +113,8 @@
         def step(c, carry, lanes=lanes, base=base, weight=weight, labels_a=labels_a):
             at = pl.multiple_of(c * CHUNK, CHUNK)
             rows = pl.ds(at, CHUNK)
-            q = sq_ref[rows, :1] - products_ref[rows, :]
-            q = jnp.where(labels_n[rows, :1] == labels_a, MASKED, q)
+            q = across(sq_ref[rows, :], n) - products_ref[rows, :]
+            q = jnp.where(across(labels_n[rows, :], n) == labels_a, MASKED, q)
             y = [b - q for b in base]
             e = [jnp.exp2(-jnp.abs(v)) for v in y]
             a = [1.0 + v for v in e]
@@ -101,7 +138,7 @@
             return tuple(x + fold(v) for x, v in zip(carry, (*s, loss)))
 
         zero = jnp.zeros((8, n), f32)
-        sums = lax.fori_loop(0, n // CHUNK, step, (zero,) * 4)
+        sums = lax.fori_loop(0, n // CHUNK, step, (zero,) * 4, unroll=4)
         for k, v in enumerate(sums):
             sums_ref[k : k + 1, lanes] += jnp.sum(v, axis=0, keepdims=True)
 
@@ -186,18 +223,31 @@
         sums_ref[k : k + 1, :] = sums_ref[k : k + 1, :] * weight
 
 
-def anchor_kernel(c0, c1, c2, n0, n1, n2, keep_ref, send_ref):
+def anchor_kernel(first, c0, c1, c2, n0, n1, n2, keep_ref, send_ref):
     n = n0.shape[0] - META
-    for i, (ref, j) in enumerate(((keep_ref, 0), (send_ref, 0), (keep_ref, 1), (send_ref, 1))):
+    for i, ref in ((first, keep_ref), (first + 1, send_ref)):
         lanes = slice(i * n, (i + 1) * n)
         total = tn(c0[:, lanes], n0[:n, :])
         total = total + tn(c1[:, lanes], n1[:n, :]) + tn(c2[:, lanes], n2[:n, :])
-        ref[j * n : (j + 1) * n, :] = 2.0 * total
-
-
-def listed_kernel(anchors_ref, coef_ref, own_where, own_coef, p0, p1, p2, p3, base_ref, out_ref):
+        ref[...] = 2.0 * total
+
+
+def halved_kernel(keep_ref, other_ref, out_ref):
+    out_ref[...] = (keep_ref[...] + other_ref[...]).astype(bf16)
+
+
+def listed_kernel(
+    anchors_ref, s0, s1, s2, s3, p0, p1, p2, p3, keep_ref, other_ref, own_ref, out_ref, loss_ref
+):
     n = p0.shape[0] - META
     tile = [p[:n, :] for p in (p0, p1, p2, p3)]
+    sums = []
+    for i in range(4):
+        parts = [s[:, (i ^ j) * n : ((i ^ j) + 1) * n] for j, s in enumerate((s0, s1, s2, s3))]
+        sums.append((parts[0] + parts[1]) + (parts[2] + parts[3]))
+    loss_ref[...] = sums[0][3:4, :] * (1.0 / (SMOOTHING_SCALE * 3 * 4 * n))
+    own_coef = [column(sums[0][k : k + 1, :]) for k in range(3)]
+    own_where = [column(anchors_ref[3 + k : 4 + k, :n]) for k in range(3)]
     total = jnp.zeros(out_ref.shape, f32)
     pushed = jnp.zeros((n, 1), f32)
     for i, part in enumerate(tile):
@@ -207,21 +257,25 @@
         matrix = jnp.zeros((n, n), f32)
         for k in range(3):
             hit = anchors_ref[3 + k : 4 + k, lanes] == mine
-            matrix = matrix + jnp.where(hit, coef_ref[k : k + 1, lanes], 0.0)
+            matrix = matrix + jnp.where(hit, sums[i][k : k + 1, :], 0.0)
         pushed = pushed + jnp.sum(matrix, axis=1, keepdims=True)
         for k in range(3):
-            hit = own_where[:, k : k + 1] == others
-            matrix = matrix + jnp.where(hit, own_coef[:, k : k + 1], 0.0)
+            matrix = matrix + jnp.where(own_where[k] == others, own_coef[k], 0.0)
         high = matrix.astype(bf16)
         low = (matrix - high.astype(f32)).astype(bf16)
         total = total + nn(high, part) + nn(low, part)
-    out_ref[...] = base_ref[...] + 2.0 * (pushed * tile[0].astype(f32) - total)
-
-
-def head_kernel(f0, f2, f13, g0, g1, g2, g3, out_ref):
-    m = f0.shape[0]
-    total = nn(f0[...], g0[...]) + nn(f13[:m, :], g1[...])
-    total = total + nn(f2[...], g2[...]) + nn(f13[m:, :], g3[...])
+    base = keep_ref[...] + other_ref[...] + own_ref[...]
+    out_ref[...] = base + 2.0 * (pushed * tile[0].astype(f32) - total)
+
+
+def gathered_kernel(base_ref, y_ref, one_ref, two_ref, out_ref):
+    total = base_ref[...] + y_ref[...].astype(f32)
+    out_ref[...] = (total + (one_ref[...].astype(f32) + two_ref[...].astype(f32))).astype(bf16)
+
+
+def head_kernel(f0, f1, f2, f3, g0, g1, g2, g3, out_ref):
+    total = nn(f0[...], g0[...]) + nn(f1[...], g1[...])
+    total = total + nn(f2[...], g2[...]) + nn(f3[...], g3[...])
     out_ref[...] = total.astype(bf16)
 
 
@@ -235,115 +289,82 @@
     def over_rows(x, flip):
         return lax.ppermute(x, "rows", [(i, i ^ flip) for i in range(rows_n)])
 
-    def over_blk(x, by):
-        return lax.ppermute(x, "blk", [(i, (i + by) % blks) for i in range(blks)])
-
-    pos = pos_index.T
-    w_hi = loss_weight.astype(bf16).astype(f32)
-    w_mid = (loss_weight - w_hi).astype(bf16).astype(f32)
-    meta = jnp.concatenate(
-        [
-            (labels >> 7)[None].astype(bf16),
-            (labels & 127)[None].astype(bf16),
-            (pos // n).astype(bf16),
-            (pos % n).astype(bf16),
-            w_hi[None].astype(bf16),
-            w_mid[None].astype(bf16),
-            (loss_weight - w_hi - w_mid)[None].astype(bf16),
+    def along(x, by, flip):
+        pairs = [
+            (b * rows_n + i, (b + by) % blks * rows_n + (i ^ flip))
+            for b in range(blks)
+            for i in range(rows_n)
         ]
-    )
-    meta = jnp.pad(meta, ((0, META - meta.shape[0]), (0, wide - n)))
-    (p0,) = call(
-        embed_kernel,
-        (features, head_weight, meta),
-        [shape(n + META, wide, dtype=bf16)],
-        flops=2 * n * depth * wide,
-        name="embed",
-    )
+        return lax.ppermute(x, ("blk", "rows"), pairs)
+
+    p0 = embed(features, head_weight, labels[None], pos_index.T, loss_weight[None])
     p2 = over_rows(p0, 2)
-    n1, n2 = over_blk(p0, 1), over_blk(p0, 2)
+    n1, n2 = along(p0, 1, 2), along(p0, 2, 0)
     p1 = over_rows(p0, 1)
-    p3 = over_rows(p2, 1)
-
+
+    features, _ = lax.optimization_barrier((features, p0))
+    m = blks * slice_rows
     turned = features.T.reshape(blks, rows_n, slice_rows, n)
     turned = [
-        lax.dynamic_index_in_dim(turned, me ^ j, 1, keepdims=False).reshape(blks * slice_rows, n)
-        for j in range(4)
+        lax.dynamic_index_in_dim(turned, me ^ j, 1, keepdims=False).reshape(m, n) for j in range(4)
     ]
-    f2 = over_rows(jnp.concatenate(turned[2:]), 2)
-    m = blks * slice_rows
-    f13 = over_rows(jnp.concatenate([turned[1], f2[m:]]), 1)
-    f2 = f2[:m]
+    f0 = turned[0]
+    p2, *turned = lax.optimization_barrier((p2, *turned))
+    p3 = over_rows(p2, 1)
+    f1 = over_rows(turned[1], 1)
+    f2, f3 = over_rows(turned[2], 2), over_rows(turned[3], 2)
 
     scal = jnp.concatenate([me[None].astype(jnp.int32), pair_mask[0]])
-    scratch = [
-        pltpu.VMEM((n, n), f32),
-        pltpu.VMEM((n, 128), f32),
-        pltpu.VMEM((n, 128), f32),
-        pltpu.VMEM((n, 128), f32),
-    ]
+    scratch = [pltpu.VMEM((n, n), f32)] + [pltpu.VMEM((n, 128), f32)] * 3
     tile = (p0, p1, p2, p3)
+    low_grad = shape(n, wide, dtype=bf16)
+    low_coef = shape(n, 4 * n, dtype=bf16)
     anchors, c0, sums, own_grad = call(
         own_kernel,
         (scal, *tile),
-        [shape(8, 4 * n), shape(n, 4 * n, dtype=bf16), shape(8, 4 * n), shape(n, wide)],
+        [shape(8, 4 * n), low_coef, shape(8, 4 * n), shape(n, wide)],
         scratch,
-        flops=2 * n * n * wide * 40,
-        name="own_block",
-    )
-    c1, c2, sums, grad1, grad2 = call(
+        micros=OWN_US, name="own_block",
+    )
+    f2, f3, sums = lax.optimization_barrier((f2, f3, sums))
+    f3 = over_rows(f3, 1)
+    c1, c2, s0, grad1, grad2 = call(
         earlier_kernel,
         (scal, n1, n2, *tile, anchors, sums),
-        [
-            shape(n, 4 * n, dtype=bf16),
-            shape(n, 4 * n, dtype=bf16),
-            shape(8, 4 * n),
-            shape(n, wide, dtype=bf16),
-            shape(n, wide, dtype=bf16),
-        ],
+        [low_coef, low_coef, shape(8, 4 * n), low_grad, low_grad],
         scratch,
-        flops=2 * n * n * wide * 40,
-        name="earlier_blocks",
-    )
-    grad1, grad2 = over_blk(grad1, -1), over_blk(grad2, -2)
+        micros=8.0, name="earlier_blocks",
+    )
+    s1, s2 = over_rows(s0, 1), over_rows(s0, 2)
+    grad1, grad2 = along(grad1, -1, 2), along(grad2, -2, 0)
+    pieces = (c0, c1, c2, p0, n1, n2)
+    rows_f32 = [shape(n, wide), shape(n, wide)]
     keep, send = call(
-        anchor_kernel,
-        (c0, c1, c2, p0, n1, n2),
-        [shape(2 * n, wide), shape(2 * n, wide)],
-        flops=2 * n * n * wide * 12,
-        name="anchor_grad",
-    )
-    half = keep + over_rows(send, 1)
-    from_y = over_rows(half[n:].astype(bf16), 2)
-
-    other = over_rows(sums, 1).reshape(8, 2, 2, n)[:, :, ::-1].reshape(8, 4 * n)
-    sums = sums + other
-    other = over_rows(sums, 2).reshape(8, 2, 2 * n)[:, ::-1].reshape(8, 4 * n)
-    sums = sums + other
-    anchor_loss = sums[3, :n] / (SMOOTHING_SCALE * 3 * 4 * n)
-    own_where = (((pos_index // n) ^ me) * n + pos_index % n).astype(f32)
-    (base,) = call(
+        functools.partial(anchor_kernel, 2), pieces, rows_f32, micros=1.3, name="anchor_grad_across"
+    )
+    (half,) = call(halved_kernel, (keep, over_rows(send, 1)), [low_grad], micros=0.5, name="half_sum")
+    from_y = over_rows(half, 2)
+    keep, send = call(functools.partial(anchor_kernel, 0), pieces, rows_f32, micros=1.3, name="anchor_grad_own")
+    s3 = over_rows(s2, 1)
+    base, anchor_loss = call(
         listed_kernel,
-        (anchors, sums, own_where, sums[:, :n].T, *tile, half[:n] + own_grad),
-        [shape(n, wide)],
-        flops=2 * n * n * wide * 8,
-        name="listed",
-    )
-    total = base + from_y.astype(f32) + grad1.astype(f32) + grad2.astype(f32)
-    g0 = total.astype(bf16)
+        (anchors, s0, s1, s2, s3, *tile, keep, over_rows(send, 1), own_grad),
+        [shape(n, wide), shape(1, n)],
+        micros=2.0, name="listed",
+    )
+    (g0,) = call(gathered_kernel, (base, from_y, grad1, grad2), [low_grad], micros=0.7, name="row_grad")
     g2 = over_rows(g0, 2)
     g1 = over_rows(g0, 1)
     g3 = over_rows(g2, 1)
     (part,) = call(
         head_kernel,
-        (turned[0], f2, f13, g0, g1, g2, g3),
+        (f0, f1, f2, f3, g0, g1, g2, g3),
         [shape(m, wide, dtype=bf16)],
-        flops=2 * m * 4 * n * wide,
-        name="head_grad",
+        micros=1.5, name="head_grad",
     )
     parts = lax.all_to_all(part, "blk", split_axis=0, concat_axis=0, tiled=True)
     weight_grad = jnp.sum(parts.reshape(blks, slice_rows, wide).astype(f32), axis=0)
-    return anchor_loss, weight_grad
+    return anchor_loss[0], weight_grad
 
 
 def solution(mesh):

time: 169 us -> 124 us (0.73)
  blocking collectives: 0 us -> 32.1 us
  waiting for transfers between devices: 66.9 us -> 39.3 us
  local copies, waits for them, and re-layouts: 16.6 us -> 0.67 us
  Pallas kernels: 37.2 us -> 25.1 us
  other arithmetic: 12.3 us -> 0.82 us
  starting transfers between devices: 34.1 us -> 24.8 us
    all_to_all x0 -> x1, blocking collectives: none -> 32.1 us  [local(): parts = lax.all_to_all(part, 'blk', split_axis=0, concat_axis=0, tiled=True)]
    all_to_all x1 -> x0, waiting for transfers between devices: 23.6 us -> none  [local(): parts = lax.all_to_all(part, 'blk', split_axis=0, concat_axis=0, tiled=True)]
    pallas_call x6 -> x8, Pallas kernels: 37.2 us -> 20.5 us  [call(): pl.pallas_call(kernel, out_shape=outs, in_specs=[SMEM if x.ndim == 1 else...]
    all_to_all x1 -> x0, starting transfers between devices: 9.69 us -> none  [local(): parts = lax.all_to_all(part, 'blk', split_axis=0, concat_axis=0, tiled=True)]
    unnamed x44 -> x6, local copies, waits for them, and re-layouts: 9.01 us -> 0.01 us
    convert_element_type x5 -> x0, other arithmetic: 4.65 us -> none  [the longest x1 1.45 us: local(): g0 = total.astype(bf16)]
    pallas_call x0 -> x1, Pallas kernels: none -> 4.6 us  [embed(): pl.pallas_call(embed_kernel, grid=(wide // step,), out_shape=shape(n + ME...]
    add x4 -> x0, other arithmetic: 4.31 us -> none  [the longest x1 1.84 us: local(): half = keep + over_rows(send, 1)]
  transfers between devices with their start and end apart: 17 -> 20, of which waited for: 8 -> 12; matrix products, arithmetic and copies ran while one was open for 11% -> 1% of each run, Pallas kernels for 7% -> 7%
where the time goes in v2:
time: 124 us
  waiting for transfers between devices  39.3 us (32%)
  blocking collectives  32.1 us (26%)
  Pallas kernels  25.1 us (20%)
  starting transfers between devices  24.8 us (20%)
    ppermute x16, waiting for transfers between devices, over_rows(): return lax.ppermute(x, 'rows', [(i, i ^ flip) for i in range(rows_n)])  36.4 us
    all_to_all x1, blocking collectives, local(): parts = lax.all_to_all(part, 'blk', split_axis=0, concat_axis=0, tiled=True)  32.1 us
    pallas_call x8, Pallas kernels, call(): pl.pallas_call(kernel, out_shape=outs, in_specs=[SMEM if x.ndim == 1 else...  20.5 us
    ppermute x4, starting transfers between devices, along(): return lax.ppermute(x, ('blk', 'rows'), pairs)  14.8 us
    ppermute x16, starting transfers between devices, over_rows(): return lax.ppermute(x, 'rows', [(i, i ^ flip) for i in range(rows_n)])  10 us
    pallas_call x1, Pallas kernels, embed(): pl.pallas_call(embed_kernel, grid=(wide // step,), out_shape=shape(n + ME...  4.6 us
    ppermute x4, waiting for transfers between devices, along(): return lax.ppermute(x, ('blk', 'rows'), pairs)  2.9 us
  transfers between devices with their start and end apart: 20, of which 12 were waited for; matrix products, arithmetic and copies ran while one was open for 1% of the time, Pallas kernels for 7%

profile of v2, /device:TPU:8, one launch (start us, length us, event | category | flops | bytes accessed | tf_op | source)
XLA Modules:
  0.0 123.5 jit_solution(8452404628278706813)
XLA Ops:
  0.6 4.6 %embed.1.p0.n0 = bf16[272,768]{1,0:T(8,128)(2,1)} custom-call(bf16[256,2048]{1,0:T(8,128)(2,1)} %features_ref.1, bf16[2048,768]{1,0:T(8,128)(2,1)} %weight_ref.1, s32[1,256]{1,0:T(1,128)} %bitcast.21, s32[3,256]{1,0:T(4,128)} %bitcast.20, f32[1,256]{1,0:T(1,128)} %bitcast.22), custom_call_target="tpu_custom_call" | custom-call | flops 1073741824 | bytes 4194304 | tf_op jit(solution)/shard_map/embed/pallas_call | solution.py:75
  5.2 2.2 %collective-permute-start.1 = (bf16[272,768]{1,0:T(8,128)(2,1)}, bf16[272,768]{1,0:T(8,128)(2,1)S(1)}, u32[]{:S(2)}, u32[]{:S(2)}) collective-permute-start(bf16[272,768]{1,0:T(8,128)(2,1)} %embed.1.p0.n0), channel_id=1, source_target_pairs={{0,2},{1,3},{2,0},{3,1},{4,6},{5,7},{6,4},{7,5},{8,10},{9,11},{10,... | collective-permute-start | bytes 1253384 | tf_op jit(solution)/shard_map/ppermute | solution.py:290
  7.4 0.5 copy.12
  8.1 8.7 %collective-permute-done.1.p2 = bf16[272,768]{1,0:T(8,128)(2,1)S(1)} collective-permute-done((bf16[272,768]{1,0:T(8,128)(2,1)}, bf16[272,768]{1,0:T(8,128)(2,1)S(1)}, u32[]{:S(2)}, u32[]{:S(2)}) %collective-permute-start.1) | collective-permute-done | bytes 417824 | tf_op jit(solution)/shard_map/ppermute | solution.py:290
  16.8 1.6 %collective-permute-start.3 = (bf16[272,768]{1,0:T(8,128)(2,1)S(1)}, bf16[272,768]{1,0:T(8,128)(2,1)S(1)}, u32[]{:S(2)}, u32[]{:S(2)}) collective-permute-start(bf16[272,768]{1,0:T(8,128)(2,1)S(1)} %copy-done), channel_id=1, source_target_pairs={{0,6},{1,7},{2,4},{3,5},{4,10},{5,11},{6,8},{7,9},{8,14},{9,15},{1... | collective-permute-start | bytes 1253384 | tf_op jit(solution)/shard_map/ppermute | solution.py:298
  18.4 1.9 %collective-permute-start.4 = (bf16[272,768]{1,0:T(8,128)(2,1)S(1)}, bf16[272,768]{1,0:T(8,128)(2,1)S(1)}, u32[]{:S(2)}, u32[]{:S(2)}) collective-permute-start(bf16[272,768]{1,0:T(8,128)(2,1)S(1)} %copy-done), channel_id=1, source_target_pairs={{0,8},{1,9},{2,10},{3,11},{4,12},{5,13},{6,14},{7,15},{8,16},{9,17... | collective-permute-start | bytes 1253384 | tf_op jit(solution)/shard_map/ppermute | solution.py:298
  20.4 1.9 %collective-permute-start.5 = (bf16[512,256]{1,0:T(8,128)(2,1)S(1)}, bf16[512,256]{1,0:T(8,128)(2,1)S(1)}, u32[]{:S(2)}, u32[]{:S(2)}) collective-permute-start(bf16[512,256]{1,0:T(8,128)(2,1)S(1)} %get-tuple-element.28), channel_id=1, source_target_pairs={{0,2},{1,3},{2,0},{3,1},{4,6},{5,7},{6,4},{7,5},{8,10},{9,11},{10,... | collective-permute-start | bytes 786440 | tf_op jit(solution)/shard_map/ppermute | solution.py:290
  22.6 6.1 %own_block.1 = (f32[8,1024]{1,0:T(8,128)S(1)}, bf16[256,1024]{1,0:T(8,128)(2,1)S(1)}, f32[8,1024]{1,0:T(8,128)S(1)}, f32[256,768]{1,0:T(8,128)S(1)}) custom-call(s32[4]{0:T(128)S(1)} %pad_add_fusion.scal_ref, bf16[272,768]{1,0:T(8,128)(2,1)S(1)} %copy-done, bf16[272,768]{1,0:T(8,128)(2,1)S(1)} %collective-permute-done.p1, ...), custom_call_target="tpu_custom_call" | custom-call | flops 3449999872 | bytes 1024 | tf_op jit(solution)/shard_map/own_block/pallas_call | solution.py:26
  28.7 0.9 collective-permute-done.5.f2
  29.6 4.8 %collective-permute-done.6 = bf16[512,256]{1,0:T(8,128)(2,1)S(1)} collective-permute-done((bf16[512,256]{1,0:T(8,128)(2,1)S(1)}, bf16[512,256]{1,0:T(8,128)(2,1)S(1)}, u32[]{:S(2)}, u32[]{:S(2)}) %collective-permute-start.6) | collective-permute-done | bytes 262176 | tf_op jit(solution)/shard_map/ppermute | solution.py:290
  34.4 2.0 %collective-permute-done.3.n1 = bf16[272,768]{1,0:T(8,128)(2,1)S(1)} collective-permute-done((bf16[272,768]{1,0:T(8,128)(2,1)S(1)}, bf16[272,768]{1,0:T(8,128)(2,1)S(1)}, u32[]{:S(2)}, u32[]{:S(2)}) %collective-permute-start.3) | collective-permute-done | bytes 417824 | tf_op jit(solution)/shard_map/ppermute | solution.py:298
  36.5 9.4 %earlier_blocks.1 = (bf16[256,1024]{1,0:T(8,128)(2,1)S(1)}, bf16[256,1024]{1,0:T(8,128)(2,1)S(1)}, f32[8,1024]{1,0:T(8,128)S(1)}, bf16[256,768]{1,0:T(8,128)(2,1)S(1)}, bf16[256,768]{1,0:T(8,128)(2,1)S(1)}) custom-call(s32[4]{0:T(128)S(1)} %pad_add_fusion.scal_ref, bf16[272,768]{1,0:T(8,128)(2,1)S(1)} %collective-permute-done.3.n1, ...), custom_call_target="tpu_custom_call" | custom-call | flops 9200000000 | bytes 1024 | tf_op jit(solution)/shard_map/earlier_blocks/pallas_call | solution.py:26
  46.0 0.8 anchor_grad_across.1
  46.9 0.8 anchor_grad_own.1
  47.7 0.6 collective-permute-start.10
  48.3 10.3 %collective-permute-start.15 = (bf16[256,768]{1,0:T(8,128)(2,1)S(1)}, bf16[256,768]{1,0:T(8,128)(2,1)S(1)}, u32[]{:S(2)}, u32[]{:S(2)}) collective-permute-start(bf16[256,768]{1,0:T(8,128)(2,1)S(1)} %get-tuple-element.46), channel_id=1, source_target_pairs={{0,254},{1,255},{2,252},{3,253},{4,2},{5,3},{6,0},{7,1},{8,6},{9,7... | collective-permute-start | bytes 1179656 | tf_op jit(solution)/shard_map/ppermute | solution.py:298
  58.6 1.0 collective-permute-start.16
  59.7 2.0 %collective-permute-start.14 = (bf16[256,768]{1,0:T(8,128)(2,1)S(1)}, bf16[256,768]{1,0:T(8,128)(2,1)S(1)}, u32[]{:S(2)}, u32[]{:S(2)}) collective-permute-start(bf16[256,768]{1,0:T(8,128)(2,1)S(1)} %half_sum.1), channel_id=1, source_target_pairs={{0,2},{1,3},{2,0},{3,1},{4,6},{5,7},{6,4},{7,5},{8,10},{9,11},{10,... | collective-permute-start | bytes 1179656 | tf_op jit(solution)/shard_map/ppermute | solution.py:290
  61.7 0.4 collective-permute-start.8
  62.1 9.2 %collective-permute-done.8.s2 = f32[8,1024]{1,0:T(8,128)S(1)} collective-permute-done((f32[8,1024]{1,0:T(8,128)S(1)}, f32[8,1024]{1,0:T(8,128)S(1)}, u32[]{:S(2)}, u32[]{:S(2)}) %collective-permute-start.8) | collective-permute-done | bytes 32800 | tf_op jit(solution)/shard_map/ppermute | solution.py:290
  71.3 1.2 collective-permute-done.7.s1
  72.7 1.0 collective-permute-done.9.s3
  73.7 2.0 %listed.1 = (f32[256,768]{1,0:T(8,128)S(1)}, f32[1,256]{1,0:T(1,128)}) custom-call(f32[8,1024]{1,0:T(8,128)S(1)} %get-tuple-element.27.anchors_ref, f32[8,1024]{1,0:T(8,128)S(1)} %get-tuple-element.32.s0, f32[8,1024]{1,0:T(8,128)S(1)} %collective-permute-done.7.s1, f32[8,1024]{1,0:T(8,128)S(1)} %collective-permute-done.8.s2, ...), custom_call_target="tpu_custom_call" | custom-call | flops 2300000000 | bytes 1024 | tf_op jit(solution)/shard_map/listed/pallas_call | solution.py:26
  75.7 0.8 collective-permute-done.16.two_ref
  76.7 2.0 %collective-permute-start.18 = (bf16[256,768]{1,0:T(8,128)(2,1)S(1)}, bf16[256,768]{1,0:T(8,128)(2,1)S(1)}, u32[]{:S(2)}, u32[]{:S(2)}) collective-permute-start(bf16[256,768]{1,0:T(8,128)(2,1)S(1)} %row_grad.1.g0), channel_id=1, source_target_pairs={{0,2},{1,3},{2,0},{3,1},{4,6},{5,7},{6,4},{7,5},{8,10},{9,11},{10,... | collective-permute-start | bytes 1179656 | tf_op jit(solution)/shard_map/ppermute | solution.py:290
  78.7 8.5 %collective-permute-done.18.g2 = bf16[256,768]{1,0:T(8,128)(2,1)S(1)} collective-permute-done((bf16[256,768]{1,0:T(8,128)(2,1)S(1)}, bf16[256,768]{1,0:T(8,128)(2,1)S(1)}, u32[]{:S(2)}, u32[]{:S(2)}) %collective-permute-start.18) | collective-permute-done | bytes 393248 | tf_op jit(solution)/shard_map/ppermute | solution.py:290
  87.2 0.5 collective-permute-start.11
  87.7 1.6 %collective-permute-done.11.f1 = bf16[512,256]{1,0:T(8,128)(2,1)S(1)} collective-permute-done((bf16[512,256]{1,0:T(8,128)(2,1)S(1)}, bf16[512,256]{1,0:T(8,128)(2,1)S(1)}, u32[]{:S(2)}, u32[]{:S(2)}) %collective-permute-start.11) | collective-permute-done | bytes 262176 | tf_op jit(solution)/shard_map/ppermute | solution.py:290
  89.3 0.4 collective-permute-done.12.f3
  89.7 1.0 head_grad.1
  90.7 32.1 %all_to_all.9 = bf16[64,8,768]{2,1,0:T(8,128)(2,1)S(1)} all-to-all(bf16[64,8,768]{2,1,0:T(8,128)(2,1)S(1)} %bitcast.18), channel_id=1, replica_groups=mesh['blk'=64,'rows'=4] {'blk'}, dimensions={0} | all-to-all | bytes 1572864 | tf_op jit(solution)/shard_map/all_to_all | solution.py:365
  122.8 0.7 convert_reduce_fusion
  (28 shorter events, 1.2 us)
Async XLA Ops:
  0.6 6.8 %copy-start.1 = (bf16[256,2048]{1,0:T(8,128)(2,1)S(1)}, bf16[256,2048]{1,0:T(8,128)(2,1)}, u32[]{:S(2)}) copy-start(bf16[256,2048]{1,0:T(8,128)(2,1)} %features_ref.1) | copy-start | bytes 3145732
  5.2 11.6 %copy-start = (bf16[272,768]{1,0:T(8,128)(2,1)S(1)}, bf16[272,768]{1,0:T(8,128)(2,1)}, u32[]{:S(2)}) copy-start(bf16[272,768]{1,0:T(8,128)(2,1)} %embed.1.p0.n0) | copy-start | bytes 1253380
  5.2 15.1 %copy-start.2 = (s32[1,3]{1,0:T(1,128)S(1)}, s32[1,3]{1,0:T(1,128)}, u32[]{:S(2)}) copy-start(s32[1,3]{1,0:T(1,128)} %param.10) | copy-start | bytes 40
  5.2 11.6 %collective-permute-start.1 = (bf16[272,768]{1,0:T(8,128)(2,1)}, bf16[272,768]{1,0:T(8,128)(2,1)S(1)}, u32[]{:S(2)}, u32[]{:S(2)}) collective-permute-start(bf16[272,768]{1,0:T(8,128)(2,1)} %embed.1.p0.n0), channel_id=1, source_target_pairs={{0,2},{1,3},{2,0},{3,1},{4,6},{5,7},{6,4},{7,5},{8,10},{9,11},{10,... | collective-permute-start | bytes 1253384 | tf_op jit(solution)/shard_map/ppermute | solution.py:290
  7.4 14.9 %collective-permute-start = (bf16[272,768]{1,0:T(8,128)(2,1)}, bf16[272,768]{1,0:T(8,128)(2,1)S(1)}, u32[]{:S(2)}, u32[]{:S(2)}) collective-permute-start(bf16[272,768]{1,0:T(8,128)(2,1)} %embed.1.p0.n0), channel_id=1, source_target_pairs={{0,1},{1,0},{2,3},{3,2},{4,5},{5,4},{6,7},{7,6},{8,9},{9,8},{10,11... | collective-permute-start | bytes 1253384 | tf_op jit(solution)/shard_map/ppermute | solution.py:290
  16.8 5.8 %collective-permute-start.2 = (bf16[272,768]{1,0:T(8,128)(2,1)S(1)}, bf16[272,768]{1,0:T(8,128)(2,1)S(1)}, u32[]{:S(2)}, u32[]{:S(2)}) collective-permute-start(bf16[272,768]{1,0:T(8,128)(2,1)S(1)} %collective-permute-done.1.p2), channel_id=1, source_target_pairs={{0,1},{1,0},{2,3},{3,2},{4,5},{5,4},{6,7},{7,6},{8,9},{9,8},{10,11... | collective-permute-start | bytes 1253384 | tf_op jit(solution)/shard_map/ppermute | solution.py:290
  16.8 19.6 %collective-permute-start.3 = (bf16[272,768]{1,0:T(8,128)(2,1)S(1)}, bf16[272,768]{1,0:T(8,128)(2,1)S(1)}, u32[]{:S(2)}, u32[]{:S(2)}) collective-permute-start(bf16[272,768]{1,0:T(8,128)(2,1)S(1)} %copy-done), channel_id=1, source_target_pairs={{0,6},{1,7},{2,4},{3,5},{4,10},{5,11},{6,8},{7,9},{8,14},{9,15},{1... | collective-permute-start | bytes 1253384 | tf_op jit(solution)/shard_map/ppermute | solution.py:298
  18.4 18.1 %collective-permute-start.4 = (bf16[272,768]{1,0:T(8,128)(2,1)S(1)}, bf16[272,768]{1,0:T(8,128)(2,1)S(1)}, u32[]{:S(2)}, u32[]{:S(2)}) collective-permute-start(bf16[272,768]{1,0:T(8,128)(2,1)S(1)} %copy-done), channel_id=1, source_target_pairs={{0,8},{1,9},{2,10},{3,11},{4,12},{5,13},{6,14},{7,15},{8,16},{9,17... | collective-permute-start | bytes 1253384 | tf_op jit(solution)/shard_map/ppermute | solution.py:298
  20.4 9.2 %collective-permute-start.5 = (bf16[512,256]{1,0:T(8,128)(2,1)S(1)}, bf16[512,256]{1,0:T(8,128)(2,1)S(1)}, u32[]{:S(2)}, u32[]{:S(2)}) collective-permute-start(bf16[512,256]{1,0:T(8,128)(2,1)S(1)} %get-tuple-element.28), channel_id=1, source_target_pairs={{0,2},{1,3},{2,0},{3,1},{4,6},{5,7},{6,4},{7,5},{8,10},{9,11},{10,... | collective-permute-start | bytes 786440 | tf_op jit(solution)/shard_map/ppermute | solution.py:290
  22.3 12.0 %collective-permute-start.6 = (bf16[512,256]{1,0:T(8,128)(2,1)S(1)}, bf16[512,256]{1,0:T(8,128)(2,1)S(1)}, u32[]{:S(2)}, u32[]{:S(2)}) collective-permute-start(bf16[512,256]{1,0:T(8,128)(2,1)S(1)} %get-tuple-element.29), channel_id=1, source_target_pairs={{0,2},{1,3},{2,0},{3,1},{4,6},{5,7},{6,4},{7,5},{8,10},{9,11},{10,... | collective-permute-start | bytes 786440 | tf_op jit(solution)/shard_map/ppermute | solution.py:290
  46.8 12.8 %collective-permute-start.13 = (f32[256,768]{1,0:T(8,128)S(1)}, f32[256,768]{1,0:T(8,128)S(1)}, u32[]{:S(2)}, u32[]{:S(2)}) collective-permute-start(f32[256,768]{1,0:T(8,128)S(1)} %get-tuple-element.45), channel_id=1, source_target_pairs={{0,1},{1,0},{2,3},{3,2},{4,5},{5,4},{6,7},{7,6},{8,9},{9,8},{10,11... | collective-permute-start | bytes 2359304 | tf_op jit(solution)/shard_map/ppermute | solution.py:290
  47.7 26.0 %collective-permute-start.10 = (f32[256,768]{1,0:T(8,128)S(1)}, f32[256,768]{1,0:T(8,128)S(1)}, u32[]{:S(2)}, u32[]{:S(2)}) collective-permute-start(f32[256,768]{1,0:T(8,128)S(1)} %get-tuple-element.37), channel_id=1, source_target_pairs={{0,1},{1,0},{2,3},{3,2},{4,5},{5,4},{6,7},{7,6},{8,9},{9,8},{10,11... | collective-permute-start | bytes 2359304 | tf_op jit(solution)/shard_map/ppermute | solution.py:290
  48.3 27.4 %collective-permute-start.15 = (bf16[256,768]{1,0:T(8,128)(2,1)S(1)}, bf16[256,768]{1,0:T(8,128)(2,1)S(1)}, u32[]{:S(2)}, u32[]{:S(2)}) collective-permute-start(bf16[256,768]{1,0:T(8,128)(2,1)S(1)} %get-tuple-element.46), channel_id=1, source_target_pairs={{0,254},{1,255},{2,252},{3,253},{4,2},{5,3},{6,0},{7,1},{8,6},{9,7... | collective-permute-start | bytes 1179656 | tf_op jit(solution)/shard_map/ppermute | solution.py:298
  58.6 17.9 %collective-permute-start.16 = (bf16[256,768]{1,0:T(8,128)(2,1)S(1)}, bf16[256,768]{1,0:T(8,128)(2,1)S(1)}, u32[]{:S(2)}, u32[]{:S(2)}) collective-permute-start(bf16[256,768]{1,0:T(8,128)(2,1)S(1)} %get-tuple-element.47), channel_id=1, source_target_pairs={{0,248},{1,249},{2,250},{3,251},{4,252},{5,253},{6,254},{7,255},{8... | collective-permute-start | bytes 1179656 | tf_op jit(solution)/shard_map/ppermute | solution.py:298
  59.7 16.8 %collective-permute-start.14 = (bf16[256,768]{1,0:T(8,128)(2,1)S(1)}, bf16[256,768]{1,0:T(8,128)(2,1)S(1)}, u32[]{:S(2)}, u32[]{:S(2)}) collective-permute-start(bf16[256,768]{1,0:T(8,128)(2,1)S(1)} %half_sum.1), channel_id=1, source_target_pairs={{0,2},{1,3},{2,0},{3,1},{4,6},{5,7},{6,4},{7,5},{8,10},{9,11},{10,... | collective-permute-start | bytes 1179656 | tf_op jit(solution)/shard_map/ppermute | solution.py:290
  61.7 9.6 %collective-permute-start.8 = (f32[8,1024]{1,0:T(8,128)S(1)}, f32[8,1024]{1,0:T(8,128)S(1)}, u32[]{:S(2)}, u32[]{:S(2)}) collective-permute-start(f32[8,1024]{1,0:T(8,128)S(1)} %get-tuple-element.32.s0), channel_id=1, source_target_pairs={{0,2},{1,3},{2,0},{3,1},{4,6},{5,7},{6,4},{7,5},{8,10},{9,11},{10,... | collective-permute-start | bytes 98312 | tf_op jit(solution)/shard_map/ppermute | solution.py:290
  71.3 1.2 collective-permute-start.7
  72.5 1.2 collective-permute-start.9
  76.7 10.5 %collective-permute-start.18 = (bf16[256,768]{1,0:T(8,128)(2,1)S(1)}, bf16[256,768]{1,0:T(8,128)(2,1)S(1)}, u32[]{:S(2)}, u32[]{:S(2)}) collective-permute-start(bf16[256,768]{1,0:T(8,128)(2,1)S(1)} %row_grad.1.g0), channel_id=1, source_target_pairs={{0,2},{1,3},{2,0},{3,1},{4,6},{5,7},{6,4},{7,5},{8,10},{9,11},{10,... | collective-permute-start | bytes 1179656 | tf_op jit(solution)/shard_map/ppermute | solution.py:290
  78.7 11.0 %collective-permute-start.17 = (bf16[256,768]{1,0:T(8,128)(2,1)S(1)}, bf16[256,768]{1,0:T(8,128)(2,1)S(1)}, u32[]{:S(2)}, u32[]{:S(2)}) collective-permute-start(bf16[256,768]{1,0:T(8,128)(2,1)S(1)} %row_grad.1.g0), channel_id=1, source_target_pairs={{0,1},{1,0},{2,3},{3,2},{4,5},{5,4},{6,7},{7,6},{8,9},{9,8},{10,11... | collective-permute-start | bytes 1179656 | tf_op jit(solution)/shard_map/ppermute | solution.py:290
  87.2 2.5 %collective-permute-start.19 = (bf16[256,768]{1,0:T(8,128)(2,1)S(1)}, bf16[256,768]{1,0:T(8,128)(2,1)S(1)}, u32[]{:S(2)}, u32[]{:S(2)}) collective-permute-start(bf16[256,768]{1,0:T(8,128)(2,1)S(1)} %collective-permute-done.18.g2), channel_id=1, source_target_pairs={{0,1},{1,0},{2,3},{3,2},{4,5},{5,4},{6,7},{7,6},{8,9},{9,8},{10,11... | collective-permute-start | bytes 1179656 | tf_op jit(solution)/shard_map/ppermute | solution.py:290
  87.2 2.1 %collective-permute-start.11 = (bf16[512,256]{1,0:T(8,128)(2,1)S(1)}, bf16[512,256]{1,0:T(8,128)(2,1)S(1)}, u32[]{:S(2)}, u32[]{:S(2)}) collective-permute-start(bf16[512,256]{1,0:T(8,128)(2,1)S(1)} %get-tuple-element.40), channel_id=1, source_target_pairs={{0,1},{1,0},{2,3},{3,2},{4,5},{5,4},{6,7},{7,6},{8,9},{9,8},{10,11... | collective-permute-start | bytes 786440 | tf_op jit(solution)/shard_map/ppermute | solution.py:290
  87.7 2.0 %collective-permute-start.12 = (bf16[512,256]{1,0:T(8,128)(2,1)S(1)}, bf16[512,256]{1,0:T(8,128)(2,1)S(1)}, u32[]{:S(2)}, u32[]{:S(2)}) collective-permute-start(bf16[512,256]{1,0:T(8,128)(2,1)S(1)} %collective-permute-done.6), channel_id=1, source_target_pairs={{0,1},{1,0},{2,3},{3,2},{4,5},{5,4},{6,7},{7,6},{8,9},{9,8},{10,11... | collective-permute-start | bytes 786440 | tf_op jit(solution)/shard_map/ppermute | solution.py:290

commit v3 on v2

--- a/solution.py
+++ b/solution.py
@@ -13,7 +13,6 @@
 BASE2 = SMOOTHING_SCALE / LN2
 MASKED = 1e30
 META = 16
-OWN_US = 3.0
 CHUNK = 16
 f32 = jnp.float32
 bf16 = jnp.bfloat16
@@ -71,7 +70,8 @@
 
 def embed(features, head_weight, labels, pos, loss_weight):
     n, depth = features.shape
-    wide, step = head_weight.shape[1], n
+    wide = head_weight.shape[1]
+    step = wide // 2
     return pl.pallas_call(
         embed_kernel,
         grid=(wide // step,),
@@ -160,8 +160,8 @@
     return ref[n : n + META, :n].astype(f32)[i : i + 1, :]
 
 
-def own_kernel(
-    scal_ref, p0, p1, p2, p3, anchors_ref, coef_ref, sums_ref, grad_ref,
+def score_kernel(
+    scal_ref, p0, p1, p2, p3, n1, n2, anchors_ref, c0, c1, c2, sums_ref, grad0, grad1, grad2,
     products_ref, lanes_ref, sq_ref, label_ref,
 ):
     blocks = (p0, p1, p2, p3)
@@ -193,34 +193,20 @@
         weight = meta[8:9, :] + meta[9:10, :] + meta[10:11, :]
         anchors_ref[6:7, lanes] = weight * scale
         anchors_ref[7:8, lanes] = meta[0:1, :] * 128.0 + meta[1:2, :]
-    label_ref[...] = jnp.broadcast_to(column(anchors_ref[7:8, :n]), label_ref.shape)
     sums_ref[...] = jnp.zeros_like(sums_ref)
-    score_block(
-        tile[0], scal_ref[1] > 0, tile, anchors_ref, label_ref, products_ref, coef_ref, lanes_ref,
-        sq_ref, sums_ref,
-    )
-    grad_ref[...] = negative_grad(tile[0], tile, coef_ref, lanes_ref)
-
-
-def earlier_kernel(
-    scal_ref, n1, n2, p0, p1, p2, p3, anchors_ref, before_ref, coef1, coef2, sums_ref, grad1, grad2,
-    products_ref, lanes_ref, sq_ref, label_ref,
-):
-    n = p0.shape[0] - META
-    tile = [p[:n, :] for p in (p0, p1, p2, p3)]
-    sums_ref[...] = before_ref[...]
-    for s, (p, coef_ref, grad_ref) in enumerate(((n1, coef1, grad1), (n2, coef2, grad2))):
+    negatives = ((p0, c0, grad0), (n1, c1, grad1), (n2, c2, grad2))
+    for offset, (p, coef_ref, grad_ref) in enumerate(negatives):
         labels = meta_row(p, n, 0) * 128.0 + meta_row(p, n, 1)
         label_ref[...] = jnp.broadcast_to(column(labels), label_ref.shape)
         rows_n = p[:n, :]
         score_block(
-            rows_n, scal_ref[2 + s] > 0, tile, anchors_ref, label_ref, products_ref, coef_ref,
+            rows_n, scal_ref[1 + offset] > 0, tile, anchors_ref, label_ref, products_ref, coef_ref,
             lanes_ref, sq_ref, sums_ref,
         )
-        grad_ref[...] = negative_grad(rows_n, tile, coef_ref, lanes_ref).astype(bf16)
-    weight = anchors_ref[6:7, :]
+        grad = negative_grad(rows_n, tile, coef_ref, lanes_ref)
+        grad_ref[...] = grad.astype(grad_ref.dtype)
     for k in range(3):
-        sums_ref[k : k + 1, :] = sums_ref[k : k + 1, :] * weight
+        sums_ref[k : k + 1, :] = sums_ref[k : k + 1, :] * anchors_ref[6:7, :]
 
 
 def anchor_kernel(first, c0, c1, c2, n0, n1, n2, keep_ref, send_ref):
@@ -319,40 +305,45 @@
     tile = (p0, p1, p2, p3)
     low_grad = shape(n, wide, dtype=bf16)
     low_coef = shape(n, 4 * n, dtype=bf16)
-    anchors, c0, sums, own_grad = call(
-        own_kernel,
-        (scal, *tile),
-        [shape(8, 4 * n), low_coef, shape(8, 4 * n), shape(n, wide)],
+    anchors, c0, c1, c2, s0, own_grad, grad1, grad2 = call(
+        score_kernel,
+        (scal, *tile, n1, n2),
+        [shape(8, 4 * n)] + [low_coef] * 3 + [shape(8, 4 * n), shape(n, wide)] + [low_grad] * 2,
         scratch,
-        micros=OWN_US, name="own_block",
-    )
-    f2, f3, sums = lax.optimization_barrier((f2, f3, sums))
-    f3 = over_rows(f3, 1)
-    c1, c2, s0, grad1, grad2 = call(
-        earlier_kernel,
-        (scal, n1, n2, *tile, anchors, sums),
-        [low_coef, low_coef, shape(8, 4 * n), low_grad, low_grad],
-        scratch,
-        micros=8.0, name="earlier_blocks",
-    )
-    s1, s2 = over_rows(s0, 1), over_rows(s0, 2)
-    grad1, grad2 = along(grad1, -1, 2), along(grad2, -2, 0)
+        micros=14.0,
+        name="score",
+    )
+    c0, f2, f3 = lax.optimization_barrier((c0, f2, f3))
+    s2 = over_rows(s0, 2)
+    s1 = over_rows(s0, 1)
     pieces = (c0, c1, c2, p0, n1, n2)
     rows_f32 = [shape(n, wide), shape(n, wide)]
     keep, send = call(
         functools.partial(anchor_kernel, 2), pieces, rows_f32, micros=1.3, name="anchor_grad_across"
     )
-    (half,) = call(halved_kernel, (keep, over_rows(send, 1)), [low_grad], micros=0.5, name="half_sum")
+    keep, f1 = lax.optimization_barrier((keep, f1))
+    c0, s2 = lax.optimization_barrier((c0, s2))
+    (half,) = call(
+        halved_kernel, (keep, over_rows(send, 1)), [low_grad], micros=0.5, name="half_sum"
+    )
+    half, grad1, grad2 = lax.optimization_barrier((half, grad1, grad2))
     from_y = over_rows(half, 2)
-    keep, send = call(functools.partial(anchor_kernel, 0), pieces, rows_f32, micros=1.3, name="anchor_grad_own")
-    s3 = over_rows(s2, 1)
+    grad1, grad2 = along(grad1, -1, 2), along(grad2, -2, 0)
+    f3, s3 = over_rows(f3, 1), over_rows(s2, 1)
+    keep, send = call(
+        functools.partial(anchor_kernel, 0), (c0, *pieces[1:]), rows_f32, micros=1.3, name="anchor_grad_own"
+    )
+    s1, s3, f3 = lax.optimization_barrier((s1, s3, f3))
     base, anchor_loss = call(
         listed_kernel,
         (anchors, s0, s1, s2, s3, *tile, keep, over_rows(send, 1), own_grad),
         [shape(n, wide), shape(1, n)],
-        micros=2.0, name="listed",
-    )
-    (g0,) = call(gathered_kernel, (base, from_y, grad1, grad2), [low_grad], micros=0.7, name="row_grad")
+        micros=2.0,
+        name="listed",
+    )
+    (g0,) = call(
+        gathered_kernel, (base, from_y, grad1, grad2), [low_grad], micros=0.7, name="row_grad"
+    )
     g2 = over_rows(g0, 2)
     g1 = over_rows(g0, 1)
     g3 = over_rows(g2, 1)

time: 124 us -> 126 us (1.016)
  starting transfers between devices: 24.8 us -> 21 us
  waiting for transfers between devices: 39.3 us -> 42.8 us
  local copies, waits for them, and re-layouts: 0.67 us -> 2.59 us
    ppermute x4, waiting for transfers between devices: 2.9 us -> 23.4 us  [along(): return lax.ppermute(x, ('blk', 'rows'), pairs)]
    ppermute x16, waiting for transfers between devices: 36.4 us -> 19.4 us  [over_rows(): return lax.ppermute(x, 'rows', [(i, i ^ flip) for i in range(rows_n)])]
    ppermute x4, starting transfers between devices: 14.8 us -> 12.3 us  [along(): return lax.ppermute(x, ('blk', 'rows'), pairs)]
    ppermute x16, starting transfers between devices: 10 us -> 8.73 us  [over_rows(): return lax.ppermute(x, 'rows', [(i, i ^ flip) for i in range(rows_n)])]
    pallas_call x8 -> x7, Pallas kernels: 20.5 us -> 20.9 us  [call(): pl.pallas_call(kernel, out_shape=outs, in_specs=[SMEM if x.ndim == 1 else...]
  transfers between devices with their start and end apart: 20 -> 20, of which waited for: 12 -> 8; matrix products, arithmetic and copies ran while one was open for 1% -> 2% of each run, Pallas kernels for 7% -> 15%
where the time goes in v3:
time: 126 us
  waiting for transfers between devices  42.8 us (34%)
  blocking collectives  32.7 us (26%)
  Pallas kernels  24.9 us (20%)
  starting transfers between devices  21 us (17%)
  local copies, waits for them, and re-layouts  2.59 us (2%)
    all_to_all x1, blocking collectives, local(): parts = lax.all_to_all(part, 'blk', split_axis=0, concat_axis=0, tiled=True)  32.7 us
    ppermute x4, waiting for transfers between devices, along(): return lax.ppermute(x, ('blk', 'rows'), pairs)  23.4 us
    pallas_call x7, Pallas kernels, call(): pl.pallas_call(kernel, out_shape=outs, in_specs=[SMEM if x.ndim == 1 else...  20.9 us
    ppermute x16, waiting for transfers between devices, over_rows(): return lax.ppermute(x, 'rows', [(i, i ^ flip) for i in range(rows_n)])  19.4 us
    ppermute x4, starting transfers between devices, along(): return lax.ppermute(x, ('blk', 'rows'), pairs)  12.3 us
    ppermute x16, starting transfers between devices, over_rows(): return lax.ppermute(x, 'rows', [(i, i ^ flip) for i in range(rows_n)])  8.73 us
    pallas_call x1, Pallas kernels, embed(): pl.pallas_call(embed_kernel, grid=(wide // step,), out_shape=shape(n + ME...  4.01 us
  transfers between devices with their start and end apart: 20, of which 8 were waited for; matrix products, arithmetic and copies ran while one was open for 2% of the time, Pallas kernels for 15%

profile of v3, /device:TPU:8, one launch (start us, length us, event | category | flops | bytes accessed | tf_op | source)
XLA Modules:
  0.0 125.6 jit_solution(10695762816597540324)
XLA Ops:
  0.6 4.0 %embed.1.p0.n0 = bf16[272,768]{1,0:T(8,128)(2,1)} custom-call(bf16[256,2048]{1,0:T(8,128)(2,1)} %features_ref.1, bf16[2048,768]{1,0:T(8,128)(2,1)} %weight_ref.1, s32[1,256]{1,0:T(1,128)} %bitcast.21, s32[3,256]{1,0:T(4,128)} %bitcast.20, f32[1,256]{1,0:T(1,128)} %bitcast.22), custom_call_target="tpu_custom_call" | custom-call | flops 1073741824 | bytes 4194304 | tf_op jit(solution)/shard_map/embed/pallas_call | solution.py:75
  4.7 2.2 %collective-permute-start.1 = (bf16[272,768]{1,0:T(8,128)(2,1)}, bf16[272,768]{1,0:T(8,128)(2,1)S(1)}, u32[]{:S(2)}, u32[]{:S(2)}) collective-permute-start(bf16[272,768]{1,0:T(8,128)(2,1)} %embed.1.p0.n0), channel_id=1, source_target_pairs={{0,2},{1,3},{2,0},{3,1},{4,6},{5,7},{6,4},{7,5},{8,10},{9,11},{10,... | collective-permute-start | bytes 1253384 | tf_op jit(solution)/shard_map/ppermute | solution.py:276
  6.8 0.7 collective-permute-start.3
  7.5 1.9 %collective-permute-start.4 = (bf16[272,768]{1,0:T(8,128)(2,1)}, bf16[272,768]{1,0:T(8,128)(2,1)S(1)}, u32[]{:S(2)}, u32[]{:S(2)}) collective-permute-start(bf16[272,768]{1,0:T(8,128)(2,1)} %embed.1.p0.n0), channel_id=1, source_target_pairs={{0,8},{1,9},{2,10},{3,11},{4,12},{5,13},{6,14},{7,15},{8,16},{9,17... | collective-permute-start | bytes 1253384 | tf_op jit(solution)/shard_map/ppermute | solution.py:284
  9.4 1.3 %copy.12 = bf16[256,2048]{0,1:T(8,128)(2,1)} copy(bf16[256,2048]{1,0:T(8,128)(2,1)S(1)} %copy-done.1) | data formatting | bytes 2097152 | tf_op jit(solution)/shard_map/optimization_barrier | solution.py:291
  10.7 1.3 %dynamic-slice_bitcast_fusion = (bf16[512,256]{1,0:T(8,128)(2,1)S(1)}, bf16[512,256]{1,0:T(8,128)(2,1)S(1)}, bf16[512,256]{1,0:T(8,128)(2,1)S(1)}, bf16[512,256]{1,0:T(8,128)(2,1)S(1)}) fusion(bf16[64,4,8,256]{3,2,1,0:T(8,128)(2,1)} %bitcast.19, s32[]{:T(128)S(6)} %select_n.16, s32[]{:T(128)S(6)} %select_n.15, s32[]{:T(128)S(6)} %select_n.14, s32[]{:T(128)S(6)} %select_n.13), kind=kLoop, calls=%fused_computation.1 | loop fusion | bytes 2097168 | tf_op jit(solution)/shard_map/reshape | solution.py:295
  12.0 4.2 %collective-permute-done.1.p2 = bf16[272,768]{1,0:T(8,128)(2,1)S(1)} collective-permute-done((bf16[272,768]{1,0:T(8,128)(2,1)}, bf16[272,768]{1,0:T(8,128)(2,1)S(1)}, u32[]{:S(2)}, u32[]{:S(2)}) %collective-permute-start.1) | collective-permute-done | bytes 417824 | tf_op jit(solution)/shard_map/ppermute | solution.py:276
  16.3 0.3 collective-permute-start.6
  16.7 9.1 %collective-permute-done.3.n1 = bf16[272,768]{1,0:T(8,128)(2,1)S(1)} collective-permute-done((bf16[272,768]{1,0:T(8,128)(2,1)}, bf16[272,768]{1,0:T(8,128)(2,1)S(1)}, u32[]{:S(2)}, u32[]{:S(2)}) %collective-permute-start.3) | collective-permute-done | bytes 417824 | tf_op jit(solution)/shard_map/ppermute | solution.py:284
  25.7 1.3 %collective-permute-start.7 = (bf16[512,256]{1,0:T(8,128)(2,1)S(1)}, bf16[512,256]{1,0:T(8,128)(2,1)S(1)}, u32[]{:S(2)}, u32[]{:S(2)}) collective-permute-start(bf16[512,256]{1,0:T(8,128)(2,1)S(1)} %get-tuple-element.40), channel_id=1, source_target_pairs={{0,2},{1,3},{2,0},{3,1},{4,6},{5,7},{6,4},{7,5},{8,10},{9,11},{10,... | collective-permute-start | bytes 786440 | tf_op jit(solution)/shard_map/ppermute | solution.py:276
  27.1 16.0 %score.1 = (f32[8,1024]{1,0:T(8,128)S(1)}, bf16[256,1024]{1,0:T(8,128)(2,1)S(1)}, bf16[256,1024]{1,0:T(8,128)(2,1)S(1)}, bf16[256,1024]{1,0:T(8,128)(2,1)S(1)}, ...) custom-call(s32[4]{0:T(128)S(1)} %pad_add_fusion.scal_ref, ...), custom_call_target="tpu_custom_call" | custom-call | flops 16099999744 | bytes 1024 | tf_op jit(solution)/shard_map/score/pallas_call | solution.py:25
  43.1 0.8 anchor_grad_across.1
  44.1 0.8 collective-permute-start.8
  44.8 3.2 %collective-permute-done.8.s2 = f32[8,1024]{1,0:T(8,128)S(1)} collective-permute-done((f32[8,1024]{1,0:T(8,128)S(1)}, f32[8,1024]{1,0:T(8,128)S(1)}, u32[]{:S(2)}, u32[]{:S(2)}) %collective-permute-start.8) | collective-permute-done | bytes 32800 | tf_op jit(solution)/shard_map/ppermute | solution.py:276
  48.1 0.8 anchor_grad_own.1
  49.0 0.5 collective-permute-start.12
  49.6 0.4 collective-permute-start.5
  50.0 1.6 %collective-permute-done.12.f1 = bf16[512,256]{1,0:T(8,128)(2,1)S(1)} collective-permute-done((bf16[512,256]{1,0:T(8,128)(2,1)S(1)}, bf16[512,256]{1,0:T(8,128)(2,1)S(1)}, u32[]{:S(2)}, u32[]{:S(2)}) %collective-permute-start.12) | collective-permute-done | bytes 262176 | tf_op jit(solution)/shard_map/ppermute | solution.py:276
  51.8 0.1 half_sum.1
  51.9 0.8 collective-permute-start.14
  52.7 8.7 %collective-permute-start.15 = (bf16[256,768]{1,0:T(8,128)(2,1)S(1)}, bf16[256,768]{1,0:T(8,128)(2,1)S(1)}, u32[]{:S(2)}, u32[]{:S(2)}) collective-permute-start(bf16[256,768]{1,0:T(8,128)(2,1)S(1)} %get-tuple-element.64), channel_id=1, source_target_pairs={{0,254},{1,255},{2,252},{3,253},{4,2},{5,3},{6,0},{7,1},{8,6},{9,7... | collective-permute-start | bytes 1179656 | tf_op jit(solution)/shard_map/ppermute | solution.py:284
  61.4 1.0 collective-permute-start.16
  62.4 2.0 %listed.1 = (f32[256,768]{1,0:T(8,128)S(1)}, f32[1,256]{1,0:T(1,128)}) custom-call(f32[8,1024]{1,0:T(8,128)S(1)} %get-tuple-element.36.anchors_ref, f32[8,1024]{1,0:T(8,128)S(1)} %get-tuple-element.37.s0, f32[8,1024]{1,0:T(8,128)S(1)} %collective-permute-done.5.s1, f32[8,1024]{1,0:T(8,128)S(1)} %collective-permute-done.8.s2, ...), custom_call_target="tpu_custom_call" | custom-call | flops 2300000000 | bytes 1024 | tf_op jit(solution)/shard_map/listed/pallas_call | solution.py:25
  64.4 6.5 %collective-permute-done.15.one_ref = bf16[256,768]{1,0:T(8,128)(2,1)S(1)} collective-permute-done((bf16[256,768]{1,0:T(8,128)(2,1)S(1)}, bf16[256,768]{1,0:T(8,128)(2,1)S(1)}, u32[]{:S(2)}, u32[]{:S(2)}) %collective-permute-start.15) | collective-permute-done | bytes 393248 | tf_op jit(solution)/shard_map/ppermute | solution.py:284
  70.9 7.8 %collective-permute-done.16.two_ref = bf16[256,768]{1,0:T(8,128)(2,1)S(1)} collective-permute-done((bf16[256,768]{1,0:T(8,128)(2,1)S(1)}, bf16[256,768]{1,0:T(8,128)(2,1)S(1)}, u32[]{:S(2)}, u32[]{:S(2)}) %collective-permute-start.16) | collective-permute-done | bytes 393248 | tf_op jit(solution)/shard_map/ppermute | solution.py:284
  78.7 0.2 row_grad.1.g0
  78.9 2.0 %collective-permute-start.18 = (bf16[256,768]{1,0:T(8,128)(2,1)S(1)}, bf16[256,768]{1,0:T(8,128)(2,1)S(1)}, u32[]{:S(2)}, u32[]{:S(2)}) collective-permute-start(bf16[256,768]{1,0:T(8,128)(2,1)S(1)} %row_grad.1.g0), channel_id=1, source_target_pairs={{0,2},{1,3},{2,0},{3,1},{4,6},{5,7},{6,4},{7,5},{8,10},{9,11},{10,... | collective-permute-start | bytes 1179656 | tf_op jit(solution)/shard_map/ppermute | solution.py:276
  80.9 8.5 %collective-permute-done.18.g2 = bf16[256,768]{1,0:T(8,128)(2,1)S(1)} collective-permute-done((bf16[256,768]{1,0:T(8,128)(2,1)S(1)}, bf16[256,768]{1,0:T(8,128)(2,1)S(1)}, u32[]{:S(2)}, u32[]{:S(2)}) %collective-permute-start.18) | collective-permute-done | bytes 393248 | tf_op jit(solution)/shard_map/ppermute | solution.py:276
  89.4 1.7 %collective-permute-done.19.g3 = bf16[256,768]{1,0:T(8,128)(2,1)S(1)} collective-permute-done((bf16[256,768]{1,0:T(8,128)(2,1)S(1)}, bf16[256,768]{1,0:T(8,128)(2,1)S(1)}, u32[]{:S(2)}, u32[]{:S(2)}) %collective-permute-start.19) | collective-permute-done | bytes 393248 | tf_op jit(solution)/shard_map/ppermute | solution.py:276
  91.1 1.0 head_grad.1
  92.1 32.7 %all_to_all.9 = bf16[64,8,768]{2,1,0:T(8,128)(2,1)S(1)} all-to-all(bf16[64,8,768]{2,1,0:T(8,128)(2,1)S(1)} %bitcast.18), channel_id=1, replica_groups=mesh['blk'=64,'rows'=4] {'blk'}, dimensions={0} | all-to-all | bytes 1572864 | tf_op jit(solution)/shard_map/all_to_all | solution.py:356
  124.8 0.7 convert_reduce_fusion
  (27 shorter events, 0.6 us)
Async XLA Ops:
  0.6 8.8 %copy-start.1 = (bf16[256,2048]{1,0:T(8,128)(2,1)S(1)}, bf16[256,2048]{1,0:T(8,128)(2,1)}, u32[]{:S(2)}) copy-start(bf16[256,2048]{1,0:T(8,128)(2,1)} %features_ref.1) | copy-start | bytes 3145732
  4.6 11.6 %copy-start.2 = (s32[1,3]{1,0:T(1,128)S(1)}, s32[1,3]{1,0:T(1,128)}, u32[]{:S(2)}) copy-start(s32[1,3]{1,0:T(1,128)} %param.10) | copy-start | bytes 40
  4.7 22.5 %copy-start = (bf16[272,768]{1,0:T(8,128)(2,1)S(1)}, bf16[272,768]{1,0:T(8,128)(2,1)}, u32[]{:S(2)}) copy-start(bf16[272,768]{1,0:T(8,128)(2,1)} %embed.1.p0.n0) | copy-start | bytes 1253380
  4.7 11.6 %collective-permute-start.1 = (bf16[272,768]{1,0:T(8,128)(2,1)}, bf16[272,768]{1,0:T(8,128)(2,1)S(1)}, u32[]{:S(2)}, u32[]{:S(2)}) collective-permute-start(bf16[272,768]{1,0:T(8,128)(2,1)} %embed.1.p0.n0), channel_id=1, source_target_pairs={{0,2},{1,3},{2,0},{3,1},{4,6},{5,7},{6,4},{7,5},{8,10},{9,11},{10,... | collective-permute-start | bytes 1253384 | tf_op jit(solution)/shard_map/ppermute | solution.py:276
  6.8 18.9 %collective-permute-start.3 = (bf16[272,768]{1,0:T(8,128)(2,1)}, bf16[272,768]{1,0:T(8,128)(2,1)S(1)}, u32[]{:S(2)}, u32[]{:S(2)}) collective-permute-start(bf16[272,768]{1,0:T(8,128)(2,1)} %embed.1.p0.n0), channel_id=1, source_target_pairs={{0,6},{1,7},{2,4},{3,5},{4,10},{5,11},{6,8},{7,9},{8,14},{9,15},{1... | collective-permute-start | bytes 1253384 | tf_op jit(solution)/shard_map/ppermute | solution.py:284
  7.5 19.6 %collective-permute-start.4 = (bf16[272,768]{1,0:T(8,128)(2,1)}, bf16[272,768]{1,0:T(8,128)(2,1)S(1)}, u32[]{:S(2)}, u32[]{:S(2)}) collective-permute-start(bf16[272,768]{1,0:T(8,128)(2,1)} %embed.1.p0.n0), channel_id=1, source_target_pairs={{0,8},{1,9},{2,10},{3,11},{4,12},{5,13},{6,14},{7,15},{8,16},{9,17... | collective-permute-start | bytes 1253384 | tf_op jit(solution)/shard_map/ppermute | solution.py:284
  9.4 17.7 %collective-permute-start = (bf16[272,768]{1,0:T(8,128)(2,1)}, bf16[272,768]{1,0:T(8,128)(2,1)S(1)}, u32[]{:S(2)}, u32[]{:S(2)}) collective-permute-start(bf16[272,768]{1,0:T(8,128)(2,1)} %embed.1.p0.n0), channel_id=1, source_target_pairs={{0,1},{1,0},{2,3},{3,2},{4,5},{5,4},{6,7},{7,6},{8,9},{9,8},{10,11... | collective-permute-start | bytes 1253384 | tf_op jit(solution)/shard_map/ppermute | solution.py:276
  16.2 10.9 %collective-permute-start.2 = (bf16[272,768]{1,0:T(8,128)(2,1)S(1)}, bf16[272,768]{1,0:T(8,128)(2,1)S(1)}, u32[]{:S(2)}, u32[]{:S(2)}) collective-permute-start(bf16[272,768]{1,0:T(8,128)(2,1)S(1)} %collective-permute-done.1.p2), channel_id=1, source_target_pairs={{0,1},{1,0},{2,3},{3,2},{4,5},{5,4},{6,7},{7,6},{8,9},{9,8},{10,11... | collective-permute-start | bytes 1253384 | tf_op jit(solution)/shard_map/ppermute | solution.py:276
  16.3 26.8 %collective-permute-start.6 = (bf16[512,256]{1,0:T(8,128)(2,1)S(1)}, bf16[512,256]{1,0:T(8,128)(2,1)S(1)}, u32[]{:S(2)}, u32[]{:S(2)}) collective-permute-start(bf16[512,256]{1,0:T(8,128)(2,1)S(1)} %get-tuple-element.39), channel_id=1, source_target_pairs={{0,2},{1,3},{2,0},{3,1},{4,6},{5,7},{6,4},{7,5},{8,10},{9,11},{10,... | collective-permute-start | bytes 786440 | tf_op jit(solution)/shard_map/ppermute | solution.py:276
  25.7 17.4 %collective-permute-start.7 = (bf16[512,256]{1,0:T(8,128)(2,1)S(1)}, bf16[512,256]{1,0:T(8,128)(2,1)S(1)}, u32[]{:S(2)}, u32[]{:S(2)}) collective-permute-start(bf16[512,256]{1,0:T(8,128)(2,1)S(1)} %get-tuple-element.40), channel_id=1, source_target_pairs={{0,2},{1,3},{2,0},{3,1},{4,6},{5,7},{6,4},{7,5},{8,10},{9,11},{10,... | collective-permute-start | bytes 786440 | tf_op jit(solution)/shard_map/ppermute | solution.py:276
  44.0 7.8 %collective-permute-start.13 = (f32[256,768]{1,0:T(8,128)S(1)}, f32[256,768]{1,0:T(8,128)S(1)}, u32[]{:S(2)}, u32[]{:S(2)}) collective-permute-start(f32[256,768]{1,0:T(8,128)S(1)} %get-tuple-element.60), channel_id=1, source_target_pairs={{0,1},{1,0},{2,3},{3,2},{4,5},{5,4},{6,7},{7,6},{8,9},{9,8},{10,11... | collective-permute-start | bytes 2359304 | tf_op jit(solution)/shard_map/ppermute | solution.py:276
  44.1 4.0 %collective-permute-start.8 = (f32[8,1024]{1,0:T(8,128)S(1)}, f32[8,1024]{1,0:T(8,128)S(1)}, u32[]{:S(2)}, u32[]{:S(2)}) collective-permute-start(f32[8,1024]{1,0:T(8,128)S(1)} %get-tuple-element.37.s0), channel_id=1, source_target_pairs={{0,2},{1,3},{2,0},{3,1},{4,6},{5,7},{6,4},{7,5},{8,10},{9,11},{10,... | collective-permute-start | bytes 98312 | tf_op jit(solution)/shard_map/ppermute | solution.py:276
  48.9 13.5 %collective-permute-start.11 = (f32[256,768]{1,0:T(8,128)S(1)}, f32[256,768]{1,0:T(8,128)S(1)}, u32[]{:S(2)}, u32[]{:S(2)}) collective-permute-start(f32[256,768]{1,0:T(8,128)S(1)} %get-tuple-element.50), channel_id=1, source_target_pairs={{0,1},{1,0},{2,3},{3,2},{4,5},{5,4},{6,7},{7,6},{8,9},{9,8},{10,11... | collective-permute-start | bytes 2359304 | tf_op jit(solution)/shard_map/ppermute | solution.py:276
  49.0 2.6 %collective-permute-start.12 = (bf16[512,256]{1,0:T(8,128)(2,1)S(1)}, bf16[512,256]{1,0:T(8,128)(2,1)S(1)}, u32[]{:S(2)}, u32[]{:S(2)}) collective-permute-start(bf16[512,256]{1,0:T(8,128)(2,1)S(1)} %get-tuple-element.54), channel_id=1, source_target_pairs={{0,1},{1,0},{2,3},{3,2},{4,5},{5,4},{6,7},{7,6},{8,9},{9,8},{10,11... | collective-permute-start | bytes 786440 | tf_op jit(solution)/shard_map/ppermute | solution.py:276
  49.5 12.9 %collective-permute-start.10 = (bf16[512,256]{1,0:T(8,128)(2,1)S(1)}, bf16[512,256]{1,0:T(8,128)(2,1)S(1)}, u32[]{:S(2)}, u32[]{:S(2)}) collective-permute-start(bf16[512,256]{1,0:T(8,128)(2,1)S(1)} %collective-permute-done.7), channel_id=1, source_target_pairs={{0,1},{1,0},{2,3},{3,2},{4,5},{5,4},{6,7},{7,6},{8,9},{9,8},{10,11... | collective-permute-start | bytes 786440 | tf_op jit(solution)/shard_map/ppermute | solution.py:276
  49.6 3.1 %collective-permute-start.5 = (f32[8,1024]{1,0:T(8,128)S(1)}, f32[8,1024]{1,0:T(8,128)S(1)}, u32[]{:S(2)}, u32[]{:S(2)}) collective-permute-start(f32[8,1024]{1,0:T(8,128)S(1)} %get-tuple-element.37.s0), channel_id=1, source_target_pairs={{0,1},{1,0},{2,3},{3,2},{4,5},{5,4},{6,7},{7,6},{8,9},{9,8},{10,11... | collective-permute-start | bytes 98312 | tf_op jit(solution)/shard_map/ppermute | solution.py:276
  51.6 9.8 %collective-permute-start.9 = (f32[8,1024]{1,0:T(8,128)S(1)}, f32[8,1024]{1,0:T(8,128)S(1)}, u32[]{:S(2)}, u32[]{:S(2)}) collective-permute-start(f32[8,1024]{1,0:T(8,128)S(1)} %collective-permute-done.8.s2), channel_id=1, source_target_pairs={{0,1},{1,0},{2,3},{3,2},{4,5},{5,4},{6,7},{7,6},{8,9},{9,8},{10,11... | collective-permute-start | bytes 98312 | tf_op jit(solution)/shard_map/ppermute | solution.py:276
  51.9 12.5 %collective-permute-start.14 = (bf16[256,768]{1,0:T(8,128)(2,1)S(1)}, bf16[256,768]{1,0:T(8,128)(2,1)S(1)}, u32[]{:S(2)}, u32[]{:S(2)}) collective-permute-start(bf16[256,768]{1,0:T(8,128)(2,1)S(1)} %half_sum.1), channel_id=1, source_target_pairs={{0,2},{1,3},{2,0},{3,1},{4,6},{5,7},{6,4},{7,5},{8,10},{9,11},{10,... | collective-permute-start | bytes 1179656 | tf_op jit(solution)/shard_map/ppermute | solution.py:276
  52.7 18.2 %collective-permute-start.15 = (bf16[256,768]{1,0:T(8,128)(2,1)S(1)}, bf16[256,768]{1,0:T(8,128)(2,1)S(1)}, u32[]{:S(2)}, u32[]{:S(2)}) collective-permute-start(bf16[256,768]{1,0:T(8,128)(2,1)S(1)} %get-tuple-element.64), channel_id=1, source_target_pairs={{0,254},{1,255},{2,252},{3,253},{4,2},{5,3},{6,0},{7,1},{8,6},{9,7... | collective-permute-start | bytes 1179656 | tf_op jit(solution)/shard_map/ppermute | solution.py:284
  61.4 17.3 %collective-permute-start.16 = (bf16[256,768]{1,0:T(8,128)(2,1)S(1)}, bf16[256,768]{1,0:T(8,128)(2,1)S(1)}, u32[]{:S(2)}, u32[]{:S(2)}) collective-permute-start(bf16[256,768]{1,0:T(8,128)(2,1)S(1)} %get-tuple-element.65), channel_id=1, source_target_pairs={{0,248},{1,249},{2,250},{3,251},{4,252},{5,253},{6,254},{7,255},{8... | collective-permute-start | bytes 1179656 | tf_op jit(solution)/shard_map/ppermute | solution.py:284
  78.9 10.5 %collective-permute-start.18 = (bf16[256,768]{1,0:T(8,128)(2,1)S(1)}, bf16[256,768]{1,0:T(8,128)(2,1)S(1)}, u32[]{:S(2)}, u32[]{:S(2)}) collective-permute-start(bf16[256,768]{1,0:T(8,128)(2,1)S(1)} %row_grad.1.g0), channel_id=1, source_target_pairs={{0,2},{1,3},{2,0},{3,1},{4,6},{5,7},{6,4},{7,5},{8,10},{9,11},{10,... | collective-permute-start | bytes 1179656 | tf_op jit(solution)/shard_map/ppermute | solution.py:276
  80.9 8.5 %collective-permute-start.17 = (bf16[256,768]{1,0:T(8,128)(2,1)S(1)}, bf16[256,768]{1,0:T(8,128)(2,1)S(1)}, u32[]{:S(2)}, u32[]{:S(2)}) collective-permute-start(bf16[256,768]{1,0:T(8,128)(2,1)S(1)} %row_grad.1.g0), channel_id=1, source_target_pairs={{0,1},{1,0},{2,3},{3,2},{4,5},{5,4},{6,7},{7,6},{8,9},{9,8},{10,11... | collective-permute-start | bytes 1179656 | tf_op jit(solution)/shard_map/ppermute | solution.py:276
  89.4 1.7 %collective-permute-start.19 = (bf16[256,768]{1,0:T(8,128)(2,1)S(1)}, bf16[256,768]{1,0:T(8,128)(2,1)S(1)}, u32[]{:S(2)}, u32[]{:S(2)}) collective-permute-start(bf16[256,768]{1,0:T(8,128)(2,1)S(1)} %collective-permute-done.18.g2), channel_id=1, source_target_pairs={{0,1},{1,0},{2,3},{3,2},{4,5},{5,4},{6,7},{7,6},{8,9},{9,8},{10,11... | collective-permute-start | bytes 1179656 | tf_op jit(solution)/shard_map/ppermute | solution.py:276

commit v4 on v3

--- a/solution.py
+++ b/solution.py
@@ -21,7 +21,7 @@
 SMEM = pl.BlockSpec(memory_space=pltpu.SMEM)
 
 
-def call(kernel, inputs, outs, scratch=(), micros=0.0, name=None):
+def call(kernel, inputs, outs, scratch=(), micros=0.01, name=None):
     return pl.pallas_call(
         kernel,
         out_shape=outs,
@@ -310,7 +310,7 @@
         (scal, *tile, n1, n2),
         [shape(8, 4 * n)] + [low_coef] * 3 + [shape(8, 4 * n), shape(n, wide)] + [low_grad] * 2,
         scratch,
-        micros=14.0,
+        micros=0.01,
         name="score",
     )
     c0, f2, f3 = lax.optimization_barrier((c0, f2, f3))
@@ -319,30 +319,28 @@
     pieces = (c0, c1, c2, p0, n1, n2)
     rows_f32 = [shape(n, wide), shape(n, wide)]
     keep, send = call(
-        functools.partial(anchor_kernel, 2), pieces, rows_f32, micros=1.3, name="anchor_grad_across"
-    )
-    keep, f1 = lax.optimization_barrier((keep, f1))
-    c0, s2 = lax.optimization_barrier((c0, s2))
+        functools.partial(anchor_kernel, 2), pieces, rows_f32, micros=0.01, name="anchor_grad_across"
+    )
+    keep, f1, s2 = lax.optimization_barrier((keep, f1, s2))
     (half,) = call(
-        halved_kernel, (keep, over_rows(send, 1)), [low_grad], micros=0.5, name="half_sum"
-    )
-    half, grad1, grad2 = lax.optimization_barrier((half, grad1, grad2))
+        halved_kernel, (keep, over_rows(send, 1)), [low_grad], micros=0.01, name="half_sum"
+    )
     from_y = over_rows(half, 2)
     grad1, grad2 = along(grad1, -1, 2), along(grad2, -2, 0)
     f3, s3 = over_rows(f3, 1), over_rows(s2, 1)
     keep, send = call(
-        functools.partial(anchor_kernel, 0), (c0, *pieces[1:]), rows_f32, micros=1.3, name="anchor_grad_own"
+        functools.partial(anchor_kernel, 0), pieces, rows_f32, micros=0.01, name="anchor_grad_own"
     )
     s1, s3, f3 = lax.optimization_barrier((s1, s3, f3))
     base, anchor_loss = call(
         listed_kernel,
         (anchors, s0, s1, s2, s3, *tile, keep, over_rows(send, 1), own_grad),
         [shape(n, wide), shape(1, n)],
-        micros=2.0,
+        micros=0.01,
         name="listed",
     )
     (g0,) = call(
-        gathered_kernel, (base, from_y, grad1, grad2), [low_grad], micros=0.7, name="row_grad"
+        gathered_kernel, (base, from_y, grad1, grad2), [low_grad], micros=0.01, name="row_grad"
     )
     g2 = over_rows(g0, 2)
     g1 = over_rows(g0, 1)
@@ -351,7 +349,7 @@
         head_kernel,
         (f0, f1, f2, f3, g0, g1, g2, g3),
         [shape(m, wide, dtype=bf16)],
-        micros=1.5, name="head_grad",
+        micros=0.01, name="head_grad",
     )
     parts = lax.all_to_all(part, "blk", split_axis=0, concat_axis=0, tiled=True)
     weight_grad = jnp.sum(parts.reshape(blks, slice_rows, wide).astype(f32), axis=0)

time: 126 us -> 119 us (0.944)
  waiting for transfers between devices: 42.8 us -> 36.8 us
    ppermute x4, waiting for transfers between devices: 23.4 us -> 18.6 us  [along(): return lax.ppermute(x, ('blk', 'rows'), pairs)]
  transfers between devices with their start and end apart: 20 -> 20, of which waited for: 8 -> 9; matrix products, arithmetic and copies ran while one was open for 2% -> 2% of each run, Pallas kernels for 15% -> 16%
where the time goes in v4:
time: 119 us
  waiting for transfers between devices  36.8 us (31%)
  blocking collectives  32.7 us (27%)
  Pallas kernels  25 us (21%)
  starting transfers between devices  20.6 us (17%)
  local copies, waits for them, and re-layouts  2.59 us (2%)
    all_to_all x1, blocking collectives, local(): parts = lax.all_to_all(part, 'blk', split_axis=0, concat_axis=0, tiled=True)  32.7 us
    pallas_call x7, Pallas kernels, call(): pl.pallas_call(kernel, out_shape=outs, in_specs=[SMEM if x.ndim == 1 else...  21 us
    ppermute x4, waiting for transfers between devices, along(): return lax.ppermute(x, ('blk', 'rows'), pairs)  18.6 us
    ppermute x16, waiting for transfers between devices, over_rows(): return lax.ppermute(x, 'rows', [(i, i ^ flip) for i in range(rows_n)])  18.2 us
    ppermute x4, starting transfers between devices, along(): return lax.ppermute(x, ('blk', 'rows'), pairs)  12.2 us
    ppermute x16, starting transfers between devices, over_rows(): return lax.ppermute(x, 'rows', [(i, i ^ flip) for i in range(rows_n)])  8.39 us
    pallas_call x1, Pallas kernels, embed(): pl.pallas_call(embed_kernel, grid=(wide // step,), out_shape=shape(n + ME...  4.01 us
  transfers between devices with their start and end apart: 20, of which 9 were waited for; matrix products, arithmetic and copies ran while one was open for 2% of the time, Pallas kernels for 16%

profile of v4, /device:TPU:8, one launch (start us, length us, event | category | flops | bytes accessed | tf_op | source)
XLA Modules:
  0.0 119.3 jit_solution(14693352833142810084)
XLA Ops:
  0.6 4.0 %embed.1.p0.n0 = bf16[272,768]{1,0:T(8,128)(2,1)} custom-call(bf16[256,2048]{1,0:T(8,128)(2,1)} %features_ref.1, bf16[2048,768]{1,0:T(8,128)(2,1)} %weight_ref.1, s32[1,256]{1,0:T(1,128)} %bitcast.21, s32[3,256]{1,0:T(4,128)} %bitcast.20, f32[1,256]{1,0:T(1,128)} %bitcast.22), custom_call_target="tpu_custom_call" | custom-call | flops 1073741824 | bytes 4194304 | tf_op jit(solution)/shard_map/embed/pallas_call | solution.py:75
  4.7 2.2 %collective-permute-start.1 = (bf16[272,768]{1,0:T(8,128)(2,1)}, bf16[272,768]{1,0:T(8,128)(2,1)S(1)}, u32[]{:S(2)}, u32[]{:S(2)}) collective-permute-start(bf16[272,768]{1,0:T(8,128)(2,1)} %embed.1.p0.n0), channel_id=1, source_target_pairs={{0,2},{1,3},{2,0},{3,1},{4,6},{5,7},{6,4},{7,5},{8,10},{9,11},{10,... | collective-permute-start | bytes 1253384 | tf_op jit(solution)/shard_map/ppermute | solution.py:276
  6.8 0.7 collective-permute-start.3
  7.5 1.9 %collective-permute-start.4 = (bf16[272,768]{1,0:T(8,128)(2,1)}, bf16[272,768]{1,0:T(8,128)(2,1)S(1)}, u32[]{:S(2)}, u32[]{:S(2)}) collective-permute-start(bf16[272,768]{1,0:T(8,128)(2,1)} %embed.1.p0.n0), channel_id=1, source_target_pairs={{0,8},{1,9},{2,10},{3,11},{4,12},{5,13},{6,14},{7,15},{8,16},{9,17... | collective-permute-start | bytes 1253384 | tf_op jit(solution)/shard_map/ppermute | solution.py:284
  9.4 1.3 %copy.12 = bf16[256,2048]{0,1:T(8,128)(2,1)} copy(bf16[256,2048]{1,0:T(8,128)(2,1)S(1)} %copy-done.1) | data formatting | bytes 2097152 | tf_op jit(solution)/shard_map/optimization_barrier | solution.py:291
  10.7 1.3 %dynamic-slice_bitcast_fusion = (bf16[512,256]{1,0:T(8,128)(2,1)S(1)}, bf16[512,256]{1,0:T(8,128)(2,1)S(1)}, bf16[512,256]{1,0:T(8,128)(2,1)S(1)}, bf16[512,256]{1,0:T(8,128)(2,1)S(1)}) fusion(bf16[64,4,8,256]{3,2,1,0:T(8,128)(2,1)} %bitcast.19, s32[]{:T(128)S(6)} %select_n.16, s32[]{:T(128)S(6)} %select_n.15, s32[]{:T(128)S(6)} %select_n.14, s32[]{:T(128)S(6)} %select_n.13), kind=kLoop, calls=%fused_computation.1 | loop fusion | bytes 2097168 | tf_op jit(solution)/shard_map/reshape | solution.py:295
  12.0 4.2 %collective-permute-done.1.p2 = bf16[272,768]{1,0:T(8,128)(2,1)S(1)} collective-permute-done((bf16[272,768]{1,0:T(8,128)(2,1)}, bf16[272,768]{1,0:T(8,128)(2,1)S(1)}, u32[]{:S(2)}, u32[]{:S(2)}) %collective-permute-start.1) | collective-permute-done | bytes 417824 | tf_op jit(solution)/shard_map/ppermute | solution.py:276
  16.2 0.3 collective-permute-start.6
  16.6 9.2 %collective-permute-done.3.n1 = bf16[272,768]{1,0:T(8,128)(2,1)S(1)} collective-permute-done((bf16[272,768]{1,0:T(8,128)(2,1)}, bf16[272,768]{1,0:T(8,128)(2,1)S(1)}, u32[]{:S(2)}, u32[]{:S(2)}) %collective-permute-start.3) | collective-permute-done | bytes 417824 | tf_op jit(solution)/shard_map/ppermute | solution.py:284
  25.7 1.3 %collective-permute-start.7 = (bf16[512,256]{1,0:T(8,128)(2,1)S(1)}, bf16[512,256]{1,0:T(8,128)(2,1)S(1)}, u32[]{:S(2)}, u32[]{:S(2)}) collective-permute-start(bf16[512,256]{1,0:T(8,128)(2,1)S(1)} %get-tuple-element.36), channel_id=1, source_target_pairs={{0,2},{1,3},{2,0},{3,1},{4,6},{5,7},{6,4},{7,5},{8,10},{9,11},{10,... | collective-permute-start | bytes 786440 | tf_op jit(solution)/shard_map/ppermute | solution.py:276
  27.2 16.0 %score.1 = (f32[8,1024]{1,0:T(8,128)S(1)}, bf16[256,1024]{1,0:T(8,128)(2,1)S(1)}, bf16[256,1024]{1,0:T(8,128)(2,1)S(1)}, bf16[256,1024]{1,0:T(8,128)(2,1)S(1)}, ...) custom-call(s32[4]{0:T(128)S(1)} %pad_add_fusion.scal_ref, ...), custom_call_target="tpu_custom_call" | custom-call | flops 11500000 | bytes 1024 | tf_op jit(solution)/shard_map/score/pallas_call | solution.py:25
  43.2 0.8 anchor_grad_across.1
  44.1 0.8 anchor_grad_own.1
  45.0 0.6 collective-permute-start.12
  45.6 0.7 collective-permute-start.9
  46.3 8.6 %collective-permute-start.15 = (bf16[256,768]{1,0:T(8,128)(2,1)S(1)}, bf16[256,768]{1,0:T(8,128)(2,1)S(1)}, u32[]{:S(2)}, u32[]{:S(2)}) collective-permute-start(bf16[256,768]{1,0:T(8,128)(2,1)S(1)} %get-tuple-element.56), channel_id=1, source_target_pairs={{0,254},{1,255},{2,252},{3,253},{4,2},{5,3},{6,0},{7,1},{8,6},{9,7... | collective-permute-start | bytes 1179656 | tf_op jit(solution)/shard_map/ppermute | solution.py:284
  55.0 1.0 collective-permute-start.16
  56.1 0.8 collective-permute-start.14
  56.9 1.2 %collective-permute-done.5.s1 = f32[8,1024]{1,0:T(8,128)S(1)} collective-permute-done((f32[8,1024]{1,0:T(8,128)S(1)}, f32[8,1024]{1,0:T(8,128)S(1)}, u32[]{:S(2)}, u32[]{:S(2)}) %collective-permute-start.5) | collective-permute-done | bytes 32800 | tf_op jit(solution)/shard_map/ppermute | solution.py:276
  58.1 0.2 collective-permute-start.10
  58.3 1.0 collective-permute-done.10.s3
  59.5 1.4 %collective-permute-done.11.f3 = bf16[512,256]{1,0:T(8,128)(2,1)S(1)} collective-permute-done((bf16[512,256]{1,0:T(8,128)(2,1)S(1)}, bf16[512,256]{1,0:T(8,128)(2,1)S(1)}, u32[]{:S(2)}, u32[]{:S(2)}) %collective-permute-start.11) | collective-permute-done | bytes 262176 | tf_op jit(solution)/shard_map/ppermute | solution.py:276
  60.9 2.1 %listed.1 = (f32[256,768]{1,0:T(8,128)S(1)}, f32[1,256]{1,0:T(1,128)}) custom-call(f32[8,1024]{1,0:T(8,128)S(1)} %get-tuple-element.32.anchors_ref, f32[8,1024]{1,0:T(8,128)S(1)} %get-tuple-element.33.s0, f32[8,1024]{1,0:T(8,128)S(1)} %collective-permute-done.5.s1, f32[8,1024]{1,0:T(8,128)S(1)} %collective-permute-done.9.s2, ...), custom_call_target="tpu_custom_call" | custom-call | flops 11500000 | bytes 1024 | tf_op jit(solution)/shard_map/listed/pallas_call | solution.py:25
  62.9 1.5 %collective-permute-done.15.one_ref = bf16[256,768]{1,0:T(8,128)(2,1)S(1)} collective-permute-done((bf16[256,768]{1,0:T(8,128)(2,1)S(1)}, bf16[256,768]{1,0:T(8,128)(2,1)S(1)}, u32[]{:S(2)}, u32[]{:S(2)}) %collective-permute-start.15) | collective-permute-done | bytes 393248 | tf_op jit(solution)/shard_map/ppermute | solution.py:284
  64.4 7.9 %collective-permute-done.16.two_ref = bf16[256,768]{1,0:T(8,128)(2,1)S(1)} collective-permute-done((bf16[256,768]{1,0:T(8,128)(2,1)S(1)}, bf16[256,768]{1,0:T(8,128)(2,1)S(1)}, u32[]{:S(2)}, u32[]{:S(2)}) %collective-permute-start.16) | collective-permute-done | bytes 393248 | tf_op jit(solution)/shard_map/ppermute | solution.py:284
  72.4 0.2 row_grad.1.g0
  72.5 2.0 %collective-permute-start.18 = (bf16[256,768]{1,0:T(8,128)(2,1)S(1)}, bf16[256,768]{1,0:T(8,128)(2,1)S(1)}, u32[]{:S(2)}, u32[]{:S(2)}) collective-permute-start(bf16[256,768]{1,0:T(8,128)(2,1)S(1)} %row_grad.1.g0), channel_id=1, source_target_pairs={{0,2},{1,3},{2,0},{3,1},{4,6},{5,7},{6,4},{7,5},{8,10},{9,11},{10,... | collective-permute-start | bytes 1179656 | tf_op jit(solution)/shard_map/ppermute | solution.py:276
  74.5 8.6 %collective-permute-done.18.g2 = bf16[256,768]{1,0:T(8,128)(2,1)S(1)} collective-permute-done((bf16[256,768]{1,0:T(8,128)(2,1)S(1)}, bf16[256,768]{1,0:T(8,128)(2,1)S(1)}, u32[]{:S(2)}, u32[]{:S(2)}) %collective-permute-start.18) | collective-permute-done | bytes 393248 | tf_op jit(solution)/shard_map/ppermute | solution.py:276
  83.1 1.7 %collective-permute-done.19.g3 = bf16[256,768]{1,0:T(8,128)(2,1)S(1)} collective-permute-done((bf16[256,768]{1,0:T(8,128)(2,1)S(1)}, bf16[256,768]{1,0:T(8,128)(2,1)S(1)}, u32[]{:S(2)}, u32[]{:S(2)}) %collective-permute-start.19) | collective-permute-done | bytes 393248 | tf_op jit(solution)/shard_map/ppermute | solution.py:276
  84.8 1.0 head_grad.1
  85.8 32.7 %all_to_all.9 = bf16[64,8,768]{2,1,0:T(8,128)(2,1)S(1)} all-to-all(bf16[64,8,768]{2,1,0:T(8,128)(2,1)S(1)} %bitcast.18), channel_id=1, replica_groups=mesh['blk'=64,'rows'=4] {'blk'}, dimensions={0} | all-to-all | bytes 1572864 | tf_op jit(solution)/shard_map/all_to_all | solution.py:354
  118.5 0.7 convert_reduce_fusion
  (27 shorter events, 0.6 us)
Async XLA Ops:
  0.6 8.8 %copy-start.1 = (bf16[256,2048]{1,0:T(8,128)(2,1)S(1)}, bf16[256,2048]{1,0:T(8,128)(2,1)}, u32[]{:S(2)}) copy-start(bf16[256,2048]{1,0:T(8,128)(2,1)} %features_ref.1) | copy-start | bytes 3145732
  4.6 22.5 %copy-start.2 = (s32[1,3]{1,0:T(1,128)S(1)}, s32[1,3]{1,0:T(1,128)}, u32[]{:S(2)}) copy-start(s32[1,3]{1,0:T(1,128)} %param.10) | copy-start | bytes 40
  4.7 22.5 %copy-start = (bf16[272,768]{1,0:T(8,128)(2,1)S(1)}, bf16[272,768]{1,0:T(8,128)(2,1)}, u32[]{:S(2)}) copy-start(bf16[272,768]{1,0:T(8,128)(2,1)} %embed.1.p0.n0) | copy-start | bytes 1253380
  4.7 11.6 %collective-permute-start.1 = (bf16[272,768]{1,0:T(8,128)(2,1)}, bf16[272,768]{1,0:T(8,128)(2,1)S(1)}, u32[]{:S(2)}, u32[]{:S(2)}) collective-permute-start(bf16[272,768]{1,0:T(8,128)(2,1)} %embed.1.p0.n0), channel_id=1, source_target_pairs={{0,2},{1,3},{2,0},{3,1},{4,6},{5,7},{6,4},{7,5},{8,10},{9,11},{10,... | collective-permute-start | bytes 1253384 | tf_op jit(solution)/shard_map/ppermute | solution.py:276
  6.8 18.9 %collective-permute-start.3 = (bf16[272,768]{1,0:T(8,128)(2,1)}, bf16[272,768]{1,0:T(8,128)(2,1)S(1)}, u32[]{:S(2)}, u32[]{:S(2)}) collective-permute-start(bf16[272,768]{1,0:T(8,128)(2,1)} %embed.1.p0.n0), channel_id=1, source_target_pairs={{0,6},{1,7},{2,4},{3,5},{4,10},{5,11},{6,8},{7,9},{8,14},{9,15},{1... | collective-permute-start | bytes 1253384 | tf_op jit(solution)/shard_map/ppermute | solution.py:284
  7.5 19.7 %collective-permute-start.4 = (bf16[272,768]{1,0:T(8,128)(2,1)}, bf16[272,768]{1,0:T(8,128)(2,1)S(1)}, u32[]{:S(2)}, u32[]{:S(2)}) collective-permute-start(bf16[272,768]{1,0:T(8,128)(2,1)} %embed.1.p0.n0), channel_id=1, source_target_pairs={{0,8},{1,9},{2,10},{3,11},{4,12},{5,13},{6,14},{7,15},{8,16},{9,17... | collective-permute-start | bytes 1253384 | tf_op jit(solution)/shard_map/ppermute | solution.py:284
  9.4 17.8 %collective-permute-start = (bf16[272,768]{1,0:T(8,128)(2,1)}, bf16[272,768]{1,0:T(8,128)(2,1)S(1)}, u32[]{:S(2)}, u32[]{:S(2)}) collective-permute-start(bf16[272,768]{1,0:T(8,128)(2,1)} %embed.1.p0.n0), channel_id=1, source_target_pairs={{0,1},{1,0},{2,3},{3,2},{4,5},{5,4},{6,7},{7,6},{8,9},{9,8},{10,11... | collective-permute-start | bytes 1253384 | tf_op jit(solution)/shard_map/ppermute | solution.py:276
  16.2 10.9 %collective-permute-start.2 = (bf16[272,768]{1,0:T(8,128)(2,1)S(1)}, bf16[272,768]{1,0:T(8,128)(2,1)S(1)}, u32[]{:S(2)}, u32[]{:S(2)}) collective-permute-start(bf16[272,768]{1,0:T(8,128)(2,1)S(1)} %collective-permute-done.1.p2), channel_id=1, source_target_pairs={{0,1},{1,0},{2,3},{3,2},{4,5},{5,4},{6,7},{7,6},{8,9},{9,8},{10,11... | collective-permute-start | bytes 1253384 | tf_op jit(solution)/shard_map/ppermute | solution.py:276
  16.2 26.9 %collective-permute-start.6 = (bf16[512,256]{1,0:T(8,128)(2,1)S(1)}, bf16[512,256]{1,0:T(8,128)(2,1)S(1)}, u32[]{:S(2)}, u32[]{:S(2)}) collective-permute-start(bf16[512,256]{1,0:T(8,128)(2,1)S(1)} %get-tuple-element.35), channel_id=1, source_target_pairs={{0,2},{1,3},{2,0},{3,1},{4,6},{5,7},{6,4},{7,5},{8,10},{9,11},{10,... | collective-permute-start | bytes 786440 | tf_op jit(solution)/shard_map/ppermute | solution.py:276
  25.7 17.5 %collective-permute-start.7 = (bf16[512,256]{1,0:T(8,128)(2,1)S(1)}, bf16[512,256]{1,0:T(8,128)(2,1)S(1)}, u32[]{:S(2)}, u32[]{:S(2)}) collective-permute-start(bf16[512,256]{1,0:T(8,128)(2,1)S(1)} %get-tuple-element.36), channel_id=1, source_target_pairs={{0,2},{1,3},{2,0},{3,1},{4,6},{5,7},{6,4},{7,5},{8,10},{9,11},{10,... | collective-permute-start | bytes 786440 | tf_op jit(solution)/shard_map/ppermute | solution.py:276
  44.0 11.9 %collective-permute-start.13 = (f32[256,768]{1,0:T(8,128)S(1)}, f32[256,768]{1,0:T(8,128)S(1)}, u32[]{:S(2)}, u32[]{:S(2)}) collective-permute-start(f32[256,768]{1,0:T(8,128)S(1)} %get-tuple-element.55), channel_id=1, source_target_pairs={{0,1},{1,0},{2,3},{3,2},{4,5},{5,4},{6,7},{7,6},{8,9},{9,8},{10,11... | collective-permute-start | bytes 2359304 | tf_op jit(solution)/shard_map/ppermute | solution.py:276
  45.0 15.9 %collective-permute-start.12 = (f32[256,768]{1,0:T(8,128)S(1)}, f32[256,768]{1,0:T(8,128)S(1)}, u32[]{:S(2)}, u32[]{:S(2)}) collective-permute-start(f32[256,768]{1,0:T(8,128)S(1)} %get-tuple-element.47), channel_id=1, source_target_pairs={{0,1},{1,0},{2,3},{3,2},{4,5},{5,4},{6,7},{7,6},{8,9},{9,8},{10,11... | collective-permute-start | bytes 2359304 | tf_op jit(solution)/shard_map/ppermute | solution.py:276
  45.5 9.4 %collective-permute-start.8 = (bf16[512,256]{1,0:T(8,128)(2,1)S(1)}, bf16[512,256]{1,0:T(8,128)(2,1)S(1)}, u32[]{:S(2)}, u32[]{:S(2)}) collective-permute-start(bf16[512,256]{1,0:T(8,128)(2,1)S(1)} %get-tuple-element.41), channel_id=1, source_target_pairs={{0,1},{1,0},{2,3},{3,2},{4,5},{5,4},{6,7},{7,6},{8,9},{9,8},{10,11... | collective-permute-start | bytes 786440 | tf_op jit(solution)/shard_map/ppermute | solution.py:276
  45.6 10.3 %collective-permute-start.9 = (f32[8,1024]{1,0:T(8,128)S(1)}, f32[8,1024]{1,0:T(8,128)S(1)}, u32[]{:S(2)}, u32[]{:S(2)}) collective-permute-start(f32[8,1024]{1,0:T(8,128)S(1)} %get-tuple-element.33.s0), channel_id=1, source_target_pairs={{0,2},{1,3},{2,0},{3,1},{4,6},{5,7},{6,4},{7,5},{8,10},{9,11},{10,... | collective-permute-start | bytes 98312 | tf_op jit(solution)/shard_map/ppermute | solution.py:276
  46.3 18.1 %collective-permute-start.15 = (bf16[256,768]{1,0:T(8,128)(2,1)S(1)}, bf16[256,768]{1,0:T(8,128)(2,1)S(1)}, u32[]{:S(2)}, u32[]{:S(2)}) collective-permute-start(bf16[256,768]{1,0:T(8,128)(2,1)S(1)} %get-tuple-element.56), channel_id=1, source_target_pairs={{0,254},{1,255},{2,252},{3,253},{4,2},{5,3},{6,0},{7,1},{8,6},{9,7... | collective-permute-start | bytes 1179656 | tf_op jit(solution)/shard_map/ppermute | solution.py:284
  55.0 17.4 %collective-permute-start.16 = (bf16[256,768]{1,0:T(8,128)(2,1)S(1)}, bf16[256,768]{1,0:T(8,128)(2,1)S(1)}, u32[]{:S(2)}, u32[]{:S(2)}) collective-permute-start(bf16[256,768]{1,0:T(8,128)(2,1)S(1)} %get-tuple-element.57), channel_id=1, source_target_pairs={{0,248},{1,249},{2,250},{3,251},{4,252},{5,253},{6,254},{7,255},{8... | collective-permute-start | bytes 1179656 | tf_op jit(solution)/shard_map/ppermute | solution.py:284
  56.1 16.2 %collective-permute-start.14 = (bf16[256,768]{1,0:T(8,128)(2,1)S(1)}, bf16[256,768]{1,0:T(8,128)(2,1)S(1)}, u32[]{:S(2)}, u32[]{:S(2)}) collective-permute-start(bf16[256,768]{1,0:T(8,128)(2,1)S(1)} %half_sum.1), channel_id=1, source_target_pairs={{0,2},{1,3},{2,0},{3,1},{4,6},{5,7},{6,4},{7,5},{8,10},{9,11},{10,... | collective-permute-start | bytes 1179656 | tf_op jit(solution)/shard_map/ppermute | solution.py:276
  56.9 1.2 %collective-permute-start.5 = (f32[8,1024]{1,0:T(8,128)S(1)}, f32[8,1024]{1,0:T(8,128)S(1)}, u32[]{:S(2)}, u32[]{:S(2)}) collective-permute-start(f32[8,1024]{1,0:T(8,128)S(1)} %get-tuple-element.33.s0), channel_id=1, source_target_pairs={{0,1},{1,0},{2,3},{3,2},{4,5},{5,4},{6,7},{7,6},{8,9},{9,8},{10,11... | collective-permute-start | bytes 98312 | tf_op jit(solution)/shard_map/ppermute | solution.py:276
  58.1 1.2 %collective-permute-start.10 = (f32[8,1024]{1,0:T(8,128)S(1)}, f32[8,1024]{1,0:T(8,128)S(1)}, u32[]{:S(2)}, u32[]{:S(2)}) collective-permute-start(f32[8,1024]{1,0:T(8,128)S(1)} %collective-permute-done.9.s2), channel_id=1, source_target_pairs={{0,1},{1,0},{2,3},{3,2},{4,5},{5,4},{6,7},{7,6},{8,9},{9,8},{10,11... | collective-permute-start | bytes 98312 | tf_op jit(solution)/shard_map/ppermute | solution.py:276
  59.3 1.5 %collective-permute-start.11 = (bf16[512,256]{1,0:T(8,128)(2,1)S(1)}, bf16[512,256]{1,0:T(8,128)(2,1)S(1)}, u32[]{:S(2)}, u32[]{:S(2)}) collective-permute-start(bf16[512,256]{1,0:T(8,128)(2,1)S(1)} %collective-permute-done.7), channel_id=1, source_target_pairs={{0,1},{1,0},{2,3},{3,2},{4,5},{5,4},{6,7},{7,6},{8,9},{9,8},{10,11... | collective-permute-start | bytes 786440 | tf_op jit(solution)/shard_map/ppermute | solution.py:276
  72.5 10.6 %collective-permute-start.18 = (bf16[256,768]{1,0:T(8,128)(2,1)S(1)}, bf16[256,768]{1,0:T(8,128)(2,1)S(1)}, u32[]{:S(2)}, u32[]{:S(2)}) collective-permute-start(bf16[256,768]{1,0:T(8,128)(2,1)S(1)} %row_grad.1.g0), channel_id=1, source_target_pairs={{0,2},{1,3},{2,0},{3,1},{4,6},{5,7},{6,4},{7,5},{8,10},{9,11},{10,... | collective-permute-start | bytes 1179656 | tf_op jit(solution)/shard_map/ppermute | solution.py:276
  74.5 8.6 %collective-permute-start.17 = (bf16[256,768]{1,0:T(8,128)(2,1)S(1)}, bf16[256,768]{1,0:T(8,128)(2,1)S(1)}, u32[]{:S(2)}, u32[]{:S(2)}) collective-permute-start(bf16[256,768]{1,0:T(8,128)(2,1)S(1)} %row_grad.1.g0), channel_id=1, source_target_pairs={{0,1},{1,0},{2,3},{3,2},{4,5},{5,4},{6,7},{7,6},{8,9},{9,8},{10,11... | collective-permute-start | bytes 1179656 | tf_op jit(solution)/shard_map/ppermute | solution.py:276
  83.1 1.7 %collective-permute-start.19 = (bf16[256,768]{1,0:T(8,128)(2,1)S(1)}, bf16[256,768]{1,0:T(8,128)(2,1)S(1)}, u32[]{:S(2)}, u32[]{:S(2)}) collective-permute-start(bf16[256,768]{1,0:T(8,128)(2,1)S(1)} %collective-permute-done.18.g2), channel_id=1, source_target_pairs={{0,1},{1,0},{2,3},{3,2},{4,5},{5,4},{6,7},{7,6},{8,9},{9,8},{10,11... | collective-permute-start | bytes 1179656 | tf_op jit(solution)/shard_map/ppermute | solution.py:276

commit v5 on v4

--- a/solution.py
+++ b/solution.py
@@ -160,8 +160,23 @@
     return ref[n : n + META, :n].astype(f32)[i : i + 1, :]
 
 
-def score_kernel(
-    scal_ref, p0, p1, p2, p3, n1, n2, anchors_ref, c0, c1, c2, sums_ref, grad0, grad1, grad2,
+def score_negatives(
+    offset, scal_ref, p, tile, anchors_ref, coef_ref, sums_ref, grad_ref, products_ref, lanes_ref,
+    sq_ref, label_ref,
+):
+    n = p.shape[0] - META
+    labels = meta_row(p, n, 0) * 128.0 + meta_row(p, n, 1)
+    label_ref[...] = jnp.broadcast_to(column(labels), label_ref.shape)
+    rows_n = p[:n, :]
+    score_block(
+        rows_n, scal_ref[1 + offset] > 0, tile, anchors_ref, label_ref, products_ref, coef_ref,
+        lanes_ref, sq_ref, sums_ref,
+    )
+    grad_ref[...] = negative_grad(rows_n, tile, coef_ref, lanes_ref).astype(grad_ref.dtype)
+
+
+def own_kernel(
+    scal_ref, p0, p1, p2, p3, n2, anchors_ref, c0, c2, sums_ref, grad0, grad2,
     products_ref, lanes_ref, sq_ref, label_ref,
 ):
     blocks = (p0, p1, p2, p3)
@@ -194,17 +209,24 @@
         anchors_ref[6:7, lanes] = weight * scale
         anchors_ref[7:8, lanes] = meta[0:1, :] * 128.0 + meta[1:2, :]
     sums_ref[...] = jnp.zeros_like(sums_ref)
-    negatives = ((p0, c0, grad0), (n1, c1, grad1), (n2, c2, grad2))
-    for offset, (p, coef_ref, grad_ref) in enumerate(negatives):
-        labels = meta_row(p, n, 0) * 128.0 + meta_row(p, n, 1)
-        label_ref[...] = jnp.broadcast_to(column(labels), label_ref.shape)
-        rows_n = p[:n, :]
-        score_block(
-            rows_n, scal_ref[1 + offset] > 0, tile, anchors_ref, label_ref, products_ref, coef_ref,
-            lanes_ref, sq_ref, sums_ref,
+    for offset, p, coef_ref, grad_ref in ((0, p0, c0, grad0), (2, n2, c2, grad2)):
+        score_negatives(
+            offset, scal_ref, p, tile, anchors_ref, coef_ref, sums_ref, grad_ref, products_ref,
+            lanes_ref, sq_ref, label_ref,
         )
-        grad = negative_grad(rows_n, tile, coef_ref, lanes_ref)
-        grad_ref[...] = grad.astype(grad_ref.dtype)
+
+
+def earlier_kernel(
+    scal_ref, rows_ref, p0, p1, p2, p3, anchors_ref, before_ref, coef_ref, sums_ref,
+    grad_ref, products_ref, lanes_ref, sq_ref, label_ref,
+):
+    n = p0.shape[0] - META
+    tile = [p[:n, :] for p in (p0, p1, p2, p3)]
+    sums_ref[...] = before_ref[...]
+    score_negatives(
+        1, scal_ref, rows_ref, tile, anchors_ref, coef_ref, sums_ref, grad_ref, products_ref,
+        lanes_ref, sq_ref, label_ref,
+    )
     for k in range(3):
         sums_ref[k : k + 1, :] = sums_ref[k : k + 1, :] * anchors_ref[6:7, :]
 
@@ -254,9 +276,19 @@
     out_ref[...] = base + 2.0 * (pushed * tile[0].astype(f32) - total)
 
 
-def gathered_kernel(base_ref, y_ref, one_ref, two_ref, out_ref):
+def passed_kernel(scal_ref, grad_ref, swapped_ref, out_ref):
+    extra = jnp.where(scal_ref[4] > 0, swapped_ref[...].astype(f32), 0.0)
+    out_ref[...] = (grad_ref[...] + extra).astype(bf16)
+
+
+def gathered_kernel(scal_ref, base_ref, y_ref, swapped_ref, two_ref, out_ref):
+    extra = jnp.where(scal_ref[4] > 0, 0.0, swapped_ref[...].astype(f32))
     total = base_ref[...] + y_ref[...].astype(f32)
-    out_ref[...] = (total + (one_ref[...].astype(f32) + two_ref[...].astype(f32))).astype(bf16)
+    out_ref[...] = (total + (extra + two_ref[...].astype(f32))).astype(bf16)
+
+
+def chosen_kernel(scal_ref, own_ref, other_ref, out_ref):
+    out_ref[...] = jnp.where(scal_ref[4] > 0, other_ref[...], own_ref[...])
 
 
 def head_kernel(f0, f1, f2, f3, g0, g1, g2, g3, out_ref):
@@ -275,17 +307,20 @@
     def over_rows(x, flip):
         return lax.ppermute(x, "rows", [(i, i ^ flip) for i in range(rows_n)])
 
-    def along(x, by, flip):
+    def two_on(x, by):
+        return lax.ppermute(x, "blk", [(b, (b + by) % blks) for b in range(blks)])
+
+    def swapped(x):
         pairs = [
-            (b * rows_n + i, (b + by) % blks * rows_n + (i ^ flip))
-            for b in range(blks)
-            for i in range(rows_n)
+            (b * rows_n + i, (b ^ 1) * rows_n + (i ^ 2)) for b in range(blks) for i in range(rows_n)
         ]
         return lax.ppermute(x, ("blk", "rows"), pairs)
 
+    odd = lax.axis_index("blk") % 2
+    scal = jnp.concatenate([me[None], pair_mask[0], odd[None]]).astype(jnp.int32)
     p0 = embed(features, head_weight, labels[None], pos_index.T, loss_weight[None])
     p2 = over_rows(p0, 2)
-    n1, n2 = along(p0, 1, 2), along(p0, 2, 0)
+    n2 = two_on(p0, 2)
     p1 = over_rows(p0, 1)
 
     features, _ = lax.optimization_barrier((features, p0))
@@ -300,20 +335,36 @@
     f1 = over_rows(turned[1], 1)
     f2, f3 = over_rows(turned[2], 2), over_rows(turned[3], 2)
 
-    scal = jnp.concatenate([me[None].astype(jnp.int32), pair_mask[0]])
+    (chosen,) = call(
+        chosen_kernel,
+        (scal, p0, n2),
+        [shape(n + META, wide, dtype=bf16)],
+        micros=0.01,
+        name="row_choice",
+    )
+    n1 = swapped(chosen)
     scratch = [pltpu.VMEM((n, n), f32)] + [pltpu.VMEM((n, 128), f32)] * 3
     tile = (p0, p1, p2, p3)
     low_grad = shape(n, wide, dtype=bf16)
     low_coef = shape(n, 4 * n, dtype=bf16)
-    anchors, c0, c1, c2, s0, own_grad, grad1, grad2 = call(
-        score_kernel,
-        (scal, *tile, n1, n2),
-        [shape(8, 4 * n)] + [low_coef] * 3 + [shape(8, 4 * n), shape(n, wide)] + [low_grad] * 2,
+    anchors, c0, c2, sums, own_grad, grad2 = call(
+        own_kernel,
+        (scal, *tile, n2),
+        [shape(8, 4 * n), low_coef, low_coef, shape(8, 4 * n), shape(n, wide), shape(n, wide)],
         scratch,
         micros=0.01,
-        name="score",
-    )
-    c0, f2, f3 = lax.optimization_barrier((c0, f2, f3))
+        name="own_and_two_before",
+    )
+    c1, s0, grad1 = call(
+        earlier_kernel,
+        (scal, n1, *tile, anchors, sums),
+        [low_coef, shape(8, 4 * n), low_grad],
+        scratch,
+        micros=0.01,
+        name="block_before",
+    )
+    grad1 = swapped(grad1)
+    c1, f2, f3 = lax.optimization_barrier((c1, f2, f3))
     s2 = over_rows(s0, 2)
     s1 = over_rows(s0, 1)
     pieces = (c0, c1, c2, p0, n1, n2)
@@ -326,7 +377,11 @@
         halved_kernel, (keep, over_rows(send, 1)), [low_grad], micros=0.01, name="half_sum"
     )
     from_y = over_rows(half, 2)
-    grad1, grad2 = along(grad1, -1, 2), along(grad2, -2, 0)
+    grad2, _ = lax.optimization_barrier((grad2, half))
+    (grad2,) = call(
+        passed_kernel, (scal, grad2, grad1), [low_grad], micros=0.01, name="passed_grad"
+    )
+    grad2 = two_on(grad2, -2)
     f3, s3 = over_rows(f3, 1), over_rows(s2, 1)
     keep, send = call(
         functools.partial(anchor_kernel, 0), pieces, rows_f32, micros=0.01, name="anchor_grad_own"
@@ -340,7 +395,7 @@
         name="listed",
     )
     (g0,) = call(
-        gathered_kernel, (base, from_y, grad1, grad2), [low_grad], micros=0.01, name="row_grad"
+        gathered_kernel, (scal, base, from_y, grad1, grad2), [low_grad], micros=0.01, name="row_grad"
     )
     g2 = over_rows(g0, 2)
     g1 = over_rows(g0, 1)

time: 119 us -> 117 us (0.983)
  starting transfers between devices: 20.6 us -> 16.8 us
  Pallas kernels: 25 us -> 27.4 us
    ppermute x4, starting transfers between devices: 12.2 us -> 4.56 us  [the longest x2 2.6 us: swapped(): return lax.ppermute(x, ('blk', 'rows'), pairs)]
    ppermute x4, waiting for transfers between devices: 18.6 us -> 14.3 us  [the longest x2 7.68 us: two_on(): return lax.ppermute(x, 'blk', [(b, (b + by) % blks) for b in range(blks)])]
    ppermute x16, waiting for transfers between devices: 18.2 us -> 22.3 us  [over_rows(): return lax.ppermute(x, 'rows', [(i, i ^ flip) for i in range(rows_n)])]
    ppermute x16, starting transfers between devices: 8.39 us -> 12.2 us  [over_rows(): return lax.ppermute(x, 'rows', [(i, i ^ flip) for i in range(rows_n)])]
    pallas_call x7 -> x10, Pallas kernels: 21 us -> 23.4 us  [call(): pl.pallas_call(kernel, out_shape=outs, in_specs=[SMEM if x.ndim == 1 else...]
  transfers between devices with their start and end apart: 20 -> 20, of which waited for: 9 -> 10; matrix products, arithmetic and copies ran while one was open for 2% -> 2% of each run, Pallas kernels for 16% -> 18%
where the time goes in v5:
time: 117 us
  waiting for transfers between devices  36.6 us (31%)
  blocking collectives  32 us (27%)
  Pallas kernels  27.4 us (23%)
  starting transfers between devices  16.8 us (14%)
  local copies, waits for them, and re-layouts  2.59 us (2%)
    all_to_all x1, blocking collectives, local(): parts = lax.all_to_all(part, 'blk', split_axis=0, concat_axis=0, tiled=True)  32 us
    pallas_call x10, Pallas kernels, call(): pl.pallas_call(kernel, out_shape=outs, in_specs=[SMEM if x.ndim == 1 else...  23.4 us
    ppermute x16, waiting for transfers between devices, over_rows(): return lax.ppermute(x, 'rows', [(i, i ^ flip) for i in range(rows_n)])  22.3 us
    ppermute x16, starting transfers between devices, over_rows(): return lax.ppermute(x, 'rows', [(i, i ^ flip) for i in range(rows_n)])  12.2 us
    ppermute x2, waiting for transfers between devices, two_on(): return lax.ppermute(x, 'blk', [(b, (b + by) % blks) for b in range(blks)])  7.68 us
    ppermute x2, waiting for transfers between devices, swapped(): return lax.ppermute(x, ('blk', 'rows'), pairs)  6.58 us
    pallas_call x1, Pallas kernels, embed(): pl.pallas_call(embed_kernel, grid=(wide // step,), out_shape=shape(n + ME...  4 us
    ppermute x2, starting transfers between devices, swapped(): return lax.ppermute(x, ('blk', 'rows'), pairs)  2.6 us
  transfers between devices with their start and end apart: 20, of which 10 were waited for; matrix products, arithmetic and copies ran while one was open for 2% of the time, Pallas kernels for 18%

profile of v5, /device:TPU:8, one launch (start us, length us, event | category | flops | bytes accessed | tf_op | source)
XLA Modules:
  0.0 117.0 jit_solution(1296178589666068804)
XLA Ops:
  0.7 4.0 %embed.1.p0.own_ref.n0 = bf16[272,768]{1,0:T(8,128)(2,1)} custom-call(bf16[256,2048]{1,0:T(8,128)(2,1)} %features_ref.1, bf16[2048,768]{1,0:T(8,128)(2,1)} %weight_ref.1, s32[1,256]{1,0:T(1,128)} %bitcast.22, s32[3,256]{1,0:T(4,128)} %bitcast.21, f32[1,256]{1,0:T(1,128)} %bitcast.23), custom_call_target="tpu_custom_call" | custom-call | flops 1073741824 | bytes 4194304 | tf_op jit(solution)/shard_map/embed/pallas_call | solution.py:75
  4.6 2.2 %collective-permute-start.1 = (bf16[272,768]{1,0:T(8,128)(2,1)}, bf16[272,768]{1,0:T(8,128)(2,1)S(1)}, u32[]{:S(2)}, u32[]{:S(2)}) collective-permute-start(bf16[272,768]{1,0:T(8,128)(2,1)} %embed.1.p0.own_ref.n0), channel_id=1, source_target_pairs={{0,2},{1,3},{2,0},{3,1},{4,6},{5,7},{6,4},{7,5},{8,10},{9,11},{10,... | collective-permute-start | bytes 1253384 | tf_op jit(solution)/shard_map/ppermute | solution.py:308
  7.0 1.3 %copy.12 = bf16[256,2048]{0,1:T(8,128)(2,1)} copy(bf16[256,2048]{1,0:T(8,128)(2,1)S(1)} %copy-done.1) | data formatting | bytes 2097152 | tf_op jit(solution)/shard_map/optimization_barrier | solution.py:326
  8.4 1.3 %dynamic-slice_bitcast_fusion = (bf16[512,256]{1,0:T(8,128)(2,1)S(1)}, bf16[512,256]{1,0:T(8,128)(2,1)S(1)}, bf16[512,256]{1,0:T(8,128)(2,1)S(1)}, bf16[512,256]{1,0:T(8,128)(2,1)S(1)}) fusion(bf16[64,4,8,256]{3,2,1,0:T(8,128)(2,1)} %bitcast.20, s32[]{:T(128)S(6)} %select_n.24, s32[]{:T(128)S(6)} %select_n.23, s32[]{:T(128)S(6)} %select_n.22, s32[]{:T(128)S(6)} %select_n.21), kind=kLoop, calls=%fused_computation.1 | loop fusion | bytes 2097168 | tf_op jit(solution)/shard_map/reshape | solution.py:330
  9.7 6.6 %collective-permute-done.1.p2 = bf16[272,768]{1,0:T(8,128)(2,1)S(1)} collective-permute-done((bf16[272,768]{1,0:T(8,128)(2,1)}, bf16[272,768]{1,0:T(8,128)(2,1)S(1)}, u32[]{:S(2)}, u32[]{:S(2)}) %collective-permute-start.1) | collective-permute-done | bytes 417824 | tf_op jit(solution)/shard_map/ppermute | solution.py:308
  16.2 6.5 %collective-permute-done.3.n2.other_ref = bf16[272,768]{1,0:T(8,128)(2,1)S(1)} collective-permute-done((bf16[272,768]{1,0:T(8,128)(2,1)}, bf16[272,768]{1,0:T(8,128)(2,1)S(1)}, u32[]{:S(2)}, u32[]{:S(2)}) %collective-permute-start.3) | collective-permute-done | bytes 417824 | tf_op jit(solution)/shard_map/ppermute | solution.py:311
  22.8 0.6 row_choice.1
  23.3 2.5 %collective-permute-start.4 = (bf16[272,768]{1,0:T(8,128)(2,1)S(1)}, bf16[272,768]{1,0:T(8,128)(2,1)S(1)}, u32[]{:S(2)}, u32[]{:S(2)}) collective-permute-start(bf16[272,768]{1,0:T(8,128)(2,1)S(1)} %row_choice.1), channel_id=1, source_target_pairs={{0,6},{1,7},{2,4},{3,5},{4,2},{5,3},{6,0},{7,1},{8,14},{9,15},{10,... | collective-permute-start | bytes 1253384 | tf_op jit(solution)/shard_map/ppermute | solution.py:317
  25.8 1.3 %collective-permute-start.6 = (bf16[512,256]{1,0:T(8,128)(2,1)S(1)}, bf16[512,256]{1,0:T(8,128)(2,1)S(1)}, u32[]{:S(2)}, u32[]{:S(2)}) collective-permute-start(bf16[512,256]{1,0:T(8,128)(2,1)S(1)} %get-tuple-element.39), channel_id=1, source_target_pairs={{0,2},{1,3},{2,0},{3,1},{4,6},{5,7},{6,4},{7,5},{8,10},{9,11},{10,... | collective-permute-start | bytes 786440 | tf_op jit(solution)/shard_map/ppermute | solution.py:308
  27.2 0.7 collective-permute-start.7
  27.9 11.6 %own_and_two_before.1 = (f32[8,1024]{1,0:T(8,128)S(1)}, bf16[256,1024]{1,0:T(8,128)(2,1)S(1)}, bf16[256,1024]{1,0:T(8,128)(2,1)S(1)}, f32[8,1024]{1,0:T(8,128)S(...) custom-call(s32[5]{0:T(128)S(1)} %pad_add_fusion.scal_ref, bf16[272,768]{1,0:T(8,128)(2,1)S(1)} %copy-done, ...), custom_call_target="tpu_custom_call" | custom-call | flops 11500000 | bytes 1024 | tf_op jit(solution)/shard_map/own_and_two_before/pallas_call | solution.py:25
  39.5 5.1 %block_before.1 = (bf16[256,1024]{1,0:T(8,128)(2,1)S(1)}, f32[8,1024]{1,0:T(8,128)S(1)}, bf16[256,768]{1,0:T(8,128)(2,1)S(1)}) custom-call(s32[5]{0:T(128)S(1)} %pad_add_fusion.scal_ref, bf16[272,768]{1,0:T(8,128)(2,1)S(1)} %collective-permute-done.4.rows_ref.n1, bf16[272,768]{1,0:T(8,128)(2,1)S(1)} %copy-done, ...), custom_call_target="tpu_custom_call" | custom-call | flops 11500000 | bytes 1024 | tf_op jit(solution)/shard_map/block_before/pallas_call | solution.py:25
  44.6 0.8 anchor_grad_across.1
  45.6 0.8 anchor_grad_own.1
  47.2 2.2 %collective-permute-start.9 = (f32[8,1024]{1,0:T(8,128)S(1)}, f32[8,1024]{1,0:T(8,128)S(1)}, u32[]{:S(2)}, u32[]{:S(2)}) collective-permute-start(f32[8,1024]{1,0:T(8,128)S(1)} %get-tuple-element.36.s0), channel_id=1, source_target_pairs={{0,2},{1,3},{2,0},{3,1},{4,6},{5,7},{6,4},{7,5},{8,10},{9,11},{10,... | collective-permute-start | bytes 98312 | tf_op jit(solution)/shard_map/ppermute | solution.py:308
  49.4 2.1 %collective-permute-done.9.s2 = f32[8,1024]{1,0:T(8,128)S(1)} collective-permute-done((f32[8,1024]{1,0:T(8,128)S(1)}, f32[8,1024]{1,0:T(8,128)S(1)}, u32[]{:S(2)}, u32[]{:S(2)}) %collective-permute-start.9) | collective-permute-done | bytes 32800 | tf_op jit(solution)/shard_map/ppermute | solution.py:308
  51.5 6.6 %collective-permute-done.15.swapped_ref = bf16[256,768]{1,0:T(8,128)(2,1)S(1)} collective-permute-done((bf16[256,768]{1,0:T(8,128)(2,1)S(1)}, bf16[256,768]{1,0:T(8,128)(2,1)S(1)}, u32[]{:S(2)}, u32[]{:S(2)}) %collective-permute-start.15) | collective-permute-done | bytes 393248 | tf_op jit(solution)/shard_map/ppermute | solution.py:317
  58.1 0.6 passed_grad.1
  58.7 1.8 %collective-permute-start.16 = (bf16[256,768]{1,0:T(8,128)(2,1)S(1)}, bf16[256,768]{1,0:T(8,128)(2,1)S(1)}, u32[]{:S(2)}, u32[]{:S(2)}) collective-permute-start(bf16[256,768]{1,0:T(8,128)(2,1)S(1)} %passed_grad.1), channel_id=1, source_target_pairs={{0,248},{4,252},{8,0},{12,4},{16,8},{20,12},{24,16},{28,20},{32,24... | collective-permute-start | bytes 1179656 | tf_op jit(solution)/shard_map/ppermute | solution.py:311
  60.5 2.6 %collective-permute-start.14 = (bf16[256,768]{1,0:T(8,128)(2,1)S(1)}, bf16[256,768]{1,0:T(8,128)(2,1)S(1)}, u32[]{:S(2)}, u32[]{:S(2)}) collective-permute-start(bf16[256,768]{1,0:T(8,128)(2,1)S(1)} %half_sum.1), channel_id=1, source_target_pairs={{0,2},{1,3},{2,0},{3,1},{4,6},{5,7},{6,4},{7,5},{8,10},{9,11},{10,... | collective-permute-start | bytes 1179656 | tf_op jit(solution)/shard_map/ppermute | solution.py:308
  63.6 1.1 collective-permute-done.5.s1
  64.8 1.1 collective-permute-done.10.s3
  65.9 2.1 %listed.1 = (f32[256,768]{1,0:T(8,128)S(1)}, f32[1,256]{1,0:T(1,128)}) custom-call(f32[8,1024]{1,0:T(8,128)S(1)} %get-tuple-element.34.anchors_ref, f32[8,1024]{1,0:T(8,128)S(1)} %get-tuple-element.36.s0, f32[8,1024]{1,0:T(8,128)S(1)} %collective-permute-done.5.s1, f32[8,1024]{1,0:T(8,128)S(1)} %collective-permute-done.9.s2, ...), custom_call_target="tpu_custom_call" | custom-call | flops 11500000 | bytes 1024 | tf_op jit(solution)/shard_map/listed/pallas_call | solution.py:25
  67.9 1.2 %collective-permute-done.16.two_ref = bf16[256,768]{1,0:T(8,128)(2,1)S(1)} collective-permute-done((bf16[256,768]{1,0:T(8,128)(2,1)S(1)}, bf16[256,768]{1,0:T(8,128)(2,1)S(1)}, u32[]{:S(2)}, u32[]{:S(2)}) %collective-permute-start.16) | collective-permute-done | bytes 393248 | tf_op jit(solution)/shard_map/ppermute | solution.py:311
  69.1 2.2 %collective-permute-done.14.y_ref = bf16[256,768]{1,0:T(8,128)(2,1)S(1)} collective-permute-done((bf16[256,768]{1,0:T(8,128)(2,1)S(1)}, bf16[256,768]{1,0:T(8,128)(2,1)S(1)}, u32[]{:S(2)}, u32[]{:S(2)}) %collective-permute-start.14) | collective-permute-done | bytes 393248 | tf_op jit(solution)/shard_map/ppermute | solution.py:308
  71.3 0.7 row_grad.1.g0
  72.1 1.8 %collective-permute-start.18 = (bf16[256,768]{1,0:T(8,128)(2,1)S(1)}, bf16[256,768]{1,0:T(8,128)(2,1)S(1)}, u32[]{:S(2)}, u32[]{:S(2)}) collective-permute-start(bf16[256,768]{1,0:T(8,128)(2,1)S(1)} %row_grad.1.g0), channel_id=1, source_target_pairs={{0,2},{1,3},{2,0},{3,1},{4,6},{5,7},{6,4},{7,5},{8,10},{9,11},{10,... | collective-permute-start | bytes 1179656 | tf_op jit(solution)/shard_map/ppermute | solution.py:308
  73.9 7.6 %collective-permute-done.18.g2 = bf16[256,768]{1,0:T(8,128)(2,1)S(1)} collective-permute-done((bf16[256,768]{1,0:T(8,128)(2,1)S(1)}, bf16[256,768]{1,0:T(8,128)(2,1)S(1)}, u32[]{:S(2)}, u32[]{:S(2)}) %collective-permute-start.18) | collective-permute-done | bytes 393248 | tf_op jit(solution)/shard_map/ppermute | solution.py:308
  81.5 1.7 %collective-permute-done.19.g3 = bf16[256,768]{1,0:T(8,128)(2,1)S(1)} collective-permute-done((bf16[256,768]{1,0:T(8,128)(2,1)S(1)}, bf16[256,768]{1,0:T(8,128)(2,1)S(1)}, u32[]{:S(2)}, u32[]{:S(2)}) %collective-permute-start.19) | collective-permute-done | bytes 393248 | tf_op jit(solution)/shard_map/ppermute | solution.py:308
  83.3 1.0 head_grad.1
  84.3 32.0 %all_to_all.9 = bf16[64,8,768]{2,1,0:T(8,128)(2,1)S(1)} all-to-all(bf16[64,8,768]{2,1,0:T(8,128)(2,1)S(1)} %bitcast.19), channel_id=1, replica_groups=mesh['blk'=64,'rows'=4] {'blk'}, dimensions={0} | all-to-all | bytes 1572864 | tf_op jit(solution)/shard_map/all_to_all | solution.py:409
  116.3 0.7 convert_reduce_fusion
  (30 shorter events, 1.9 us)
Async XLA Ops:
  0.6 6.4 %copy-start.1 = (bf16[256,2048]{1,0:T(8,128)(2,1)S(1)}, bf16[256,2048]{1,0:T(8,128)(2,1)}, u32[]{:S(2)}) copy-start(bf16[256,2048]{1,0:T(8,128)(2,1)} %features_ref.1) | copy-start | bytes 3145732
  0.6 7.7 %copy-start.2 = (s32[1,3]{1,0:T(1,128)S(1)}, s32[1,3]{1,0:T(1,128)}, u32[]{:S(2)}) copy-start(s32[1,3]{1,0:T(1,128)} %param.10) | copy-start | bytes 40
  4.6 18.1 %copy-start = (bf16[272,768]{1,0:T(8,128)(2,1)S(1)}, bf16[272,768]{1,0:T(8,128)(2,1)}, u32[]{:S(2)}) copy-start(bf16[272,768]{1,0:T(8,128)(2,1)} %embed.1.p0.own_ref.n0) | copy-start | bytes 1253380
  4.6 11.6 %collective-permute-start.1 = (bf16[272,768]{1,0:T(8,128)(2,1)}, bf16[272,768]{1,0:T(8,128)(2,1)S(1)}, u32[]{:S(2)}, u32[]{:S(2)}) collective-permute-start(bf16[272,768]{1,0:T(8,128)(2,1)} %embed.1.p0.own_ref.n0), channel_id=1, source_target_pairs={{0,2},{1,3},{2,0},{3,1},{4,6},{5,7},{6,4},{7,5},{8,10},{9,11},{10,... | collective-permute-start | bytes 1253384 | tf_op jit(solution)/shard_map/ppermute | solution.py:308
  6.8 15.9 %collective-permute-start.3 = (bf16[272,768]{1,0:T(8,128)(2,1)}, bf16[272,768]{1,0:T(8,128)(2,1)S(1)}, u32[]{:S(2)}, u32[]{:S(2)}) collective-permute-start(bf16[272,768]{1,0:T(8,128)(2,1)} %embed.1.p0.own_ref.n0), channel_id=1, source_target_pairs={{0,8},{4,12},{8,16},{12,20},{16,24},{20,28},{24,32},{28,36},{32,40... | collective-permute-start | bytes 1253384 | tf_op jit(solution)/shard_map/ppermute | solution.py:311
  7.0 20.9 %collective-permute-start = (bf16[272,768]{1,0:T(8,128)(2,1)}, bf16[272,768]{1,0:T(8,128)(2,1)S(1)}, u32[]{:S(2)}, u32[]{:S(2)}) collective-permute-start(bf16[272,768]{1,0:T(8,128)(2,1)} %embed.1.p0.own_ref.n0), channel_id=1, source_target_pairs={{0,1},{1,0},{2,3},{3,2},{4,5},{5,4},{6,7},{7,6},{8,9},{9,8},{10,11... | collective-permute-start | bytes 1253384 | tf_op jit(solution)/shard_map/ppermute | solution.py:308
  16.2 11.6 %collective-permute-start.2 = (bf16[272,768]{1,0:T(8,128)(2,1)S(1)}, bf16[272,768]{1,0:T(8,128)(2,1)S(1)}, u32[]{:S(2)}, u32[]{:S(2)}) collective-permute-start(bf16[272,768]{1,0:T(8,128)(2,1)S(1)} %collective-permute-done.1.p2), channel_id=1, source_target_pairs={{0,1},{1,0},{2,3},{3,2},{4,5},{5,4},{6,7},{7,6},{8,9},{9,8},{10,11... | collective-permute-start | bytes 1253384 | tf_op jit(solution)/shard_map/ppermute | solution.py:308
  23.3 16.2 %collective-permute-start.4 = (bf16[272,768]{1,0:T(8,128)(2,1)S(1)}, bf16[272,768]{1,0:T(8,128)(2,1)S(1)}, u32[]{:S(2)}, u32[]{:S(2)}) collective-permute-start(bf16[272,768]{1,0:T(8,128)(2,1)S(1)} %row_choice.1), channel_id=1, source_target_pairs={{0,6},{1,7},{2,4},{3,5},{4,2},{5,3},{6,0},{7,1},{8,14},{9,15},{10,... | collective-permute-start | bytes 1253384 | tf_op jit(solution)/shard_map/ppermute | solution.py:317
  25.8 18.8 %collective-permute-start.6 = (bf16[512,256]{1,0:T(8,128)(2,1)S(1)}, bf16[512,256]{1,0:T(8,128)(2,1)S(1)}, u32[]{:S(2)}, u32[]{:S(2)}) collective-permute-start(bf16[512,256]{1,0:T(8,128)(2,1)S(1)} %get-tuple-element.39), channel_id=1, source_target_pairs={{0,2},{1,3},{2,0},{3,1},{4,6},{5,7},{6,4},{7,5},{8,10},{9,11},{10,... | collective-permute-start | bytes 786440 | tf_op jit(solution)/shard_map/ppermute | solution.py:308
  27.2 17.4 %collective-permute-start.7 = (bf16[512,256]{1,0:T(8,128)(2,1)S(1)}, bf16[512,256]{1,0:T(8,128)(2,1)S(1)}, u32[]{:S(2)}, u32[]{:S(2)}) collective-permute-start(bf16[512,256]{1,0:T(8,128)(2,1)S(1)} %get-tuple-element.40), channel_id=1, source_target_pairs={{0,2},{1,3},{2,0},{3,1},{4,6},{5,7},{6,4},{7,5},{8,10},{9,11},{10,... | collective-permute-start | bytes 786440 | tf_op jit(solution)/shard_map/ppermute | solution.py:308
  45.5 6.0 %collective-permute-start.13 = (f32[256,768]{1,0:T(8,128)S(1)}, f32[256,768]{1,0:T(8,128)S(1)}, u32[]{:S(2)}, u32[]{:S(2)}) collective-permute-start(f32[256,768]{1,0:T(8,128)S(1)} %get-tuple-element.58), channel_id=1, source_target_pairs={{0,1},{1,0},{2,3},{3,2},{4,5},{5,4},{6,7},{7,6},{8,9},{9,8},{10,11... | collective-permute-start | bytes 2359304 | tf_op jit(solution)/shard_map/ppermute | solution.py:308
  46.4 19.5 %collective-permute-start.12 = (f32[256,768]{1,0:T(8,128)S(1)}, f32[256,768]{1,0:T(8,128)S(1)}, u32[]{:S(2)}, u32[]{:S(2)}) collective-permute-start(f32[256,768]{1,0:T(8,128)S(1)} %get-tuple-element.50), channel_id=1, source_target_pairs={{0,1},{1,0},{2,3},{3,2},{4,5},{5,4},{6,7},{7,6},{8,9},{9,8},{10,11... | collective-permute-start | bytes 2359304 | tf_op jit(solution)/shard_map/ppermute | solution.py:308
  47.0 11.1 %collective-permute-start.15 = (bf16[256,768]{1,0:T(8,128)(2,1)S(1)}, bf16[256,768]{1,0:T(8,128)(2,1)S(1)}, u32[]{:S(2)}, u32[]{:S(2)}) collective-permute-start(bf16[256,768]{1,0:T(8,128)(2,1)S(1)} %get-tuple-element.59), channel_id=1, source_target_pairs={{0,6},{1,7},{2,4},{3,5},{4,2},{5,3},{6,0},{7,1},{8,14},{9,15},{10,... | collective-permute-start | bytes 1179656 | tf_op jit(solution)/shard_map/ppermute | solution.py:317
  47.1 2.3 %collective-permute-start.8 = (bf16[512,256]{1,0:T(8,128)(2,1)S(1)}, bf16[512,256]{1,0:T(8,128)(2,1)S(1)}, u32[]{:S(2)}, u32[]{:S(2)}) collective-permute-start(bf16[512,256]{1,0:T(8,128)(2,1)S(1)} %get-tuple-element.44), channel_id=1, source_target_pairs={{0,1},{1,0},{2,3},{3,2},{4,5},{5,4},{6,7},{7,6},{8,9},{9,8},{10,11... | collective-permute-start | bytes 786440 | tf_op jit(solution)/shard_map/ppermute | solution.py:308
  47.2 4.3 %collective-permute-start.9 = (f32[8,1024]{1,0:T(8,128)S(1)}, f32[8,1024]{1,0:T(8,128)S(1)}, u32[]{:S(2)}, u32[]{:S(2)}) collective-permute-start(f32[8,1024]{1,0:T(8,128)S(1)} %get-tuple-element.36.s0), channel_id=1, source_target_pairs={{0,2},{1,3},{2,0},{3,1},{4,6},{5,7},{6,4},{7,5},{8,10},{9,11},{10,... | collective-permute-start | bytes 98312 | tf_op jit(solution)/shard_map/ppermute | solution.py:308
  58.7 10.4 %collective-permute-start.16 = (bf16[256,768]{1,0:T(8,128)(2,1)S(1)}, bf16[256,768]{1,0:T(8,128)(2,1)S(1)}, u32[]{:S(2)}, u32[]{:S(2)}) collective-permute-start(bf16[256,768]{1,0:T(8,128)(2,1)S(1)} %passed_grad.1), channel_id=1, source_target_pairs={{0,248},{4,252},{8,0},{12,4},{16,8},{20,12},{24,16},{28,20},{32,24... | collective-permute-start | bytes 1179656 | tf_op jit(solution)/shard_map/ppermute | solution.py:311
  60.5 10.8 %collective-permute-start.14 = (bf16[256,768]{1,0:T(8,128)(2,1)S(1)}, bf16[256,768]{1,0:T(8,128)(2,1)S(1)}, u32[]{:S(2)}, u32[]{:S(2)}) collective-permute-start(bf16[256,768]{1,0:T(8,128)(2,1)S(1)} %half_sum.1), channel_id=1, source_target_pairs={{0,2},{1,3},{2,0},{3,1},{4,6},{5,7},{6,4},{7,5},{8,10},{9,11},{10,... | collective-permute-start | bytes 1179656 | tf_op jit(solution)/shard_map/ppermute | solution.py:308
  63.1 2.8 %collective-permute-start.11 = (bf16[512,256]{1,0:T(8,128)(2,1)S(1)}, bf16[512,256]{1,0:T(8,128)(2,1)S(1)}, u32[]{:S(2)}, u32[]{:S(2)}) collective-permute-start(bf16[512,256]{1,0:T(8,128)(2,1)S(1)} %collective-permute-done.7), channel_id=1, source_target_pairs={{0,1},{1,0},{2,3},{3,2},{4,5},{5,4},{6,7},{7,6},{8,9},{9,8},{10,11... | collective-permute-start | bytes 786440 | tf_op jit(solution)/shard_map/ppermute | solution.py:308
  63.1 1.6 %collective-permute-start.5 = (f32[8,1024]{1,0:T(8,128)S(1)}, f32[8,1024]{1,0:T(8,128)S(1)}, u32[]{:S(2)}, u32[]{:S(2)}) collective-permute-start(f32[8,1024]{1,0:T(8,128)S(1)} %get-tuple-element.36.s0), channel_id=1, source_target_pairs={{0,1},{1,0},{2,3},{3,2},{4,5},{5,4},{6,7},{7,6},{8,9},{9,8},{10,11... | collective-permute-start | bytes 98312 | tf_op jit(solution)/shard_map/ppermute | solution.py:308
  64.7 1.2 %collective-permute-start.10 = (f32[8,1024]{1,0:T(8,128)S(1)}, f32[8,1024]{1,0:T(8,128)S(1)}, u32[]{:S(2)}, u32[]{:S(2)}) collective-permute-start(f32[8,1024]{1,0:T(8,128)S(1)} %collective-permute-done.9.s2), channel_id=1, source_target_pairs={{0,1},{1,0},{2,3},{3,2},{4,5},{5,4},{6,7},{7,6},{8,9},{9,8},{10,11... | collective-permute-start | bytes 98312 | tf_op jit(solution)/shard_map/ppermute | solution.py:308
  72.1 9.4 %collective-permute-start.18 = (bf16[256,768]{1,0:T(8,128)(2,1)S(1)}, bf16[256,768]{1,0:T(8,128)(2,1)S(1)}, u32[]{:S(2)}, u32[]{:S(2)}) collective-permute-start(bf16[256,768]{1,0:T(8,128)(2,1)S(1)} %row_grad.1.g0), channel_id=1, source_target_pairs={{0,2},{1,3},{2,0},{3,1},{4,6},{5,7},{6,4},{7,5},{8,10},{9,11},{10,... | collective-permute-start | bytes 1179656 | tf_op jit(solution)/shard_map/ppermute | solution.py:308
  73.9 7.6 %collective-permute-start.17 = (bf16[256,768]{1,0:T(8,128)(2,1)S(1)}, bf16[256,768]{1,0:T(8,128)(2,1)S(1)}, u32[]{:S(2)}, u32[]{:S(2)}) collective-permute-start(bf16[256,768]{1,0:T(8,128)(2,1)S(1)} %row_grad.1.g0), channel_id=1, source_target_pairs={{0,1},{1,0},{2,3},{3,2},{4,5},{5,4},{6,7},{7,6},{8,9},{9,8},{10,11... | collective-permute-start | bytes 1179656 | tf_op jit(solution)/shard_map/ppermute | solution.py:308
  81.5 1.7 %collective-permute-start.19 = (bf16[256,768]{1,0:T(8,128)(2,1)S(1)}, bf16[256,768]{1,0:T(8,128)(2,1)S(1)}, u32[]{:S(2)}, u32[]{:S(2)}) collective-permute-start(bf16[256,768]{1,0:T(8,128)(2,1)S(1)} %collective-permute-done.18.g2), channel_id=1, source_target_pairs={{0,1},{1,0},{2,3},{3,2},{4,5},{5,4},{6,7},{7,6},{8,9},{9,8},{10,11... | collective-permute-start | bytes 1179656 | tf_op jit(solution)/shard_map/ppermute | solution.py:308

commit v6 on v5

--- a/solution.py
+++ b/solution.py
@@ -21,7 +21,7 @@
 SMEM = pl.BlockSpec(memory_space=pltpu.SMEM)
 
 
-def call(kernel, inputs, outs, scratch=(), micros=0.01, name=None):
+def call(kernel, inputs, outs, scratch=(), name=None):
     return pl.pallas_call(
         kernel,
         out_shape=outs,
@@ -30,7 +30,7 @@
         scratch_shapes=list(scratch),
         compiler_params=pltpu.CompilerParams(vmem_limit_bytes=16 << 20),
         cost_estimate=pl.CostEstimate(
-            flops=int(micros * 1.15e9), bytes_accessed=1024, transcendentals=0
+            flops=1 << 20, bytes_accessed=1024, transcendentals=0
         ),
         name=name,
     )(*inputs)
@@ -216,27 +216,23 @@
         )
 
 
-def earlier_kernel(
-    scal_ref, rows_ref, p0, p1, p2, p3, anchors_ref, before_ref, coef_ref, sums_ref,
-    grad_ref, products_ref, lanes_ref, sq_ref, label_ref,
+def last_kernel(
+    scal_ref, n1, n2, p0, p1, p2, p3, c0, c2, anchors_ref, before_ref, sums_ref, grad_ref,
+    keep0, send1, keep2, send3, coef_ref, products_ref, lanes_ref, sq_ref, label_ref,
 ):
     n = p0.shape[0] - META
     tile = [p[:n, :] for p in (p0, p1, p2, p3)]
     sums_ref[...] = before_ref[...]
     score_negatives(
-        1, scal_ref, rows_ref, tile, anchors_ref, coef_ref, sums_ref, grad_ref, products_ref,
+        1, scal_ref, n1, tile, anchors_ref, coef_ref, sums_ref, grad_ref, products_ref,
         lanes_ref, sq_ref, label_ref,
     )
     for k in range(3):
         sums_ref[k : k + 1, :] = sums_ref[k : k + 1, :] * anchors_ref[6:7, :]
-
-
-def anchor_kernel(first, c0, c1, c2, n0, n1, n2, keep_ref, send_ref):
-    n = n0.shape[0] - META
-    for i, ref in ((first, keep_ref), (first + 1, send_ref)):
+    for i, ref in enumerate((keep0, send1, keep2, send3)):
         lanes = slice(i * n, (i + 1) * n)
-        total = tn(c0[:, lanes], n0[:n, :])
-        total = total + tn(c1[:, lanes], n1[:n, :]) + tn(c2[:, lanes], n2[:n, :])
+        total = tn(c0[:, lanes], p0[:n, :])
+        total = total + tn(coef_ref[:, lanes], n1[:n, :]) + tn(c2[:, lanes], n2[:n, :])
         ref[...] = 2.0 * total
 
 
@@ -276,15 +272,9 @@
     out_ref[...] = base + 2.0 * (pushed * tile[0].astype(f32) - total)
 
 
-def passed_kernel(scal_ref, grad_ref, swapped_ref, out_ref):
-    extra = jnp.where(scal_ref[4] > 0, swapped_ref[...].astype(f32), 0.0)
-    out_ref[...] = (grad_ref[...] + extra).astype(bf16)
-
-
-def gathered_kernel(scal_ref, base_ref, y_ref, swapped_ref, two_ref, out_ref):
-    extra = jnp.where(scal_ref[4] > 0, 0.0, swapped_ref[...].astype(f32))
+def gathered_kernel(base_ref, y_ref, one_ref, two_ref, out_ref):
     total = base_ref[...] + y_ref[...].astype(f32)
-    out_ref[...] = (total + (extra + two_ref[...].astype(f32))).astype(bf16)
+    out_ref[...] = (total + (one_ref[...].astype(f32) + two_ref[...].astype(f32))).astype(bf16)
 
 
 def chosen_kernel(scal_ref, own_ref, other_ref, out_ref):
@@ -313,6 +303,14 @@
     def swapped(x):
         pairs = [
             (b * rows_n + i, (b ^ 1) * rows_n + (i ^ 2)) for b in range(blks) for i in range(rows_n)
+        ]
+        return lax.ppermute(x, ("blk", "rows"), pairs)
+
+    def one_back(x):
+        pairs = [
+            (b * rows_n + i, (b - 1) % blks * rows_n + (i ^ 2))
+            for b in range(blks)
+            for i in range(rows_n)
         ]
         return lax.ppermute(x, ("blk", "rows"), pairs)
 
@@ -339,7 +337,6 @@
         chosen_kernel,
         (scal, p0, n2),
         [shape(n + META, wide, dtype=bf16)],
-        micros=0.01,
         name="row_choice",
     )
     n1 = swapped(chosen)
@@ -350,52 +347,36 @@
     anchors, c0, c2, sums, own_grad, grad2 = call(
         own_kernel,
         (scal, *tile, n2),
-        [shape(8, 4 * n), low_coef, low_coef, shape(8, 4 * n), shape(n, wide), shape(n, wide)],
+        [shape(8, 4 * n), low_coef, low_coef, shape(8, 4 * n), shape(n, wide), low_grad],
         scratch,
-        micros=0.01,
         name="own_and_two_before",
     )
-    c1, s0, grad1 = call(
-        earlier_kernel,
-        (scal, n1, *tile, anchors, sums),
-        [low_coef, shape(8, 4 * n), low_grad],
-        scratch,
-        micros=0.01,
+    grad2 = two_on(grad2, -2)
+    s0, grad1, keep0, send1, keep2, send3 = call(
+        last_kernel,
+        (scal, n1, n2, *tile, c0, c2, anchors, sums),
+        [shape(8, 4 * n), low_grad] + [shape(n, wide)] * 4,
+        [pltpu.VMEM((n, 4 * n), bf16), *scratch],
         name="block_before",
     )
-    grad1 = swapped(grad1)
-    c1, f2, f3 = lax.optimization_barrier((c1, f2, f3))
+    grad1 = one_back(grad1)
     s2 = over_rows(s0, 2)
     s1 = over_rows(s0, 1)
-    pieces = (c0, c1, c2, p0, n1, n2)
-    rows_f32 = [shape(n, wide), shape(n, wide)]
-    keep, send = call(
-        functools.partial(anchor_kernel, 2), pieces, rows_f32, micros=0.01, name="anchor_grad_across"
-    )
-    keep, f1, s2 = lax.optimization_barrier((keep, f1, s2))
-    (half,) = call(
-        halved_kernel, (keep, over_rows(send, 1)), [low_grad], micros=0.01, name="half_sum"
-    )
+    send3, grad2, f2, f3 = lax.optimization_barrier((send3, grad2, f2, f3))
+    other3 = over_rows(send3, 1)
+    keep2, f1, f2, f3, s2 = lax.optimization_barrier((keep2, f1, f2, f3, s2))
+    (half,) = call(halved_kernel, (keep2, other3), [low_grad], name="half_sum")
     from_y = over_rows(half, 2)
-    grad2, _ = lax.optimization_barrier((grad2, half))
-    (grad2,) = call(
-        passed_kernel, (scal, grad2, grad1), [low_grad], micros=0.01, name="passed_grad"
-    )
-    grad2 = two_on(grad2, -2)
     f3, s3 = over_rows(f3, 1), over_rows(s2, 1)
-    keep, send = call(
-        functools.partial(anchor_kernel, 0), pieces, rows_f32, micros=0.01, name="anchor_grad_own"
-    )
     s1, s3, f3 = lax.optimization_barrier((s1, s3, f3))
     base, anchor_loss = call(
         listed_kernel,
-        (anchors, s0, s1, s2, s3, *tile, keep, over_rows(send, 1), own_grad),
+        (anchors, s0, s1, s2, s3, *tile, keep0, over_rows(send1, 1), own_grad),
         [shape(n, wide), shape(1, n)],
-        micros=0.01,
         name="listed",
     )
     (g0,) = call(
-        gathered_kernel, (scal, base, from_y, grad1, grad2), [low_grad], micros=0.01, name="row_grad"
+        gathered_kernel, (base, from_y, grad1, grad2), [low_grad], name="row_grad"
     )
     g2 = over_rows(g0, 2)
     g1 = over_rows(g0, 1)
@@ -404,7 +385,7 @@
         head_kernel,
         (f0, f1, f2, f3, g0, g1, g2, g3),
         [shape(m, wide, dtype=bf16)],
-        micros=0.01, name="head_grad",
+        name="head_grad",
     )
     parts = lax.all_to_all(part, "blk", split_axis=0, concat_axis=0, tiled=True)
     weight_grad = jnp.sum(parts.reshape(blks, slice_rows, wide).astype(f32), axis=0)

time: 117 us -> 114 us (0.974)
  waiting for transfers between devices: 36.6 us -> 34.9 us
  Pallas kernels: 27.4 us -> 25.7 us
    ppermute x2 -> x1, waiting for transfers between devices: 6.58 us -> 0.01 us  [swapped(): return lax.ppermute(x, ('blk', 'rows'), pairs)]
    ppermute x16, waiting for transfers between devices: 22.3 us -> 26 us  [over_rows(): return lax.ppermute(x, 'rows', [(i, i ^ flip) for i in range(rows_n)])]
    ppermute x0 -> x1, waiting for transfers between devices: none -> 2.43 us  [one_back(): return lax.ppermute(x, ('blk', 'rows'), pairs)]
    pallas_call x10 -> x7, Pallas kernels: 23.4 us -> 21.7 us  [call(): pl.pallas_call(kernel, out_shape=outs, in_specs=[SMEM if x.ndim == 1 else...]
    ppermute x16, starting transfers between devices: 12.2 us -> 10.8 us  [over_rows(): return lax.ppermute(x, 'rows', [(i, i ^ flip) for i in range(rows_n)])]
    ppermute x2, waiting for transfers between devices: 7.68 us -> 6.43 us  [two_on(): return lax.ppermute(x, 'blk', [(b, (b + by) % blks) for b in range(blks)])]
    ppermute x2 -> x1, starting transfers between devices: 2.6 us -> 2.5 us  [swapped(): return lax.ppermute(x, ('blk', 'rows'), pairs)]
  transfers between devices with their start and end apart: 20 -> 20, of which waited for: 10 -> 12; matrix products, arithmetic and copies ran while one was open for 2% -> 2% of each run, Pallas kernels for 18% -> 18%
where the time goes in v6:
time: 114 us
  waiting for transfers between devices  34.9 us (31%)
  blocking collectives  32.9 us (29%)
  Pallas kernels  25.7 us (23%)
  starting transfers between devices  16 us (14%)
  local copies, waits for them, and re-layouts  2.6 us (2%)
    all_to_all x1, blocking collectives, local(): parts = lax.all_to_all(part, 'blk', split_axis=0, concat_axis=0, tiled=True)  32.9 us
    ppermute x16, waiting for transfers between devices, over_rows(): return lax.ppermute(x, 'rows', [(i, i ^ flip) for i in range(rows_n)])  26 us
    pallas_call x7, Pallas kernels, call(): pl.pallas_call(kernel, out_shape=outs, in_specs=[SMEM if x.ndim == 1 else...  21.7 us
    ppermute x16, starting transfers between devices, over_rows(): return lax.ppermute(x, 'rows', [(i, i ^ flip) for i in range(rows_n)])  10.8 us
    ppermute x2, waiting for transfers between devices, two_on(): return lax.ppermute(x, 'blk', [(b, (b + by) % blks) for b in range(blks)])  6.43 us
    pallas_call x1, Pallas kernels, embed(): pl.pallas_call(embed_kernel, grid=(wide // step,), out_shape=shape(n + ME...  4 us
    ppermute x1, starting transfers between devices, swapped(): return lax.ppermute(x, ('blk', 'rows'), pairs)  2.5 us
    ppermute x1, waiting for transfers between devices, one_back(): return lax.ppermute(x, ('blk', 'rows'), pairs)  2.43 us
  transfers between devices with their start and end apart: 20, of which 12 were waited for; matrix products, arithmetic and copies ran while one was open for 2% of the time, Pallas kernels for 18%

profile of v6, /device:TPU:8, one launch (start us, length us, event | category | flops | bytes accessed | tf_op | source)
XLA Modules:
  0.0 113.6 jit_solution(5244527663324754068)
XLA Ops:
  0.6 4.0 %embed.1.p0.own_ref = bf16[272,768]{1,0:T(8,128)(2,1)} custom-call(bf16[256,2048]{1,0:T(8,128)(2,1)} %features_ref.1, bf16[2048,768]{1,0:T(8,128)(2,1)} %weight_ref.1, s32[1,256]{1,0:T(1,128)} %bitcast.22, s32[3,256]{1,0:T(4,128)} %bitcast.21, f32[1,256]{1,0:T(1,128)} %bitcast.23), custom_call_target="tpu_custom_call" | custom-call | flops 1073741824 | bytes 4194304 | tf_op jit(solution)/shard_map/embed/pallas_call | solution.py:75
  4.6 2.2 %collective-permute-start.1 = (bf16[272,768]{1,0:T(8,128)(2,1)}, bf16[272,768]{1,0:T(8,128)(2,1)S(1)}, u32[]{:S(2)}, u32[]{:S(2)}) collective-permute-start(bf16[272,768]{1,0:T(8,128)(2,1)} %embed.1.p0.own_ref), channel_id=1, source_target_pairs={{0,2},{1,3},{2,0},{3,1},{4,6},{5,7},{6,4},{7,5},{8,10},{9,11},{10,... | collective-permute-start | bytes 1253384 | tf_op jit(solution)/shard_map/ppermute | solution.py:298
  7.0 1.3 %copy.12 = bf16[256,2048]{0,1:T(8,128)(2,1)} copy(bf16[256,2048]{1,0:T(8,128)(2,1)S(1)} %copy-done.1) | data formatting | bytes 2097152 | tf_op jit(solution)/shard_map/optimization_barrier | solution.py:324
  8.3 1.3 %dynamic-slice_bitcast_fusion = (bf16[512,256]{1,0:T(8,128)(2,1)S(1)}, bf16[512,256]{1,0:T(8,128)(2,1)S(1)}, bf16[512,256]{1,0:T(8,128)(2,1)S(1)}, bf16[512,256]{1,0:T(8,128)(2,1)S(1)}) fusion(bf16[64,4,8,256]{3,2,1,0:T(8,128)(2,1)} %bitcast.20, s32[]{:T(128)S(6)} %select_n.24, s32[]{:T(128)S(6)} %select_n.23, s32[]{:T(128)S(6)} %select_n.22, s32[]{:T(128)S(6)} %select_n.21), kind=kLoop, calls=%fused_computation.1 | loop fusion | bytes 2097168 | tf_op jit(solution)/shard_map/reshape | solution.py:328
  9.6 6.6 %collective-permute-done.1.p2 = bf16[272,768]{1,0:T(8,128)(2,1)S(1)} collective-permute-done((bf16[272,768]{1,0:T(8,128)(2,1)}, bf16[272,768]{1,0:T(8,128)(2,1)S(1)}, u32[]{:S(2)}, u32[]{:S(2)}) %collective-permute-start.1) | collective-permute-done | bytes 417824 | tf_op jit(solution)/shard_map/ppermute | solution.py:298
  16.3 6.4 %collective-permute-done.3.n2.other_ref = bf16[272,768]{1,0:T(8,128)(2,1)S(1)} collective-permute-done((bf16[272,768]{1,0:T(8,128)(2,1)}, bf16[272,768]{1,0:T(8,128)(2,1)S(1)}, u32[]{:S(2)}, u32[]{:S(2)}) %collective-permute-start.3) | collective-permute-done | bytes 417824 | tf_op jit(solution)/shard_map/ppermute | solution.py:301
  22.7 0.6 row_choice.1
  23.3 2.5 %collective-permute-start.4 = (bf16[272,768]{1,0:T(8,128)(2,1)S(1)}, bf16[272,768]{1,0:T(8,128)(2,1)S(1)}, u32[]{:S(2)}, u32[]{:S(2)}) collective-permute-start(bf16[272,768]{1,0:T(8,128)(2,1)S(1)} %row_choice.1), channel_id=1, source_target_pairs={{0,6},{1,7},{2,4},{3,5},{4,2},{5,3},{6,0},{7,1},{8,14},{9,15},{10,... | collective-permute-start | bytes 1253384 | tf_op jit(solution)/shard_map/ppermute | solution.py:307
  25.8 11.6 %own_and_two_before.1 = (f32[8,1024]{1,0:T(8,128)S(1)}, bf16[256,1024]{1,0:T(8,128)(2,1)S(1)}, bf16[256,1024]{1,0:T(8,128)(2,1)S(1)}, f32[8,1024]{1,0:T(8,128)S(...) custom-call(s32[5]{0:T(128)S(1)} %pad_add_fusion.scal_ref, bf16[272,768]{1,0:T(8,128)(2,1)S(1)} %copy-done, ...), custom_call_target="tpu_custom_call" | custom-call | flops 1048576 | bytes 1024 | tf_op jit(solution)/shard_map/own_and_two_before/pallas_call | solution.py:25
  37.5 1.8 %collective-permute-start.7 = (bf16[256,768]{1,0:T(8,128)(2,1)S(1)}, bf16[256,768]{1,0:T(8,128)(2,1)S(1)}, u32[]{:S(2)}, u32[]{:S(2)}) collective-permute-start(bf16[256,768]{1,0:T(8,128)(2,1)S(1)} %get-tuple-element.43), channel_id=1, source_target_pairs={{0,248},{4,252},{8,0},{12,4},{16,8},{20,12},{24,16},{28,20},{32,24... | collective-permute-start | bytes 1179656 | tf_op jit(solution)/shard_map/ppermute | solution.py:301
  39.3 1.3 %collective-permute-start.8 = (bf16[512,256]{1,0:T(8,128)(2,1)S(1)}, bf16[512,256]{1,0:T(8,128)(2,1)S(1)}, u32[]{:S(2)}, u32[]{:S(2)}) collective-permute-start(bf16[512,256]{1,0:T(8,128)(2,1)S(1)} %get-tuple-element.44), channel_id=1, source_target_pairs={{0,2},{1,3},{2,0},{3,1},{4,6},{5,7},{6,4},{7,5},{8,10},{9,11},{10,... | collective-permute-start | bytes 786440 | tf_op jit(solution)/shard_map/ppermute | solution.py:298
  40.6 0.7 collective-permute-start.9
  41.3 6.4 %block_before.1 = (f32[8,1024]{1,0:T(8,128)S(1)}, bf16[256,768]{1,0:T(8,128)(2,1)S(1)}, f32[256,768]{1,0:T(8,128)S(1)}, f32[256,768]{1,0:T(8,128)S(1)}, f32[256,768]{1,0:T(8,128)S(1)}, /*index=5*/f32[256,768]{1,0:T(8,128)S(1)}) custom-call(s32[5]{0:T(128)S(1)} %pad_add_fusion.scal_ref, bf16[272,768]{1,0:T(8,128)(2,1)S(1)} %collective-permute-done.4.n1, ...), custom_call_target="tpu_custom_call" | custom-call | flops 1048576 | bytes 1024 | tf_op jit(solution)/shard_map/block_before/pallas_call | solution.py:25
  47.7 0.8 collective-permute-done.8.f2
  48.5 3.8 %collective-permute-done.9 = bf16[512,256]{1,0:T(8,128)(2,1)S(1)} collective-permute-done((bf16[512,256]{1,0:T(8,128)(2,1)S(1)}, bf16[512,256]{1,0:T(8,128)(2,1)S(1)}, u32[]{:S(2)}, u32[]{:S(2)}) %collective-permute-start.9) | collective-permute-done | bytes 262176 | tf_op jit(solution)/shard_map/ppermute | solution.py:298
  52.3 0.5 collective-permute-start.13
  52.8 1.7 %collective-permute-start.10 = (f32[8,1024]{1,0:T(8,128)S(1)}, f32[8,1024]{1,0:T(8,128)S(1)}, u32[]{:S(2)}, u32[]{:S(2)}) collective-permute-start(f32[8,1024]{1,0:T(8,128)S(1)} %get-tuple-element.39.s0), channel_id=1, source_target_pairs={{0,2},{1,3},{2,0},{3,1},{4,6},{5,7},{6,4},{7,5},{8,10},{9,11},{10,... | collective-permute-start | bytes 98312 | tf_op jit(solution)/shard_map/ppermute | solution.py:298
  54.5 0.7 collective-permute-start.16
  55.2 0.8 collective-permute-done.6.f1
  56.0 0.6 collective-permute-done.10.s2
  56.8 1.8 %collective-permute-start.15 = (bf16[256,768]{1,0:T(8,128)(2,1)S(1)}, bf16[256,768]{1,0:T(8,128)(2,1)S(1)}, u32[]{:S(2)}, u32[]{:S(2)}) collective-permute-start(bf16[256,768]{1,0:T(8,128)(2,1)S(1)} %half_sum.1), channel_id=1, source_target_pairs={{0,2},{1,3},{2,0},{3,1},{4,6},{5,7},{6,4},{7,5},{8,10},{9,11},{10,... | collective-permute-start | bytes 1179656 | tf_op jit(solution)/shard_map/ppermute | solution.py:298
  59.1 1.1 collective-permute-done.5.s1
  60.3 1.1 collective-permute-done.11.s3
  61.4 1.9 %listed.1 = (f32[256,768]{1,0:T(8,128)S(1)}, f32[1,256]{1,0:T(1,128)}) custom-call(f32[8,1024]{1,0:T(8,128)S(1)} %get-tuple-element.35.anchors_ref, f32[8,1024]{1,0:T(8,128)S(1)} %get-tuple-element.39.s0, f32[8,1024]{1,0:T(8,128)S(1)} %collective-permute-done.5.s1, f32[8,1024]{1,0:T(8,128)S(1)} %collective-permute-done.10.s2, ...), custom_call_target="tpu_custom_call" | custom-call | flops 1048576 | bytes 1024 | tf_op jit(solution)/shard_map/listed/pallas_call | solution.py:25
  63.3 2.4 %collective-permute-done.16.one_ref = bf16[256,768]{1,0:T(8,128)(2,1)S(1)} collective-permute-done((bf16[256,768]{1,0:T(8,128)(2,1)S(1)}, bf16[256,768]{1,0:T(8,128)(2,1)S(1)}, u32[]{:S(2)}, u32[]{:S(2)}) %collective-permute-start.16) | collective-permute-done | bytes 393248 | tf_op jit(solution)/shard_map/ppermute | solution.py:315
  65.8 1.6 %collective-permute-done.15.y_ref = bf16[256,768]{1,0:T(8,128)(2,1)S(1)} collective-permute-done((bf16[256,768]{1,0:T(8,128)(2,1)S(1)}, bf16[256,768]{1,0:T(8,128)(2,1)S(1)}, u32[]{:S(2)}, u32[]{:S(2)}) %collective-permute-start.15) | collective-permute-done | bytes 393248 | tf_op jit(solution)/shard_map/ppermute | solution.py:298
  67.5 1.8 %collective-permute-start.18 = (bf16[256,768]{1,0:T(8,128)(2,1)S(1)}, bf16[256,768]{1,0:T(8,128)(2,1)S(1)}, u32[]{:S(2)}, u32[]{:S(2)}) collective-permute-start(bf16[256,768]{1,0:T(8,128)(2,1)S(1)} %row_grad.1.g0), channel_id=1, source_target_pairs={{0,2},{1,3},{2,0},{3,1},{4,6},{5,7},{6,4},{7,5},{8,10},{9,11},{10,... | collective-permute-start | bytes 1179656 | tf_op jit(solution)/shard_map/ppermute | solution.py:298
  69.4 7.8 %collective-permute-done.18.g2 = bf16[256,768]{1,0:T(8,128)(2,1)S(1)} collective-permute-done((bf16[256,768]{1,0:T(8,128)(2,1)S(1)}, bf16[256,768]{1,0:T(8,128)(2,1)S(1)}, u32[]{:S(2)}, u32[]{:S(2)}) %collective-permute-start.18) | collective-permute-done | bytes 393248 | tf_op jit(solution)/shard_map/ppermute | solution.py:298
  77.2 1.7 %collective-permute-done.19.g3 = bf16[256,768]{1,0:T(8,128)(2,1)S(1)} collective-permute-done((bf16[256,768]{1,0:T(8,128)(2,1)S(1)}, bf16[256,768]{1,0:T(8,128)(2,1)S(1)}, u32[]{:S(2)}, u32[]{:S(2)}) %collective-permute-start.19) | collective-permute-done | bytes 393248 | tf_op jit(solution)/shard_map/ppermute | solution.py:298
  78.9 1.0 head_grad.1
  79.9 32.9 %all_to_all.9 = bf16[64,8,768]{2,1,0:T(8,128)(2,1)S(1)} all-to-all(bf16[64,8,768]{2,1,0:T(8,128)(2,1)S(1)} %bitcast.19), channel_id=1, replica_groups=mesh['blk'=64,'rows'=4] {'blk'}, dimensions={0} | all-to-all | bytes 1572864 | tf_op jit(solution)/shard_map/all_to_all | solution.py:390
  112.8 0.7 convert_reduce_fusion
  (27 shorter events, 1.2 us)
Async XLA Ops:
  0.6 6.4 %copy-start.1 = (bf16[256,2048]{1,0:T(8,128)(2,1)S(1)}, bf16[256,2048]{1,0:T(8,128)(2,1)}, u32[]{:S(2)}) copy-start(bf16[256,2048]{1,0:T(8,128)(2,1)} %features_ref.1) | copy-start | bytes 3145732
  4.6 11.6 %copy-start.2 = (s32[1,3]{1,0:T(1,128)S(1)}, s32[1,3]{1,0:T(1,128)}, u32[]{:S(2)}) copy-start(s32[1,3]{1,0:T(1,128)} %param.10) | copy-start | bytes 40
  4.6 18.1 %copy-start = (bf16[272,768]{1,0:T(8,128)(2,1)S(1)}, bf16[272,768]{1,0:T(8,128)(2,1)}, u32[]{:S(2)}) copy-start(bf16[272,768]{1,0:T(8,128)(2,1)} %embed.1.p0.own_ref) | copy-start | bytes 1253380
  4.6 11.6 %collective-permute-start.1 = (bf16[272,768]{1,0:T(8,128)(2,1)}, bf16[272,768]{1,0:T(8,128)(2,1)S(1)}, u32[]{:S(2)}, u32[]{:S(2)}) collective-permute-start(bf16[272,768]{1,0:T(8,128)(2,1)} %embed.1.p0.own_ref), channel_id=1, source_target_pairs={{0,2},{1,3},{2,0},{3,1},{4,6},{5,7},{6,4},{7,5},{8,10},{9,11},{10,... | collective-permute-start | bytes 1253384 | tf_op jit(solution)/shard_map/ppermute | solution.py:298
  6.8 15.9 %collective-permute-start.3 = (bf16[272,768]{1,0:T(8,128)(2,1)}, bf16[272,768]{1,0:T(8,128)(2,1)S(1)}, u32[]{:S(2)}, u32[]{:S(2)}) collective-permute-start(bf16[272,768]{1,0:T(8,128)(2,1)} %embed.1.p0.own_ref), channel_id=1, source_target_pairs={{0,8},{4,12},{8,16},{12,20},{16,24},{20,28},{24,32},{28,36},{32,40... | collective-permute-start | bytes 1253384 | tf_op jit(solution)/shard_map/ppermute | solution.py:301
  7.0 18.8 %collective-permute-start = (bf16[272,768]{1,0:T(8,128)(2,1)}, bf16[272,768]{1,0:T(8,128)(2,1)S(1)}, u32[]{:S(2)}, u32[]{:S(2)}) collective-permute-start(bf16[272,768]{1,0:T(8,128)(2,1)} %embed.1.p0.own_ref), channel_id=1, source_target_pairs={{0,1},{1,0},{2,3},{3,2},{4,5},{5,4},{6,7},{7,6},{8,9},{9,8},{10,11... | collective-permute-start | bytes 1253384 | tf_op jit(solution)/shard_map/ppermute | solution.py:298
  16.2 9.6 %collective-permute-start.2 = (bf16[272,768]{1,0:T(8,128)(2,1)S(1)}, bf16[272,768]{1,0:T(8,128)(2,1)S(1)}, u32[]{:S(2)}, u32[]{:S(2)}) collective-permute-start(bf16[272,768]{1,0:T(8,128)(2,1)S(1)} %collective-permute-done.1.p2), channel_id=1, source_target_pairs={{0,1},{1,0},{2,3},{3,2},{4,5},{5,4},{6,7},{7,6},{8,9},{9,8},{10,11... | collective-permute-start | bytes 1253384 | tf_op jit(solution)/shard_map/ppermute | solution.py:298
  23.3 17.9 %collective-permute-start.4 = (bf16[272,768]{1,0:T(8,128)(2,1)S(1)}, bf16[272,768]{1,0:T(8,128)(2,1)S(1)}, u32[]{:S(2)}, u32[]{:S(2)}) collective-permute-start(bf16[272,768]{1,0:T(8,128)(2,1)S(1)} %row_choice.1), channel_id=1, source_target_pairs={{0,6},{1,7},{2,4},{3,5},{4,2},{5,3},{6,0},{7,1},{8,14},{9,15},{10,... | collective-permute-start | bytes 1253384 | tf_op jit(solution)/shard_map/ppermute | solution.py:307
  37.5 14.8 %collective-permute-start.7 = (bf16[256,768]{1,0:T(8,128)(2,1)S(1)}, bf16[256,768]{1,0:T(8,128)(2,1)S(1)}, u32[]{:S(2)}, u32[]{:S(2)}) collective-permute-start(bf16[256,768]{1,0:T(8,128)(2,1)S(1)} %get-tuple-element.43), channel_id=1, source_target_pairs={{0,248},{4,252},{8,0},{12,4},{16,8},{20,12},{24,16},{28,20},{32,24... | collective-permute-start | bytes 1179656 | tf_op jit(solution)/shard_map/ppermute | solution.py:301
  39.3 9.2 %collective-permute-start.8 = (bf16[512,256]{1,0:T(8,128)(2,1)S(1)}, bf16[512,256]{1,0:T(8,128)(2,1)S(1)}, u32[]{:S(2)}, u32[]{:S(2)}) collective-permute-start(bf16[512,256]{1,0:T(8,128)(2,1)S(1)} %get-tuple-element.44), channel_id=1, source_target_pairs={{0,2},{1,3},{2,0},{3,1},{4,6},{5,7},{6,4},{7,5},{8,10},{9,11},{10,... | collective-permute-start | bytes 786440 | tf_op jit(solution)/shard_map/ppermute | solution.py:298
  40.6 11.7 %collective-permute-start.9 = (bf16[512,256]{1,0:T(8,128)(2,1)S(1)}, bf16[512,256]{1,0:T(8,128)(2,1)S(1)}, u32[]{:S(2)}, u32[]{:S(2)}) collective-permute-start(bf16[512,256]{1,0:T(8,128)(2,1)S(1)} %get-tuple-element.45), channel_id=1, source_target_pairs={{0,2},{1,3},{2,0},{3,1},{4,6},{5,7},{6,4},{7,5},{8,10},{9,11},{10,... | collective-permute-start | bytes 786440 | tf_op jit(solution)/shard_map/ppermute | solution.py:298
  52.3 4.4 %collective-permute-start.14 = (f32[256,768]{1,0:T(8,128)S(1)}, f32[256,768]{1,0:T(8,128)S(1)}, u32[]{:S(2)}, u32[]{:S(2)}) collective-permute-start(f32[256,768]{1,0:T(8,128)S(1)} %get-tuple-element.61), channel_id=1, source_target_pairs={{0,1},{1,0},{2,3},{3,2},{4,5},{5,4},{6,7},{7,6},{8,9},{9,8},{10,11... | collective-permute-start | bytes 2359304 | tf_op jit(solution)/shard_map/ppermute | solution.py:298
  52.3 9.1 %collective-permute-start.13 = (f32[256,768]{1,0:T(8,128)S(1)}, f32[256,768]{1,0:T(8,128)S(1)}, u32[]{:S(2)}, u32[]{:S(2)}) collective-permute-start(f32[256,768]{1,0:T(8,128)S(1)} %get-tuple-element.53), channel_id=1, source_target_pairs={{0,1},{1,0},{2,3},{3,2},{4,5},{5,4},{6,7},{7,6},{8,9},{9,8},{10,11... | collective-permute-start | bytes 2359304 | tf_op jit(solution)/shard_map/ppermute | solution.py:298
  52.8 3.3 %collective-permute-start.6 = (bf16[512,256]{1,0:T(8,128)(2,1)S(1)}, bf16[512,256]{1,0:T(8,128)(2,1)S(1)}, u32[]{:S(2)}, u32[]{:S(2)}) collective-permute-start(bf16[512,256]{1,0:T(8,128)(2,1)S(1)} %get-tuple-element.41), channel_id=1, source_target_pairs={{0,1},{1,0},{2,3},{3,2},{4,5},{5,4},{6,7},{7,6},{8,9},{9,8},{10,11... | collective-permute-start | bytes 786440 | tf_op jit(solution)/shard_map/ppermute | solution.py:298
  52.8 3.9 %collective-permute-start.10 = (f32[8,1024]{1,0:T(8,128)S(1)}, f32[8,1024]{1,0:T(8,128)S(1)}, u32[]{:S(2)}, u32[]{:S(2)}) collective-permute-start(f32[8,1024]{1,0:T(8,128)S(1)} %get-tuple-element.39.s0), channel_id=1, source_target_pairs={{0,2},{1,3},{2,0},{3,1},{4,6},{5,7},{6,4},{7,5},{8,10},{9,11},{10,... | collective-permute-start | bytes 98312 | tf_op jit(solution)/shard_map/ppermute | solution.py:298
  54.5 11.2 %collective-permute-start.16 = (bf16[256,768]{1,0:T(8,128)(2,1)S(1)}, bf16[256,768]{1,0:T(8,128)(2,1)S(1)}, u32[]{:S(2)}, u32[]{:S(2)}) collective-permute-start(bf16[256,768]{1,0:T(8,128)(2,1)S(1)} %get-tuple-element.62), channel_id=1, source_target_pairs={{0,254},{1,255},{2,252},{3,253},{4,2},{5,3},{6,0},{7,1},{8,6},{9,7... | collective-permute-start | bytes 1179656 | tf_op jit(solution)/shard_map/ppermute | solution.py:315
  56.8 10.6 %collective-permute-start.15 = (bf16[256,768]{1,0:T(8,128)(2,1)S(1)}, bf16[256,768]{1,0:T(8,128)(2,1)S(1)}, u32[]{:S(2)}, u32[]{:S(2)}) collective-permute-start(bf16[256,768]{1,0:T(8,128)(2,1)S(1)} %half_sum.1), channel_id=1, source_target_pairs={{0,2},{1,3},{2,0},{3,1},{4,6},{5,7},{6,4},{7,5},{8,10},{9,11},{10,... | collective-permute-start | bytes 1179656 | tf_op jit(solution)/shard_map/ppermute | solution.py:298
  58.6 2.8 %collective-permute-start.12 = (bf16[512,256]{1,0:T(8,128)(2,1)S(1)}, bf16[512,256]{1,0:T(8,128)(2,1)S(1)}, u32[]{:S(2)}, u32[]{:S(2)}) collective-permute-start(bf16[512,256]{1,0:T(8,128)(2,1)S(1)} %collective-permute-done.9), channel_id=1, source_target_pairs={{0,1},{1,0},{2,3},{3,2},{4,5},{5,4},{6,7},{7,6},{8,9},{9,8},{10,11... | collective-permute-start | bytes 786440 | tf_op jit(solution)/shard_map/ppermute | solution.py:298
  58.6 1.6 %collective-permute-start.5 = (f32[8,1024]{1,0:T(8,128)S(1)}, f32[8,1024]{1,0:T(8,128)S(1)}, u32[]{:S(2)}, u32[]{:S(2)}) collective-permute-start(f32[8,1024]{1,0:T(8,128)S(1)} %get-tuple-element.39.s0), channel_id=1, source_target_pairs={{0,1},{1,0},{2,3},{3,2},{4,5},{5,4},{6,7},{7,6},{8,9},{9,8},{10,11... | collective-permute-start | bytes 98312 | tf_op jit(solution)/shard_map/ppermute | solution.py:298
  60.2 1.2 %collective-permute-start.11 = (f32[8,1024]{1,0:T(8,128)S(1)}, f32[8,1024]{1,0:T(8,128)S(1)}, u32[]{:S(2)}, u32[]{:S(2)}) collective-permute-start(f32[8,1024]{1,0:T(8,128)S(1)} %collective-permute-done.10.s2), channel_id=1, source_target_pairs={{0,1},{1,0},{2,3},{3,2},{4,5},{5,4},{6,7},{7,6},{8,9},{9,8},{10,11... | collective-permute-start | bytes 98312 | tf_op jit(solution)/shard_map/ppermute | solution.py:298
  67.5 9.7 %collective-permute-start.18 = (bf16[256,768]{1,0:T(8,128)(2,1)S(1)}, bf16[256,768]{1,0:T(8,128)(2,1)S(1)}, u32[]{:S(2)}, u32[]{:S(2)}) collective-permute-start(bf16[256,768]{1,0:T(8,128)(2,1)S(1)} %row_grad.1.g0), channel_id=1, source_target_pairs={{0,2},{1,3},{2,0},{3,1},{4,6},{5,7},{6,4},{7,5},{8,10},{9,11},{10,... | collective-permute-start | bytes 1179656 | tf_op jit(solution)/shard_map/ppermute | solution.py:298
  69.4 7.9 %collective-permute-start.17 = (bf16[256,768]{1,0:T(8,128)(2,1)S(1)}, bf16[256,768]{1,0:T(8,128)(2,1)S(1)}, u32[]{:S(2)}, u32[]{:S(2)}) collective-permute-start(bf16[256,768]{1,0:T(8,128)(2,1)S(1)} %row_grad.1.g0), channel_id=1, source_target_pairs={{0,1},{1,0},{2,3},{3,2},{4,5},{5,4},{6,7},{7,6},{8,9},{9,8},{10,11... | collective-permute-start | bytes 1179656 | tf_op jit(solution)/shard_map/ppermute | solution.py:298
  77.2 1.7 %collective-permute-start.19 = (bf16[256,768]{1,0:T(8,128)(2,1)S(1)}, bf16[256,768]{1,0:T(8,128)(2,1)S(1)}, u32[]{:S(2)}, u32[]{:S(2)}) collective-permute-start(bf16[256,768]{1,0:T(8,128)(2,1)S(1)} %collective-permute-done.18.g2), channel_id=1, source_target_pairs={{0,1},{1,0},{2,3},{3,2},{4,5},{5,4},{6,7},{7,6},{8,9},{9,8},{10,11... | collective-permute-start | bytes 1179656 | tf_op jit(solution)/shard_map/ppermute | solution.py:298

commit v7 on v6

--- a/solution.py
+++ b/solution.py
@@ -351,6 +351,7 @@
         scratch,
         name="own_and_two_before",
     )
+    grad2, f1, f2, f3 = lax.optimization_barrier((grad2, f1, f2, f3))
     grad2 = two_on(grad2, -2)
     s0, grad1, keep0, send1, keep2, send3 = call(
         last_kernel,
@@ -362,9 +363,9 @@
     grad1 = one_back(grad1)
     s2 = over_rows(s0, 2)
     s1 = over_rows(s0, 1)
-    send3, grad2, f2, f3 = lax.optimization_barrier((send3, grad2, f2, f3))
+    send3, grad2 = lax.optimization_barrier((send3, grad2))
     other3 = over_rows(send3, 1)
-    keep2, f1, f2, f3, s2 = lax.optimization_barrier((keep2, f1, f2, f3, s2))
+    keep2, s2 = lax.optimization_barrier((keep2, s2))
     (half,) = call(halved_kernel, (keep2, other3), [low_grad], name="half_sum")
     from_y = over_rows(half, 2)
     f3, s3 = over_rows(f3, 1), over_rows(s2, 1)

time: 114 us -> 114 us (level)
  waiting for transfers between devices: 34.9 us -> 28.9 us
  starting transfers between devices: 16 us -> 20.5 us
    ppermute x16, waiting for transfers between devices: 26 us -> 19.8 us  [over_rows(): return lax.ppermute(x, 'rows', [(i, i ^ flip) for i in range(rows_n)])]
    ppermute x1, starting transfers between devices: 0.73 us -> 4.94 us  [one_back(): return lax.ppermute(x, ('blk', 'rows'), pairs)]
  transfers between devices with their start and end apart: 20 -> 20, of which waited for: 12 -> 9; matrix products, arithmetic and copies ran while one was open for 2% -> 3% of each run, Pallas kernels for 18% -> 18%
where the time goes in v7:
time: 114 us
  blocking collectives  33.5 us (29%)
  waiting for transfers between devices  28.9 us (25%)
  Pallas kernels  25.8 us (23%)
  starting transfers between devices  20.5 us (18%)
  local copies, waits for them, and re-layouts  3.29 us (3%)
    all_to_all x1, blocking collectives, local(): parts = lax.all_to_all(part, 'blk', split_axis=0, concat_axis=0, tiled=True)  33.5 us
    pallas_call x7, Pallas kernels, call(): pl.pallas_call(kernel, out_shape=outs, in_specs=[SMEM if x.ndim == 1 else...  21.8 us
    ppermute x16, waiting for transfers between devices, over_rows(): return lax.ppermute(x, 'rows', [(i, i ^ flip) for i in range(rows_n)])  19.8 us
    ppermute x16, starting transfers between devices, over_rows(): return lax.ppermute(x, 'rows', [(i, i ^ flip) for i in range(rows_n)])  11 us
    ppermute x2, waiting for transfers between devices, two_on(): return lax.ppermute(x, 'blk', [(b, (b + by) % blks) for b in range(blks)])  6.97 us
    ppermute x1, starting transfers between devices, one_back(): return lax.ppermute(x, ('blk', 'rows'), pairs)  4.94 us
    pallas_call x1, Pallas kernels, embed(): pl.pallas_call(embed_kernel, grid=(wide // step,), out_shape=shape(n + ME...  4 us
    ppermute x2, starting transfers between devices, two_on(): return lax.ppermute(x, 'blk', [(b, (b + by) % blks) for b in range(blks)])  2.94 us
  transfers between devices with their start and end apart: 20, of which 9 were waited for; matrix products, arithmetic and copies ran while one was open for 3% of the time, Pallas kernels for 18%

profile of v7, /device:TPU:8, one launch (start us, length us, event | category | flops | bytes accessed | tf_op | source)
XLA Modules:
  0.0 113.5 jit_solution(11935605290955235560)
XLA Ops:
  0.6 4.0 %embed.1.p0.own_ref = bf16[272,768]{1,0:T(8,128)(2,1)} custom-call(bf16[256,2048]{1,0:T(8,128)(2,1)} %features_ref.1, bf16[2048,768]{1,0:T(8,128)(2,1)} %weight_ref.1, s32[1,256]{1,0:T(1,128)} %bitcast.22, s32[3,256]{1,0:T(4,128)} %bitcast.21, f32[1,256]{1,0:T(1,128)} %bitcast.23), custom_call_target="tpu_custom_call" | custom-call | flops 1073741824 | bytes 4194304 | tf_op jit(solution)/shard_map/embed/pallas_call | solution.py:75
  4.6 2.2 %collective-permute-start.1 = (bf16[272,768]{1,0:T(8,128)(2,1)}, bf16[272,768]{1,0:T(8,128)(2,1)S(1)}, u32[]{:S(2)}, u32[]{:S(2)}) collective-permute-start(bf16[272,768]{1,0:T(8,128)(2,1)} %embed.1.p0.own_ref), channel_id=1, source_target_pairs={{0,2},{1,3},{2,0},{3,1},{4,6},{5,7},{6,4},{7,5},{8,10},{9,11},{10,... | collective-permute-start | bytes 1253384 | tf_op jit(solution)/shard_map/ppermute | solution.py:298
  7.0 1.3 %copy.12 = bf16[256,2048]{0,1:T(8,128)(2,1)} copy(bf16[256,2048]{1,0:T(8,128)(2,1)S(1)} %copy-done.1) | data formatting | bytes 2097152 | tf_op jit(solution)/shard_map/optimization_barrier | solution.py:324
  8.3 2.0 %dynamic-slice_bitcast_fusion = (bf16[512,256]{1,0:T(8,128)(2,1)S(1)}, bf16[512,256]{1,0:T(8,128)(2,1)S(1)}, bf16[512,256]{1,0:T(8,128)(2,1)}, bf16[512,256]{1,0:T(8,128)(2,1)S(1)}) fusion(bf16[64,4,8,256]{3,2,1,0:T(8,128)(2,1)} %bitcast.20, s32[]{:T(128)S(6)} %select_n.24, s32[]{:T(128)S(6)} %select_n.23, s32[]{:T(128)S(6)} %select_n.22, s32[]{:T(128)S(6)} %select_n.21), kind=kLoop, calls=%fused_computation.1 | loop fusion | bytes 2097168 | tf_op jit(solution)/shard_map/reshape | solution.py:328
  10.3 5.9 %collective-permute-done.1.p2 = bf16[272,768]{1,0:T(8,128)(2,1)S(1)} collective-permute-done((bf16[272,768]{1,0:T(8,128)(2,1)}, bf16[272,768]{1,0:T(8,128)(2,1)S(1)}, u32[]{:S(2)}, u32[]{:S(2)}) %collective-permute-start.1) | collective-permute-done | bytes 417824 | tf_op jit(solution)/shard_map/ppermute | solution.py:298
  16.2 0.5 collective-permute-start.8
  16.7 0.3 collective-permute-start.9
  17.1 5.7 %collective-permute-done.3.n2.other_ref = bf16[272,768]{1,0:T(8,128)(2,1)S(1)} collective-permute-done((bf16[272,768]{1,0:T(8,128)(2,1)}, bf16[272,768]{1,0:T(8,128)(2,1)S(1)}, u32[]{:S(2)}, u32[]{:S(2)}) %collective-permute-start.3) | collective-permute-done | bytes 417824 | tf_op jit(solution)/shard_map/ppermute | solution.py:301
  22.7 1.6 %collective-permute-start.10 = (bf16[512,256]{1,0:T(8,128)(2,1)S(1)}, bf16[512,256]{1,0:T(8,128)(2,1)}, u32[]{:S(2)}, u32[]{:S(2)}) collective-permute-start(bf16[512,256]{1,0:T(8,128)(2,1)S(1)} %get-tuple-element.44), channel_id=1, source_target_pairs={{0,2},{1,3},{2,0},{3,1},{4,6},{5,7},{6,4},{7,5},{8,10},{9,11},{10,... | collective-permute-start | bytes 786440 | tf_op jit(solution)/shard_map/ppermute | solution.py:298
  24.4 0.6 row_choice.1
  25.0 1.7 %collective-permute-start.4 = (bf16[272,768]{1,0:T(8,128)(2,1)S(1)}, bf16[272,768]{1,0:T(8,128)(2,1)S(1)}, u32[]{:S(2)}, u32[]{:S(2)}) collective-permute-start(bf16[272,768]{1,0:T(8,128)(2,1)S(1)} %row_choice.1), channel_id=1, source_target_pairs={{0,6},{1,7},{2,4},{3,5},{4,2},{5,3},{6,0},{7,1},{8,14},{9,15},{10,... | collective-permute-start | bytes 1253384 | tf_op jit(solution)/shard_map/ppermute | solution.py:307
  26.7 11.6 %own_and_two_before.1 = (f32[8,1024]{1,0:T(8,128)S(1)}, bf16[256,1024]{1,0:T(8,128)(2,1)S(1)}, bf16[256,1024]{1,0:T(8,128)(2,1)S(1)}, f32[8,1024]{1,0:T(8,128)S(...) custom-call(s32[5]{0:T(128)S(1)} %pad_add_fusion.scal_ref, bf16[272,768]{1,0:T(8,128)(2,1)S(1)} %copy-done, ...), custom_call_target="tpu_custom_call" | custom-call | flops 1048576 | bytes 1024 | tf_op jit(solution)/shard_map/own_and_two_before/pallas_call | solution.py:25
  38.3 2.8 %collective-permute-start.13 = (bf16[256,768]{1,0:T(8,128)(2,1)S(1)}, bf16[256,768]{1,0:T(8,128)(2,1)S(1)}, u32[]{:S(2)}, u32[]{:S(2)}) collective-permute-start(bf16[256,768]{1,0:T(8,128)(2,1)S(1)} %get-tuple-element.58), channel_id=1, source_target_pairs={{0,248},{4,252},{8,0},{12,4},{16,8},{20,12},{24,16},{28,20},{32,24... | collective-permute-start | bytes 1179656 | tf_op jit(solution)/shard_map/ppermute | solution.py:301
  41.1 6.4 %block_before.1 = (f32[8,1024]{1,0:T(8,128)S(1)}, bf16[256,768]{1,0:T(8,128)(2,1)S(1)}, f32[256,768]{1,0:T(8,128)S(1)}, f32[256,768]{1,0:T(8,128)S(1)}, f32[256,768]{1,0:T(8,128)S(1)}, /*index=5*/f32[256,768]{1,0:T(8,128)S(1)}) custom-call(s32[5]{0:T(128)S(1)} %pad_add_fusion.scal_ref, bf16[272,768]{1,0:T(8,128)(2,1)S(1)} %collective-permute-done.4.n1, ...), custom_call_target="tpu_custom_call" | custom-call | flops 1048576 | bytes 1024 | tf_op jit(solution)/shard_map/block_before/pallas_call | solution.py:25
  47.5 1.3 %collective-permute-done.13.two_ref = bf16[256,768]{1,0:T(8,128)(2,1)S(1)} collective-permute-done((bf16[256,768]{1,0:T(8,128)(2,1)S(1)}, bf16[256,768]{1,0:T(8,128)(2,1)S(1)}, u32[]{:S(2)}, u32[]{:S(2)}) %collective-permute-start.13) | collective-permute-done | bytes 393248 | tf_op jit(solution)/shard_map/ppermute | solution.py:301
  48.8 0.5 collective-permute-start.12
  49.3 1.9 %collective-permute-start.6 = (f32[8,1024]{1,0:T(8,128)S(1)}, f32[8,1024]{1,0:T(8,128)S(1)}, u32[]{:S(2)}, u32[]{:S(2)}) collective-permute-start(f32[8,1024]{1,0:T(8,128)S(1)} %get-tuple-element.38.s0), channel_id=1, source_target_pairs={{0,2},{1,3},{2,0},{3,1},{4,6},{5,7},{6,4},{7,5},{8,10},{9,11},{10,... | collective-permute-start | bytes 98312 | tf_op jit(solution)/shard_map/ppermute | solution.py:298
  51.2 4.9 %collective-permute-start.16 = (bf16[256,768]{1,0:T(8,128)(2,1)S(1)}, bf16[256,768]{1,0:T(8,128)(2,1)S(1)}, u32[]{:S(2)}, u32[]{:S(2)}) collective-permute-start(bf16[256,768]{1,0:T(8,128)(2,1)S(1)} %get-tuple-element.60), channel_id=1, source_target_pairs={{0,254},{1,255},{2,252},{3,253},{4,2},{5,3},{6,0},{7,1},{8,6},{9,7... | collective-permute-start | bytes 1179656 | tf_op jit(solution)/shard_map/ppermute | solution.py:315
  56.2 1.6 %collective-permute-start.15 = (bf16[256,768]{1,0:T(8,128)(2,1)S(1)}, bf16[256,768]{1,0:T(8,128)(2,1)S(1)}, u32[]{:S(2)}, u32[]{:S(2)}) collective-permute-start(bf16[256,768]{1,0:T(8,128)(2,1)S(1)} %half_sum.1), channel_id=1, source_target_pairs={{0,2},{1,3},{2,0},{3,1},{4,6},{5,7},{6,4},{7,5},{8,10},{9,11},{10,... | collective-permute-start | bytes 1179656 | tf_op jit(solution)/shard_map/ppermute | solution.py:298
  57.8 0.5 collective-permute-start.5
  58.3 0.9 collective-permute-done.5.s1
  59.1 0.3 collective-permute-start.7
  59.5 0.9 collective-permute-done.7.s3
  60.4 1.9 %listed.1 = (f32[256,768]{1,0:T(8,128)S(1)}, f32[1,256]{1,0:T(1,128)}) custom-call(f32[8,1024]{1,0:T(8,128)S(1)} %get-tuple-element.34.anchors_ref, f32[8,1024]{1,0:T(8,128)S(1)} %get-tuple-element.38.s0, f32[8,1024]{1,0:T(8,128)S(1)} %collective-permute-done.5.s1, f32[8,1024]{1,0:T(8,128)S(1)} %collective-permute-done.6.s2, ...), custom_call_target="tpu_custom_call" | custom-call | flops 1048576 | bytes 1024 | tf_op jit(solution)/shard_map/listed/pallas_call | solution.py:25
  62.3 2.1 %collective-permute-done.16.one_ref = bf16[256,768]{1,0:T(8,128)(2,1)S(1)} collective-permute-done((bf16[256,768]{1,0:T(8,128)(2,1)S(1)}, bf16[256,768]{1,0:T(8,128)(2,1)S(1)}, u32[]{:S(2)}, u32[]{:S(2)}) %collective-permute-start.16) | collective-permute-done | bytes 393248 | tf_op jit(solution)/shard_map/ppermute | solution.py:315
  64.4 2.4 %collective-permute-done.15.y_ref = bf16[256,768]{1,0:T(8,128)(2,1)S(1)} collective-permute-done((bf16[256,768]{1,0:T(8,128)(2,1)S(1)}, bf16[256,768]{1,0:T(8,128)(2,1)S(1)}, u32[]{:S(2)}, u32[]{:S(2)}) %collective-permute-start.15) | collective-permute-done | bytes 393248 | tf_op jit(solution)/shard_map/ppermute | solution.py:298
  66.9 1.6 %collective-permute-start.18 = (bf16[256,768]{1,0:T(8,128)(2,1)S(1)}, bf16[256,768]{1,0:T(8,128)(2,1)S(1)}, u32[]{:S(2)}, u32[]{:S(2)}) collective-permute-start(bf16[256,768]{1,0:T(8,128)(2,1)S(1)} %row_grad.1.g0), channel_id=1, source_target_pairs={{0,2},{1,3},{2,0},{3,1},{4,6},{5,7},{6,4},{7,5},{8,10},{9,11},{10,... | collective-permute-start | bytes 1179656 | tf_op jit(solution)/shard_map/ppermute | solution.py:298
  68.5 8.0 %collective-permute-done.18.g2 = bf16[256,768]{1,0:T(8,128)(2,1)S(1)} collective-permute-done((bf16[256,768]{1,0:T(8,128)(2,1)S(1)}, bf16[256,768]{1,0:T(8,128)(2,1)S(1)}, u32[]{:S(2)}, u32[]{:S(2)}) %collective-permute-start.18) | collective-permute-done | bytes 393248 | tf_op jit(solution)/shard_map/ppermute | solution.py:298
  76.6 1.7 %collective-permute-done.19.g3 = bf16[256,768]{1,0:T(8,128)(2,1)S(1)} collective-permute-done((bf16[256,768]{1,0:T(8,128)(2,1)S(1)}, bf16[256,768]{1,0:T(8,128)(2,1)S(1)}, u32[]{:S(2)}, u32[]{:S(2)}) %collective-permute-start.19) | collective-permute-done | bytes 393248 | tf_op jit(solution)/shard_map/ppermute | solution.py:298
  78.3 1.0 head_grad.1
  79.3 33.5 %all_to_all.9 = bf16[64,8,768]{2,1,0:T(8,128)(2,1)S(1)} all-to-all(bf16[64,8,768]{2,1,0:T(8,128)(2,1)S(1)} %bitcast.19), channel_id=1, replica_groups=mesh['blk'=64,'rows'=4] {'blk'}, dimensions={0} | all-to-all | bytes 1572864 | tf_op jit(solution)/shard_map/all_to_all | solution.py:391
  112.8 0.7 convert_reduce_fusion
  (27 shorter events, 0.6 us)
Async XLA Ops:
  0.6 6.4 %copy-start.1 = (bf16[256,2048]{1,0:T(8,128)(2,1)S(1)}, bf16[256,2048]{1,0:T(8,128)(2,1)}, u32[]{:S(2)}) copy-start(bf16[256,2048]{1,0:T(8,128)(2,1)} %features_ref.1) | copy-start | bytes 3145732
  4.6 19.7 %copy-start.2 = (s32[1,3]{1,0:T(1,128)S(1)}, s32[1,3]{1,0:T(1,128)}, u32[]{:S(2)}) copy-start(s32[1,3]{1,0:T(1,128)} %param.10) | copy-start | bytes 40
  4.6 19.8 %copy-start = (bf16[272,768]{1,0:T(8,128)(2,1)S(1)}, bf16[272,768]{1,0:T(8,128)(2,1)}, u32[]{:S(2)}) copy-start(bf16[272,768]{1,0:T(8,128)(2,1)} %embed.1.p0.own_ref) | copy-start | bytes 1253380
  4.6 11.6 %collective-permute-start.1 = (bf16[272,768]{1,0:T(8,128)(2,1)}, bf16[272,768]{1,0:T(8,128)(2,1)S(1)}, u32[]{:S(2)}, u32[]{:S(2)}) collective-permute-start(bf16[272,768]{1,0:T(8,128)(2,1)} %embed.1.p0.own_ref), channel_id=1, source_target_pairs={{0,2},{1,3},{2,0},{3,1},{4,6},{5,7},{6,4},{7,5},{8,10},{9,11},{10,... | collective-permute-start | bytes 1253384 | tf_op jit(solution)/shard_map/ppermute | solution.py:298
  6.8 15.9 %collective-permute-start.3 = (bf16[272,768]{1,0:T(8,128)(2,1)}, bf16[272,768]{1,0:T(8,128)(2,1)S(1)}, u32[]{:S(2)}, u32[]{:S(2)}) collective-permute-start(bf16[272,768]{1,0:T(8,128)(2,1)} %embed.1.p0.own_ref), channel_id=1, source_target_pairs={{0,8},{4,12},{8,16},{12,20},{16,24},{20,28},{24,32},{28,36},{32,40... | collective-permute-start | bytes 1253384 | tf_op jit(solution)/shard_map/ppermute | solution.py:301
  7.0 18.0 %collective-permute-start = (bf16[272,768]{1,0:T(8,128)(2,1)}, bf16[272,768]{1,0:T(8,128)(2,1)S(1)}, u32[]{:S(2)}, u32[]{:S(2)}) collective-permute-start(bf16[272,768]{1,0:T(8,128)(2,1)} %embed.1.p0.own_ref), channel_id=1, source_target_pairs={{0,1},{1,0},{2,3},{3,2},{4,5},{5,4},{6,7},{7,6},{8,9},{9,8},{10,11... | collective-permute-start | bytes 1253384 | tf_op jit(solution)/shard_map/ppermute | solution.py:298
  16.2 10.4 %collective-permute-start.2 = (bf16[272,768]{1,0:T(8,128)(2,1)S(1)}, bf16[272,768]{1,0:T(8,128)(2,1)S(1)}, u32[]{:S(2)}, u32[]{:S(2)}) collective-permute-start(bf16[272,768]{1,0:T(8,128)(2,1)S(1)} %collective-permute-done.1.p2), channel_id=1, source_target_pairs={{0,1},{1,0},{2,3},{3,2},{4,5},{5,4},{6,7},{7,6},{8,9},{9,8},{10,11... | collective-permute-start | bytes 1253384 | tf_op jit(solution)/shard_map/ppermute | solution.py:298
  16.2 22.0 %collective-permute-start.8 = (bf16[512,256]{1,0:T(8,128)(2,1)}, bf16[512,256]{1,0:T(8,128)(2,1)S(1)}, u32[]{:S(2)}, u32[]{:S(2)}) collective-permute-start(bf16[512,256]{1,0:T(8,128)(2,1)} %get-tuple-element.42), channel_id=1, source_target_pairs={{0,1},{1,0},{2,3},{3,2},{4,5},{5,4},{6,7},{7,6},{8,9},{9,8},{10,11... | collective-permute-start | bytes 786440 | tf_op jit(solution)/shard_map/ppermute | solution.py:298
  16.7 21.5 %collective-permute-start.9 = (bf16[512,256]{1,0:T(8,128)(2,1)S(1)}, bf16[512,256]{1,0:T(8,128)(2,1)S(1)}, u32[]{:S(2)}, u32[]{:S(2)}) collective-permute-start(bf16[512,256]{1,0:T(8,128)(2,1)S(1)} %get-tuple-element.43), channel_id=1, source_target_pairs={{0,2},{1,3},{2,0},{3,1},{4,6},{5,7},{6,4},{7,5},{8,10},{9,11},{10,... | collective-permute-start | bytes 786440 | tf_op jit(solution)/shard_map/ppermute | solution.py:298
  22.7 15.6 %collective-permute-start.10 = (bf16[512,256]{1,0:T(8,128)(2,1)S(1)}, bf16[512,256]{1,0:T(8,128)(2,1)}, u32[]{:S(2)}, u32[]{:S(2)}) collective-permute-start(bf16[512,256]{1,0:T(8,128)(2,1)S(1)} %get-tuple-element.44), channel_id=1, source_target_pairs={{0,2},{1,3},{2,0},{3,1},{4,6},{5,7},{6,4},{7,5},{8,10},{9,11},{10,... | collective-permute-start | bytes 786440 | tf_op jit(solution)/shard_map/ppermute | solution.py:298
  25.0 16.1 %collective-permute-start.4 = (bf16[272,768]{1,0:T(8,128)(2,1)S(1)}, bf16[272,768]{1,0:T(8,128)(2,1)S(1)}, u32[]{:S(2)}, u32[]{:S(2)}) collective-permute-start(bf16[272,768]{1,0:T(8,128)(2,1)S(1)} %row_choice.1), channel_id=1, source_target_pairs={{0,6},{1,7},{2,4},{3,5},{4,2},{5,3},{6,0},{7,1},{8,14},{9,15},{10,... | collective-permute-start | bytes 1253384 | tf_op jit(solution)/shard_map/ppermute | solution.py:307
  38.3 10.5 %collective-permute-start.13 = (bf16[256,768]{1,0:T(8,128)(2,1)S(1)}, bf16[256,768]{1,0:T(8,128)(2,1)S(1)}, u32[]{:S(2)}, u32[]{:S(2)}) collective-permute-start(bf16[256,768]{1,0:T(8,128)(2,1)S(1)} %get-tuple-element.58), channel_id=1, source_target_pairs={{0,248},{4,252},{8,0},{12,4},{16,8},{20,12},{24,16},{28,20},{32,24... | collective-permute-start | bytes 1179656 | tf_op jit(solution)/shard_map/ppermute | solution.py:301
  48.8 7.3 %collective-permute-start.14 = (f32[256,768]{1,0:T(8,128)S(1)}, f32[256,768]{1,0:T(8,128)S(1)}, u32[]{:S(2)}, u32[]{:S(2)}) collective-permute-start(f32[256,768]{1,0:T(8,128)S(1)} %get-tuple-element.59), channel_id=1, source_target_pairs={{0,1},{1,0},{2,3},{3,2},{4,5},{5,4},{6,7},{7,6},{8,9},{9,8},{10,11... | collective-permute-start | bytes 2359304 | tf_op jit(solution)/shard_map/ppermute | solution.py:298
  48.8 11.6 %collective-permute-start.12 = (f32[256,768]{1,0:T(8,128)S(1)}, f32[256,768]{1,0:T(8,128)S(1)}, u32[]{:S(2)}, u32[]{:S(2)}) collective-permute-start(f32[256,768]{1,0:T(8,128)S(1)} %get-tuple-element.49), channel_id=1, source_target_pairs={{0,1},{1,0},{2,3},{3,2},{4,5},{5,4},{6,7},{7,6},{8,9},{9,8},{10,11... | collective-permute-start | bytes 2359304 | tf_op jit(solution)/shard_map/ppermute | solution.py:298
  49.3 6.8 %collective-permute-start.6 = (f32[8,1024]{1,0:T(8,128)S(1)}, f32[8,1024]{1,0:T(8,128)S(1)}, u32[]{:S(2)}, u32[]{:S(2)}) collective-permute-start(f32[8,1024]{1,0:T(8,128)S(1)} %get-tuple-element.38.s0), channel_id=1, source_target_pairs={{0,2},{1,3},{2,0},{3,1},{4,6},{5,7},{6,4},{7,5},{8,10},{9,11},{10,... | collective-permute-start | bytes 98312 | tf_op jit(solution)/shard_map/ppermute | solution.py:298
  51.2 13.2 %collective-permute-start.16 = (bf16[256,768]{1,0:T(8,128)(2,1)S(1)}, bf16[256,768]{1,0:T(8,128)(2,1)S(1)}, u32[]{:S(2)}, u32[]{:S(2)}) collective-permute-start(bf16[256,768]{1,0:T(8,128)(2,1)S(1)} %get-tuple-element.60), channel_id=1, source_target_pairs={{0,254},{1,255},{2,252},{3,253},{4,2},{5,3},{6,0},{7,1},{8,6},{9,7... | collective-permute-start | bytes 1179656 | tf_op jit(solution)/shard_map/ppermute | solution.py:315
  56.2 10.6 %collective-permute-start.15 = (bf16[256,768]{1,0:T(8,128)(2,1)S(1)}, bf16[256,768]{1,0:T(8,128)(2,1)S(1)}, u32[]{:S(2)}, u32[]{:S(2)}) collective-permute-start(bf16[256,768]{1,0:T(8,128)(2,1)S(1)} %half_sum.1), channel_id=1, source_target_pairs={{0,2},{1,3},{2,0},{3,1},{4,6},{5,7},{6,4},{7,5},{8,10},{9,11},{10,... | collective-permute-start | bytes 1179656 | tf_op jit(solution)/shard_map/ppermute | solution.py:298
  57.8 2.6 %collective-permute-start.11 = (bf16[512,256]{1,0:T(8,128)(2,1)}, bf16[512,256]{1,0:T(8,128)(2,1)S(1)}, u32[]{:S(2)}, u32[]{:S(2)}) collective-permute-start(bf16[512,256]{1,0:T(8,128)(2,1)} %collective-permute-done.10), channel_id=1, source_target_pairs={{0,1},{1,0},{2,3},{3,2},{4,5},{5,4},{6,7},{7,6},{8,9},{9,8},{10,11... | collective-permute-start | bytes 786440 | tf_op jit(solution)/shard_map/ppermute | solution.py:298
  57.8 1.4 %collective-permute-start.5 = (f32[8,1024]{1,0:T(8,128)S(1)}, f32[8,1024]{1,0:T(8,128)S(1)}, u32[]{:S(2)}, u32[]{:S(2)}) collective-permute-start(f32[8,1024]{1,0:T(8,128)S(1)} %get-tuple-element.38.s0), channel_id=1, source_target_pairs={{0,1},{1,0},{2,3},{3,2},{4,5},{5,4},{6,7},{7,6},{8,9},{9,8},{10,11... | collective-permute-start | bytes 98312 | tf_op jit(solution)/shard_map/ppermute | solution.py:298
  59.1 1.2 %collective-permute-start.7 = (f32[8,1024]{1,0:T(8,128)S(1)}, f32[8,1024]{1,0:T(8,128)S(1)}, u32[]{:S(2)}, u32[]{:S(2)}) collective-permute-start(f32[8,1024]{1,0:T(8,128)S(1)} %collective-permute-done.6.s2), channel_id=1, source_target_pairs={{0,1},{1,0},{2,3},{3,2},{4,5},{5,4},{6,7},{7,6},{8,9},{9,8},{10,11... | collective-permute-start | bytes 98312 | tf_op jit(solution)/shard_map/ppermute | solution.py:298
  66.9 9.6 %collective-permute-start.18 = (bf16[256,768]{1,0:T(8,128)(2,1)S(1)}, bf16[256,768]{1,0:T(8,128)(2,1)S(1)}, u32[]{:S(2)}, u32[]{:S(2)}) collective-permute-start(bf16[256,768]{1,0:T(8,128)(2,1)S(1)} %row_grad.1.g0), channel_id=1, source_target_pairs={{0,2},{1,3},{2,0},{3,1},{4,6},{5,7},{6,4},{7,5},{8,10},{9,11},{10,... | collective-permute-start | bytes 1179656 | tf_op jit(solution)/shard_map/ppermute | solution.py:298
  68.5 8.1 %collective-permute-start.17 = (bf16[256,768]{1,0:T(8,128)(2,1)S(1)}, bf16[256,768]{1,0:T(8,128)(2,1)S(1)}, u32[]{:S(2)}, u32[]{:S(2)}) collective-permute-start(bf16[256,768]{1,0:T(8,128)(2,1)S(1)} %row_grad.1.g0), channel_id=1, source_target_pairs={{0,1},{1,0},{2,3},{3,2},{4,5},{5,4},{6,7},{7,6},{8,9},{9,8},{10,11... | collective-permute-start | bytes 1179656 | tf_op jit(solution)/shard_map/ppermute | solution.py:298
  76.6 1.7 %collective-permute-start.19 = (bf16[256,768]{1,0:T(8,128)(2,1)S(1)}, bf16[256,768]{1,0:T(8,128)(2,1)S(1)}, u32[]{:S(2)}, u32[]{:S(2)}) collective-permute-start(bf16[256,768]{1,0:T(8,128)(2,1)S(1)} %collective-permute-done.18.g2), channel_id=1, source_target_pairs={{0,1},{1,0},{2,3},{3,2},{4,5},{5,4},{6,7},{7,6},{8,9},{9,8},{10,11... | collective-permute-start | bytes 1179656 | tf_op jit(solution)/shard_map/ppermute | solution.py:298

commit v8 on v7

--- a/solution.py
+++ b/solution.py
@@ -21,7 +21,7 @@
 SMEM = pl.BlockSpec(memory_space=pltpu.SMEM)
 
 
-def call(kernel, inputs, outs, scratch=(), name=None):
+def call(kernel, inputs, outs, scratch=(), flops=1 << 20, name=None):
     return pl.pallas_call(
         kernel,
         out_shape=outs,
@@ -30,7 +30,7 @@
         scratch_shapes=list(scratch),
         compiler_params=pltpu.CompilerParams(vmem_limit_bytes=16 << 20),
         cost_estimate=pl.CostEstimate(
-            flops=1 << 20, bytes_accessed=1024, transcendentals=0
+            flops=flops, bytes_accessed=1024, transcendentals=0
         ),
         name=name,
     )(*inputs)
@@ -138,7 +138,7 @@
             return tuple(x + fold(v) for x, v in zip(carry, (*s, loss)))
 
         zero = jnp.zeros((8, n), f32)
-        sums = lax.fori_loop(0, n // CHUNK, step, (zero,) * 4, unroll=4)
+        sums = lax.fori_loop(0, n // CHUNK, step, (zero,) * 4, unroll=n // CHUNK)
         for k, v in enumerate(sums):
             sums_ref[k : k + 1, lanes] += jnp.sum(v, axis=0, keepdims=True)
 
@@ -272,9 +272,12 @@
     out_ref[...] = base + 2.0 * (pushed * tile[0].astype(f32) - total)
 
 
-def gathered_kernel(base_ref, y_ref, one_ref, two_ref, out_ref):
-    total = base_ref[...] + y_ref[...].astype(f32)
-    out_ref[...] = (total + (one_ref[...].astype(f32) + two_ref[...].astype(f32))).astype(bf16)
+def joined_kernel(base_ref, one_ref, two_ref, out_ref):
+    out_ref[...] = base_ref[...] + (one_ref[...].astype(f32) + two_ref[...].astype(f32))
+
+
+def gathered_kernel(base_ref, y_ref, out_ref):
+    out_ref[...] = (base_ref[...] + y_ref[...].astype(f32)).astype(bf16)
 
 
 def chosen_kernel(scal_ref, own_ref, other_ref, out_ref):
@@ -367,6 +370,7 @@
     other3 = over_rows(send3, 1)
     keep2, s2 = lax.optimization_barrier((keep2, s2))
     (half,) = call(halved_kernel, (keep2, other3), [low_grad], name="half_sum")
+    own_grad, half = lax.optimization_barrier((own_grad, half))
     from_y = over_rows(half, 2)
     f3, s3 = over_rows(f3, 1), over_rows(s2, 1)
     s1, s3, f3 = lax.optimization_barrier((s1, s3, f3))
@@ -376,9 +380,10 @@
         [shape(n, wide), shape(1, n)],
         name="listed",
     )
-    (g0,) = call(
-        gathered_kernel, (base, from_y, grad1, grad2), [low_grad], name="row_grad"
-    )
+    (base,) = call(
+        joined_kernel, (base, grad1, grad2), [shape(n, wide)], flops=1 << 31, name="joined"
+    )
+    (g0,) = call(gathered_kernel, (base, from_y), [low_grad], name="row_grad")
     g2 = over_rows(g0, 2)
     g1 = over_rows(g0, 1)
     g3 = over_rows(g2, 1)

time: 114 us -> 112 us (0.982)
  Pallas kernels: 25.8 us -> 21.2 us
  waiting for transfers between devices: 28.9 us -> 33.3 us
  blocking collectives: 33.5 us -> 30 us
  starting transfers between devices: 20.5 us -> 22.9 us
    ppermute x16, waiting for transfers between devices: 19.8 us -> 24.7 us  [over_rows(): return lax.ppermute(x, 'rows', [(i, i ^ flip) for i in range(rows_n)])]
    pallas_call x7 -> x8, Pallas kernels: 21.8 us -> 17.2 us  [call(): pl.pallas_call(kernel, out_shape=outs, in_specs=[SMEM if x.ndim == 1 else...]
    all_to_all x1, blocking collectives: 33.5 us -> 30 us  [local(): parts = lax.all_to_all(part, 'blk', split_axis=0, concat_axis=0, tiled=True)]
    ppermute x1, waiting for transfers between devices: 2.08 us -> 0.01 us  [one_back(): return lax.ppermute(x, ('blk', 'rows'), pairs)]
    ppermute x1, starting transfers between devices: 4.94 us -> 6.81 us  [one_back(): return lax.ppermute(x, ('blk', 'rows'), pairs)]
    ppermute x2, waiting for transfers between devices: 6.97 us -> 8.64 us  [two_on(): return lax.ppermute(x, 'blk', [(b, (b + by) % blks) for b in range(blks)])]
  transfers between devices with their start and end apart: 20 -> 20, of which waited for: 9 -> 9; matrix products, arithmetic and copies ran while one was open for 3% -> 3% of each run, Pallas kernels for 18% -> 14%
where the time goes in v8:
time: 112 us
  waiting for transfers between devices  33.3 us (30%)
  blocking collectives  30 us (27%)
  starting transfers between devices  22.9 us (20%)
  Pallas kernels  21.2 us (19%)
  local copies, waits for them, and re-layouts  3.29 us (3%)
    all_to_all x1, blocking collectives, local(): parts = lax.all_to_all(part, 'blk', split_axis=0, concat_axis=0, tiled=True)  30 us
    ppermute x16, waiting for transfers between devices, over_rows(): return lax.ppermute(x, 'rows', [(i, i ^ flip) for i in range(rows_n)])  24.7 us
    pallas_call x8, Pallas kernels, call(): pl.pallas_call(kernel, out_shape=outs, in_specs=[SMEM if x.ndim == 1 else...  17.2 us
    ppermute x16, starting transfers between devices, over_rows(): return lax.ppermute(x, 'rows', [(i, i ^ flip) for i in range(rows_n)])  10.9 us
    ppermute x2, waiting for transfers between devices, two_on(): return lax.ppermute(x, 'blk', [(b, (b + by) % blks) for b in range(blks)])  8.64 us
    ppermute x1, starting transfers between devices, one_back(): return lax.ppermute(x, ('blk', 'rows'), pairs)  6.81 us
    pallas_call x1, Pallas kernels, embed(): pl.pallas_call(embed_kernel, grid=(wide // step,), out_shape=shape(n + ME...  4 us
    ppermute x2, starting transfers between devices, two_on(): return lax.ppermute(x, 'blk', [(b, (b + by) % blks) for b in range(blks)])  3.33 us
  transfers between devices with their start and end apart: 20, of which 9 were waited for; matrix products, arithmetic and copies ran while one was open for 3% of the time, Pallas kernels for 14%

profile of v8, /device:TPU:8, one launch (start us, length us, event | category | flops | bytes accessed | tf_op | source)
XLA Modules:
  0.0 112.2 jit_solution(17888109113695231755)
XLA Ops:
  0.6 4.0 %embed.1.p0.own_ref = bf16[272,768]{1,0:T(8,128)(2,1)} custom-call(bf16[256,2048]{1,0:T(8,128)(2,1)} %features_ref.1, bf16[2048,768]{1,0:T(8,128)(2,1)} %weight_ref.1, s32[1,256]{1,0:T(1,128)} %bitcast.22, s32[3,256]{1,0:T(4,128)} %bitcast.21, f32[1,256]{1,0:T(1,128)} %bitcast.23), custom_call_target="tpu_custom_call" | custom-call | flops 1073741824 | bytes 4194304 | tf_op jit(solution)/shard_map/embed/pallas_call | solution.py:75
  4.6 2.2 %collective-permute-start.1 = (bf16[272,768]{1,0:T(8,128)(2,1)}, bf16[272,768]{1,0:T(8,128)(2,1)S(1)}, u32[]{:S(2)}, u32[]{:S(2)}) collective-permute-start(bf16[272,768]{1,0:T(8,128)(2,1)} %embed.1.p0.own_ref), channel_id=1, source_target_pairs={{0,2},{1,3},{2,0},{3,1},{4,6},{5,7},{6,4},{7,5},{8,10},{9,11},{10,... | collective-permute-start | bytes 1253384 | tf_op jit(solution)/shard_map/ppermute | solution.py:301
  6.8 0.2 collective-permute-start.3
  7.0 1.3 %copy.12 = bf16[256,2048]{0,1:T(8,128)(2,1)} copy(bf16[256,2048]{1,0:T(8,128)(2,1)S(1)} %copy-done.1) | data formatting | bytes 2097152 | tf_op jit(solution)/shard_map/optimization_barrier | solution.py:327
  8.3 2.0 %dynamic-slice_bitcast_fusion = (bf16[512,256]{1,0:T(8,128)(2,1)S(1)}, bf16[512,256]{1,0:T(8,128)(2,1)S(1)}, bf16[512,256]{1,0:T(8,128)(2,1)}, bf16[512,256]{1,0:T(8,128)(2,1)S(1)}) fusion(bf16[64,4,8,256]{3,2,1,0:T(8,128)(2,1)} %bitcast.20, s32[]{:T(128)S(6)} %select_n.24, s32[]{:T(128)S(6)} %select_n.23, s32[]{:T(128)S(6)} %select_n.22, s32[]{:T(128)S(6)} %select_n.21), kind=kLoop, calls=%fused_computation.1 | loop fusion | bytes 2097168 | tf_op jit(solution)/shard_map/reshape | solution.py:331
  10.3 5.9 %collective-permute-done.1.p2 = bf16[272,768]{1,0:T(8,128)(2,1)S(1)} collective-permute-done((bf16[272,768]{1,0:T(8,128)(2,1)}, bf16[272,768]{1,0:T(8,128)(2,1)S(1)}, u32[]{:S(2)}, u32[]{:S(2)}) %collective-permute-start.1) | collective-permute-done | bytes 417824 | tf_op jit(solution)/shard_map/ppermute | solution.py:301
  16.2 0.5 collective-permute-start.8
  16.7 0.3 collective-permute-start.9
  17.1 5.7 %collective-permute-done.3.n2.other_ref = bf16[272,768]{1,0:T(8,128)(2,1)S(1)} collective-permute-done((bf16[272,768]{1,0:T(8,128)(2,1)}, bf16[272,768]{1,0:T(8,128)(2,1)S(1)}, u32[]{:S(2)}, u32[]{:S(2)}) %collective-permute-start.3) | collective-permute-done | bytes 417824 | tf_op jit(solution)/shard_map/ppermute | solution.py:304
  22.7 1.6 %collective-permute-start.10 = (bf16[512,256]{1,0:T(8,128)(2,1)S(1)}, bf16[512,256]{1,0:T(8,128)(2,1)}, u32[]{:S(2)}, u32[]{:S(2)}) collective-permute-start(bf16[512,256]{1,0:T(8,128)(2,1)S(1)} %get-tuple-element.46), channel_id=1, source_target_pairs={{0,2},{1,3},{2,0},{3,1},{4,6},{5,7},{6,4},{7,5},{8,10},{9,11},{10,... | collective-permute-start | bytes 786440 | tf_op jit(solution)/shard_map/ppermute | solution.py:301
  24.4 0.6 row_choice.1
  25.0 1.8 %collective-permute-start.4 = (bf16[272,768]{1,0:T(8,128)(2,1)S(1)}, bf16[272,768]{1,0:T(8,128)(2,1)S(1)}, u32[]{:S(2)}, u32[]{:S(2)}) collective-permute-start(bf16[272,768]{1,0:T(8,128)(2,1)S(1)} %row_choice.1), channel_id=1, source_target_pairs={{0,6},{1,7},{2,4},{3,5},{4,2},{5,3},{6,0},{7,1},{8,14},{9,15},{10,... | collective-permute-start | bytes 1253384 | tf_op jit(solution)/shard_map/ppermute | solution.py:310
  26.9 8.7 %own_and_two_before.1 = (f32[8,1024]{1,0:T(8,128)S(1)}, bf16[256,1024]{1,0:T(8,128)(2,1)S(1)}, bf16[256,1024]{1,0:T(8,128)(2,1)S(1)}, f32[8,1024]{1,0:T(8,128)S(...) custom-call(s32[5]{0:T(128)S(1)} %pad_add_fusion.scal_ref, bf16[272,768]{1,0:T(8,128)(2,1)S(1)} %copy-done, ...), custom_call_target="tpu_custom_call" | custom-call | flops 1048576 | bytes 1024 | tf_op jit(solution)/shard_map/own_and_two_before/pallas_call | solution.py:25
  35.6 3.1 %collective-permute-start.13 = (bf16[256,768]{1,0:T(8,128)(2,1)S(1)}, bf16[256,768]{1,0:T(8,128)(2,1)S(1)}, u32[]{:S(2)}, u32[]{:S(2)}) collective-permute-start(bf16[256,768]{1,0:T(8,128)(2,1)S(1)} %get-tuple-element.55), channel_id=1, source_target_pairs={{0,248},{4,252},{8,0},{12,4},{16,8},{20,12},{24,16},{28,20},{32,24... | collective-permute-start | bytes 1179656 | tf_op jit(solution)/shard_map/ppermute | solution.py:304
  38.7 4.7 %block_before.1 = (f32[8,1024]{1,0:T(8,128)S(1)}, bf16[256,768]{1,0:T(8,128)(2,1)S(1)}, f32[256,768]{1,0:T(8,128)S(1)}, f32[256,768]{1,0:T(8,128)S(1)}, f32[256,768]{1,0:T(8,128)S(1)}, /*index=5*/f32[256,768]{1,0:T(8,128)S(1)}) custom-call(s32[5]{0:T(128)S(1)} %pad_add_fusion.scal_ref, bf16[272,768]{1,0:T(8,128)(2,1)S(1)} %collective-permute-done.4.n1, ...), custom_call_target="tpu_custom_call" | custom-call | flops 1048576 | bytes 1024 | tf_op jit(solution)/shard_map/block_before/pallas_call | solution.py:25
  43.5 3.0 %collective-permute-done.13.two_ref = bf16[256,768]{1,0:T(8,128)(2,1)S(1)} collective-permute-done((bf16[256,768]{1,0:T(8,128)(2,1)S(1)}, bf16[256,768]{1,0:T(8,128)(2,1)S(1)}, u32[]{:S(2)}, u32[]{:S(2)}) %collective-permute-start.13) | collective-permute-done | bytes 393248 | tf_op jit(solution)/shard_map/ppermute | solution.py:304
  46.4 0.5 collective-permute-start.12
  46.9 6.8 %collective-permute-start.15 = (bf16[256,768]{1,0:T(8,128)(2,1)S(1)}, bf16[256,768]{1,0:T(8,128)(2,1)S(1)}, u32[]{:S(2)}, u32[]{:S(2)}) collective-permute-start(bf16[256,768]{1,0:T(8,128)(2,1)S(1)} %get-tuple-element.63), channel_id=1, source_target_pairs={{0,254},{1,255},{2,252},{3,253},{4,2},{5,3},{6,0},{7,1},{8,6},{9,7... | collective-permute-start | bytes 1179656 | tf_op jit(solution)/shard_map/ppermute | solution.py:318
  53.8 1.9 %collective-permute-start.6 = (f32[8,1024]{1,0:T(8,128)S(1)}, f32[8,1024]{1,0:T(8,128)S(1)}, u32[]{:S(2)}, u32[]{:S(2)}) collective-permute-start(f32[8,1024]{1,0:T(8,128)S(1)} %get-tuple-element.40.s0), channel_id=1, source_target_pairs={{0,2},{1,3},{2,0},{3,1},{4,6},{5,7},{6,4},{7,5},{8,10},{9,11},{10,... | collective-permute-start | bytes 98312 | tf_op jit(solution)/shard_map/ppermute | solution.py:301
  55.6 2.1 %collective-permute-done.6.s2 = f32[8,1024]{1,0:T(8,128)S(1)} collective-permute-done((f32[8,1024]{1,0:T(8,128)S(1)}, f32[8,1024]{1,0:T(8,128)S(1)}, u32[]{:S(2)}, u32[]{:S(2)}) %collective-permute-start.6) | collective-permute-done | bytes 32800 | tf_op jit(solution)/shard_map/ppermute | solution.py:301
  57.8 1.9 %collective-permute-start.16 = (bf16[256,768]{1,0:T(8,128)(2,1)S(1)}, bf16[256,768]{1,0:T(8,128)(2,1)S(1)}, u32[]{:S(2)}, u32[]{:S(2)}) collective-permute-start(bf16[256,768]{1,0:T(8,128)(2,1)S(1)} %half_sum.1), channel_id=1, source_target_pairs={{0,2},{1,3},{2,0},{3,1},{4,6},{5,7},{6,4},{7,5},{8,10},{9,11},{10,... | collective-permute-start | bytes 1179656 | tf_op jit(solution)/shard_map/ppermute | solution.py:301
  59.7 1.2 %collective-permute-done.5.s1 = f32[8,1024]{1,0:T(8,128)S(1)} collective-permute-done((f32[8,1024]{1,0:T(8,128)S(1)}, f32[8,1024]{1,0:T(8,128)S(1)}, u32[]{:S(2)}, u32[]{:S(2)}) %collective-permute-start.5) | collective-permute-done | bytes 32800 | tf_op jit(solution)/shard_map/ppermute | solution.py:301
  60.9 0.2 collective-permute-start.7
  61.1 1.0 collective-permute-done.7.s3
  62.1 1.9 %listed.1 = (f32[256,768]{1,0:T(8,128)S(1)}, f32[1,256]{1,0:T(1,128)}) custom-call(f32[8,1024]{1,0:T(8,128)S(1)} %get-tuple-element.36.anchors_ref, f32[8,1024]{1,0:T(8,128)S(1)} %get-tuple-element.40.s0, f32[8,1024]{1,0:T(8,128)S(1)} %collective-permute-done.5.s1, f32[8,1024]{1,0:T(8,128)S(1)} %collective-permute-done.6.s2, ...), custom_call_target="tpu_custom_call" | custom-call | flops 1048576 | bytes 1024 | tf_op jit(solution)/shard_map/listed/pallas_call | solution.py:25
  64.2 4.5 %collective-permute-done.16.y_ref = bf16[256,768]{1,0:T(8,128)(2,1)S(1)} collective-permute-done((bf16[256,768]{1,0:T(8,128)(2,1)S(1)}, bf16[256,768]{1,0:T(8,128)(2,1)S(1)}, u32[]{:S(2)}, u32[]{:S(2)}) %collective-permute-start.16) | collective-permute-done | bytes 393248 | tf_op jit(solution)/shard_map/ppermute | solution.py:301
  68.7 1.8 %collective-permute-start.18 = (bf16[256,768]{1,0:T(8,128)(2,1)S(1)}, bf16[256,768]{1,0:T(8,128)(2,1)S(1)}, u32[]{:S(2)}, u32[]{:S(2)}) collective-permute-start(bf16[256,768]{1,0:T(8,128)(2,1)S(1)} %row_grad.1.g0), channel_id=1, source_target_pairs={{0,2},{1,3},{2,0},{3,1},{4,6},{5,7},{6,4},{7,5},{8,10},{9,11},{10,... | collective-permute-start | bytes 1179656 | tf_op jit(solution)/shard_map/ppermute | solution.py:301
  70.6 8.2 %collective-permute-done.18.g2 = bf16[256,768]{1,0:T(8,128)(2,1)S(1)} collective-permute-done((bf16[256,768]{1,0:T(8,128)(2,1)S(1)}, bf16[256,768]{1,0:T(8,128)(2,1)S(1)}, u32[]{:S(2)}, u32[]{:S(2)}) %collective-permute-start.18) | collective-permute-done | bytes 393248 | tf_op jit(solution)/shard_map/ppermute | solution.py:301
  78.8 1.7 %collective-permute-done.19.g3 = bf16[256,768]{1,0:T(8,128)(2,1)S(1)} collective-permute-done((bf16[256,768]{1,0:T(8,128)(2,1)S(1)}, bf16[256,768]{1,0:T(8,128)(2,1)S(1)}, u32[]{:S(2)}, u32[]{:S(2)}) %collective-permute-start.19) | collective-permute-done | bytes 393248 | tf_op jit(solution)/shard_map/ppermute | solution.py:301
  80.5 1.0 head_grad.1
  81.5 30.0 %all_to_all.9 = bf16[64,8,768]{2,1,0:T(8,128)(2,1)S(1)} all-to-all(bf16[64,8,768]{2,1,0:T(8,128)(2,1)S(1)} %bitcast.19), channel_id=1, replica_groups=mesh['blk'=64,'rows'=4] {'blk'}, dimensions={0} | all-to-all | bytes 1572864 | tf_op jit(solution)/shard_map/all_to_all | solution.py:396
  111.4 0.7 convert_reduce_fusion
  (28 shorter events, 0.4 us)
Async XLA Ops:
  0.6 6.4 %copy-start.1 = (bf16[256,2048]{1,0:T(8,128)(2,1)S(1)}, bf16[256,2048]{1,0:T(8,128)(2,1)}, u32[]{:S(2)}) copy-start(bf16[256,2048]{1,0:T(8,128)(2,1)} %features_ref.1) | copy-start | bytes 3145732
  4.6 19.7 %copy-start.2 = (s32[1,3]{1,0:T(1,128)S(1)}, s32[1,3]{1,0:T(1,128)}, u32[]{:S(2)}) copy-start(s32[1,3]{1,0:T(1,128)} %param.10) | copy-start | bytes 40
  4.6 19.8 %copy-start = (bf16[272,768]{1,0:T(8,128)(2,1)S(1)}, bf16[272,768]{1,0:T(8,128)(2,1)}, u32[]{:S(2)}) copy-start(bf16[272,768]{1,0:T(8,128)(2,1)} %embed.1.p0.own_ref) | copy-start | bytes 1253380
  4.6 11.6 %collective-permute-start.1 = (bf16[272,768]{1,0:T(8,128)(2,1)}, bf16[272,768]{1,0:T(8,128)(2,1)S(1)}, u32[]{:S(2)}, u32[]{:S(2)}) collective-permute-start(bf16[272,768]{1,0:T(8,128)(2,1)} %embed.1.p0.own_ref), channel_id=1, source_target_pairs={{0,2},{1,3},{2,0},{3,1},{4,6},{5,7},{6,4},{7,5},{8,10},{9,11},{10,... | collective-permute-start | bytes 1253384 | tf_op jit(solution)/shard_map/ppermute | solution.py:301
  6.8 15.9 %collective-permute-start.3 = (bf16[272,768]{1,0:T(8,128)(2,1)}, bf16[272,768]{1,0:T(8,128)(2,1)S(1)}, u32[]{:S(2)}, u32[]{:S(2)}) collective-permute-start(bf16[272,768]{1,0:T(8,128)(2,1)} %embed.1.p0.own_ref), channel_id=1, source_target_pairs={{0,8},{4,12},{8,16},{12,20},{16,24},{20,28},{24,32},{28,36},{32,40... | collective-permute-start | bytes 1253384 | tf_op jit(solution)/shard_map/ppermute | solution.py:304
  7.0 18.0 %collective-permute-start = (bf16[272,768]{1,0:T(8,128)(2,1)}, bf16[272,768]{1,0:T(8,128)(2,1)S(1)}, u32[]{:S(2)}, u32[]{:S(2)}) collective-permute-start(bf16[272,768]{1,0:T(8,128)(2,1)} %embed.1.p0.own_ref), channel_id=1, source_target_pairs={{0,1},{1,0},{2,3},{3,2},{4,5},{5,4},{6,7},{7,6},{8,9},{9,8},{10,11... | collective-permute-start | bytes 1253384 | tf_op jit(solution)/shard_map/ppermute | solution.py:301
  16.2 10.6 %collective-permute-start.2 = (bf16[272,768]{1,0:T(8,128)(2,1)S(1)}, bf16[272,768]{1,0:T(8,128)(2,1)S(1)}, u32[]{:S(2)}, u32[]{:S(2)}) collective-permute-start(bf16[272,768]{1,0:T(8,128)(2,1)S(1)} %collective-permute-done.1.p2), channel_id=1, source_target_pairs={{0,1},{1,0},{2,3},{3,2},{4,5},{5,4},{6,7},{7,6},{8,9},{9,8},{10,11... | collective-permute-start | bytes 1253384 | tf_op jit(solution)/shard_map/ppermute | solution.py:301
  16.2 19.3 %collective-permute-start.8 = (bf16[512,256]{1,0:T(8,128)(2,1)}, bf16[512,256]{1,0:T(8,128)(2,1)S(1)}, u32[]{:S(2)}, u32[]{:S(2)}) collective-permute-start(bf16[512,256]{1,0:T(8,128)(2,1)} %get-tuple-element.44), channel_id=1, source_target_pairs={{0,1},{1,0},{2,3},{3,2},{4,5},{5,4},{6,7},{7,6},{8,9},{9,8},{10,11... | collective-permute-start | bytes 786440 | tf_op jit(solution)/shard_map/ppermute | solution.py:301
  16.7 18.8 %collective-permute-start.9 = (bf16[512,256]{1,0:T(8,128)(2,1)S(1)}, bf16[512,256]{1,0:T(8,128)(2,1)S(1)}, u32[]{:S(2)}, u32[]{:S(2)}) collective-permute-start(bf16[512,256]{1,0:T(8,128)(2,1)S(1)} %get-tuple-element.45), channel_id=1, source_target_pairs={{0,2},{1,3},{2,0},{3,1},{4,6},{5,7},{6,4},{7,5},{8,10},{9,11},{10,... | collective-permute-start | bytes 786440 | tf_op jit(solution)/shard_map/ppermute | solution.py:301
  22.7 12.8 %collective-permute-start.10 = (bf16[512,256]{1,0:T(8,128)(2,1)S(1)}, bf16[512,256]{1,0:T(8,128)(2,1)}, u32[]{:S(2)}, u32[]{:S(2)}) collective-permute-start(bf16[512,256]{1,0:T(8,128)(2,1)S(1)} %get-tuple-element.46), channel_id=1, source_target_pairs={{0,2},{1,3},{2,0},{3,1},{4,6},{5,7},{6,4},{7,5},{8,10},{9,11},{10,... | collective-permute-start | bytes 786440 | tf_op jit(solution)/shard_map/ppermute | solution.py:301
  25.0 13.7 %collective-permute-start.4 = (bf16[272,768]{1,0:T(8,128)(2,1)S(1)}, bf16[272,768]{1,0:T(8,128)(2,1)S(1)}, u32[]{:S(2)}, u32[]{:S(2)}) collective-permute-start(bf16[272,768]{1,0:T(8,128)(2,1)S(1)} %row_choice.1), channel_id=1, source_target_pairs={{0,6},{1,7},{2,4},{3,5},{4,2},{5,3},{6,0},{7,1},{8,14},{9,15},{10,... | collective-permute-start | bytes 1253384 | tf_op jit(solution)/shard_map/ppermute | solution.py:310
  35.6 10.8 %collective-permute-start.13 = (bf16[256,768]{1,0:T(8,128)(2,1)S(1)}, bf16[256,768]{1,0:T(8,128)(2,1)S(1)}, u32[]{:S(2)}, u32[]{:S(2)}) collective-permute-start(bf16[256,768]{1,0:T(8,128)(2,1)S(1)} %get-tuple-element.55), channel_id=1, source_target_pairs={{0,248},{4,252},{8,0},{12,4},{16,8},{20,12},{24,16},{28,20},{32,24... | collective-permute-start | bytes 1179656 | tf_op jit(solution)/shard_map/ppermute | solution.py:304
  46.4 11.3 %collective-permute-start.14 = (f32[256,768]{1,0:T(8,128)S(1)}, f32[256,768]{1,0:T(8,128)S(1)}, u32[]{:S(2)}, u32[]{:S(2)}) collective-permute-start(f32[256,768]{1,0:T(8,128)S(1)} %get-tuple-element.56), channel_id=1, source_target_pairs={{0,1},{1,0},{2,3},{3,2},{4,5},{5,4},{6,7},{7,6},{8,9},{9,8},{10,11... | collective-permute-start | bytes 2359304 | tf_op jit(solution)/shard_map/ppermute | solution.py:301
  46.4 15.7 %collective-permute-start.12 = (f32[256,768]{1,0:T(8,128)S(1)}, f32[256,768]{1,0:T(8,128)S(1)}, u32[]{:S(2)}, u32[]{:S(2)}) collective-permute-start(f32[256,768]{1,0:T(8,128)S(1)} %get-tuple-element.51), channel_id=1, source_target_pairs={{0,1},{1,0},{2,3},{3,2},{4,5},{5,4},{6,7},{7,6},{8,9},{9,8},{10,11... | collective-permute-start | bytes 2359304 | tf_op jit(solution)/shard_map/ppermute | solution.py:301
  46.9 17.2 %collective-permute-start.15 = (bf16[256,768]{1,0:T(8,128)(2,1)S(1)}, bf16[256,768]{1,0:T(8,128)(2,1)S(1)}, u32[]{:S(2)}, u32[]{:S(2)}) collective-permute-start(bf16[256,768]{1,0:T(8,128)(2,1)S(1)} %get-tuple-element.63), channel_id=1, source_target_pairs={{0,254},{1,255},{2,252},{3,253},{4,2},{5,3},{6,0},{7,1},{8,6},{9,7... | collective-permute-start | bytes 1179656 | tf_op jit(solution)/shard_map/ppermute | solution.py:318
  53.7 8.4 %collective-permute-start.11 = (bf16[512,256]{1,0:T(8,128)(2,1)}, bf16[512,256]{1,0:T(8,128)(2,1)S(1)}, u32[]{:S(2)}, u32[]{:S(2)}) collective-permute-start(bf16[512,256]{1,0:T(8,128)(2,1)} %collective-permute-done.10), channel_id=1, source_target_pairs={{0,1},{1,0},{2,3},{3,2},{4,5},{5,4},{6,7},{7,6},{8,9},{9,8},{10,11... | collective-permute-start | bytes 786440 | tf_op jit(solution)/shard_map/ppermute | solution.py:301
  53.8 3.9 %collective-permute-start.6 = (f32[8,1024]{1,0:T(8,128)S(1)}, f32[8,1024]{1,0:T(8,128)S(1)}, u32[]{:S(2)}, u32[]{:S(2)}) collective-permute-start(f32[8,1024]{1,0:T(8,128)S(1)} %get-tuple-element.40.s0), channel_id=1, source_target_pairs={{0,2},{1,3},{2,0},{3,1},{4,6},{5,7},{6,4},{7,5},{8,10},{9,11},{10,... | collective-permute-start | bytes 98312 | tf_op jit(solution)/shard_map/ppermute | solution.py:301
  57.8 10.9 %collective-permute-start.16 = (bf16[256,768]{1,0:T(8,128)(2,1)S(1)}, bf16[256,768]{1,0:T(8,128)(2,1)S(1)}, u32[]{:S(2)}, u32[]{:S(2)}) collective-permute-start(bf16[256,768]{1,0:T(8,128)(2,1)S(1)} %half_sum.1), channel_id=1, source_target_pairs={{0,2},{1,3},{2,0},{3,1},{4,6},{5,7},{6,4},{7,5},{8,10},{9,11},{10,... | collective-permute-start | bytes 1179656 | tf_op jit(solution)/shard_map/ppermute | solution.py:301
  59.7 1.2 %collective-permute-start.5 = (f32[8,1024]{1,0:T(8,128)S(1)}, f32[8,1024]{1,0:T(8,128)S(1)}, u32[]{:S(2)}, u32[]{:S(2)}) collective-permute-start(f32[8,1024]{1,0:T(8,128)S(1)} %get-tuple-element.40.s0), channel_id=1, source_target_pairs={{0,1},{1,0},{2,3},{3,2},{4,5},{5,4},{6,7},{7,6},{8,9},{9,8},{10,11... | collective-permute-start | bytes 98312 | tf_op jit(solution)/shard_map/ppermute | solution.py:301
  60.9 1.2 %collective-permute-start.7 = (f32[8,1024]{1,0:T(8,128)S(1)}, f32[8,1024]{1,0:T(8,128)S(1)}, u32[]{:S(2)}, u32[]{:S(2)}) collective-permute-start(f32[8,1024]{1,0:T(8,128)S(1)} %collective-permute-done.6.s2), channel_id=1, source_target_pairs={{0,1},{1,0},{2,3},{3,2},{4,5},{5,4},{6,7},{7,6},{8,9},{9,8},{10,11... | collective-permute-start | bytes 98312 | tf_op jit(solution)/shard_map/ppermute | solution.py:301
  68.7 10.0 %collective-permute-start.18 = (bf16[256,768]{1,0:T(8,128)(2,1)S(1)}, bf16[256,768]{1,0:T(8,128)(2,1)S(1)}, u32[]{:S(2)}, u32[]{:S(2)}) collective-permute-start(bf16[256,768]{1,0:T(8,128)(2,1)S(1)} %row_grad.1.g0), channel_id=1, source_target_pairs={{0,2},{1,3},{2,0},{3,1},{4,6},{5,7},{6,4},{7,5},{8,10},{9,11},{10,... | collective-permute-start | bytes 1179656 | tf_op jit(solution)/shard_map/ppermute | solution.py:301
  70.6 8.2 %collective-permute-start.17 = (bf16[256,768]{1,0:T(8,128)(2,1)S(1)}, bf16[256,768]{1,0:T(8,128)(2,1)S(1)}, u32[]{:S(2)}, u32[]{:S(2)}) collective-permute-start(bf16[256,768]{1,0:T(8,128)(2,1)S(1)} %row_grad.1.g0), channel_id=1, source_target_pairs={{0,1},{1,0},{2,3},{3,2},{4,5},{5,4},{6,7},{7,6},{8,9},{9,8},{10,11... | collective-permute-start | bytes 1179656 | tf_op jit(solution)/shard_map/ppermute | solution.py:301
  78.8 1.7 %collective-permute-start.19 = (bf16[256,768]{1,0:T(8,128)(2,1)S(1)}, bf16[256,768]{1,0:T(8,128)(2,1)S(1)}, u32[]{:S(2)}, u32[]{:S(2)}) collective-permute-start(bf16[256,768]{1,0:T(8,128)(2,1)S(1)} %collective-permute-done.18.g2), channel_id=1, source_target_pairs={{0,1},{1,0},{2,3},{3,2},{4,5},{5,4},{6,7},{7,6},{8,9},{9,8},{10,11... | collective-permute-start | bytes 1179656 | tf_op jit(solution)/shard_map/ppermute | solution.py:301

commit v9 on v8

--- a/solution.py
+++ b/solution.py
@@ -218,8 +218,9 @@
 
 def last_kernel(
     scal_ref, n1, n2, p0, p1, p2, p3, c0, c2, anchors_ref, before_ref, sums_ref, grad_ref,
-    keep0, send1, keep2, send3, coef_ref, products_ref, lanes_ref, sq_ref, label_ref,
+    keep0, keep2, *rest
 ):
+    sends, (coef_ref, products_ref, lanes_ref, sq_ref, label_ref) = rest[:-5], rest[-5:]
     n = p0.shape[0] - META
     tile = [p[:n, :] for p in (p0, p1, p2, p3)]
     sums_ref[...] = before_ref[...]
@@ -229,20 +230,27 @@
     )
     for k in range(3):
         sums_ref[k : k + 1, :] = sums_ref[k : k + 1, :] * anchors_ref[6:7, :]
-    for i, ref in enumerate((keep0, send1, keep2, send3)):
+    pieces = len(sends) // 2
+    targets = ((keep0,), sends[:pieces], (keep2,), sends[pieces:])
+    for i, refs in enumerate(targets):
         lanes = slice(i * n, (i + 1) * n)
         total = tn(c0[:, lanes], p0[:n, :])
         total = total + tn(coef_ref[:, lanes], n1[:n, :]) + tn(c2[:, lanes], n2[:n, :])
-        ref[...] = 2.0 * total
-
-
-def halved_kernel(keep_ref, other_ref, out_ref):
-    out_ref[...] = (keep_ref[...] + other_ref[...]).astype(bf16)
+        part = n // len(refs)
+        for j, ref in enumerate(refs):
+            ref[...] = 2.0 * total[j * part : (j + 1) * part, :]
+
+
+def halved_kernel(keep_ref, *refs):
+    others, out_ref = refs[:-1], refs[-1]
+    other = jnp.concatenate([x[...] for x in others], axis=0)
+    out_ref[...] = (keep_ref[...] + other).astype(bf16)
 
 
 def listed_kernel(
-    anchors_ref, s0, s1, s2, s3, p0, p1, p2, p3, keep_ref, other_ref, own_ref, out_ref, loss_ref
+    anchors_ref, s0, s1, s2, s3, p0, p1, p2, p3, keep_ref, own_ref, *refs
 ):
+    sent, (out_ref, loss_ref) = refs[:-2], refs[-2:]
     n = p0.shape[0] - META
     tile = [p[:n, :] for p in (p0, p1, p2, p3)]
     sums = []
@@ -268,7 +276,7 @@
         high = matrix.astype(bf16)
         low = (matrix - high.astype(f32)).astype(bf16)
         total = total + nn(high, part) + nn(low, part)
-    base = keep_ref[...] + other_ref[...] + own_ref[...]
+    base = keep_ref[...] + jnp.concatenate([x[...] for x in sent], axis=0) + own_ref[...]
     out_ref[...] = base + 2.0 * (pushed * tile[0].astype(f32) - total)
 
 
@@ -356,27 +364,26 @@
     )
     grad2, f1, f2, f3 = lax.optimization_barrier((grad2, f1, f2, f3))
     grad2 = two_on(grad2, -2)
-    s0, grad1, keep0, send1, keep2, send3 = call(
+    s0, grad1, keep0, keep2, *sends = call(
         last_kernel,
         (scal, n1, n2, *tile, c0, c2, anchors, sums),
-        [shape(8, 4 * n), low_grad] + [shape(n, wide)] * 4,
+        [shape(8, 4 * n), low_grad] + [shape(n, wide)] * 2 + [shape(n // 4, wide)] * 8,
         [pltpu.VMEM((n, 4 * n), bf16), *scratch],
         name="block_before",
     )
     grad1 = one_back(grad1)
     s2 = over_rows(s0, 2)
     s1 = over_rows(s0, 1)
-    send3, grad2 = lax.optimization_barrier((send3, grad2))
-    other3 = over_rows(send3, 1)
-    keep2, s2 = lax.optimization_barrier((keep2, s2))
-    (half,) = call(halved_kernel, (keep2, other3), [low_grad], name="half_sum")
+    sends = [over_rows(x, 1) for x in sends]
+    keep2, s2, grad2 = lax.optimization_barrier((keep2, s2, grad2))
+    (half,) = call(halved_kernel, (keep2, *sends[4:]), [low_grad], name="half_sum")
     own_grad, half = lax.optimization_barrier((own_grad, half))
     from_y = over_rows(half, 2)
     f3, s3 = over_rows(f3, 1), over_rows(s2, 1)
     s1, s3, f3 = lax.optimization_barrier((s1, s3, f3))
     base, anchor_loss = call(
         listed_kernel,
-        (anchors, s0, s1, s2, s3, *tile, keep0, over_rows(send1, 1), own_grad),
+        (anchors, s0, s1, s2, s3, *tile, keep0, own_grad, *sends[:4]),
         [shape(n, wide), shape(1, n)],
         name="listed",
     )

time: 112 us -> 110 us (0.982)
  starting transfers between devices: 22.9 us -> 21 us
    ppermute x1, starting transfers between devices: 6.81 us -> 3.42 us  [one_back(): return lax.ppermute(x, ('blk', 'rows'), pairs)]
    ppermute x2, waiting for transfers between devices: 8.64 us -> 5.69 us  [two_on(): return lax.ppermute(x, 'blk', [(b, (b + by) % blks) for b in range(blks)])]
    ppermute x1, waiting for transfers between devices: 0.01 us -> 2.61 us  [one_back(): return lax.ppermute(x, ('blk', 'rows'), pairs)]
    ppermute x16 -> x22, starting transfers between devices: 10.9 us -> 12.4 us  [over_rows(): return lax.ppermute(x, 'rows', [(i, i ^ flip) for i in range(rows_n)])]
    ppermute x16 -> x22, waiting for transfers between devices: 24.7 us -> 24.7 us  [over_rows(): return lax.ppermute(x, 'rows', [(i, i ^ flip) for i in range(rows_n)])]
  transfers between devices with their start and end apart: 20 -> 26, of which waited for: 9 -> 9; matrix products, arithmetic and copies ran while one was open for 3% -> 3% of each run, Pallas kernels for 14% -> 15%
where the time goes in v9:
time: 110 us
  waiting for transfers between devices  33 us (30%)
  blocking collectives  30.4 us (28%)
  Pallas kernels  21.1 us (19%)
  starting transfers between devices  21 us (19%)
  local copies, waits for them, and re-layouts  3.3 us (3%)
    all_to_all x1, blocking collectives, local(): parts = lax.all_to_all(part, 'blk', split_axis=0, concat_axis=0, tiled=True)  30.4 us
    ppermute x22, waiting for transfers between devices, over_rows(): return lax.ppermute(x, 'rows', [(i, i ^ flip) for i in range(rows_n)])  24.7 us
    pallas_call x8, Pallas kernels, call(): pl.pallas_call(kernel, out_shape=outs, in_specs=[SMEM if x.ndim == 1 else...  17.1 us
    ppermute x22, starting transfers between devices, over_rows(): return lax.ppermute(x, 'rows', [(i, i ^ flip) for i in range(rows_n)])  12.4 us
    ppermute x2, waiting for transfers between devices, two_on(): return lax.ppermute(x, 'blk', [(b, (b + by) % blks) for b in range(blks)])  5.69 us
    pallas_call x1, Pallas kernels, embed(): pl.pallas_call(embed_kernel, grid=(wide // step,), out_shape=shape(n + ME...  3.99 us
    ppermute x1, starting transfers between devices, one_back(): return lax.ppermute(x, ('blk', 'rows'), pairs)  3.42 us
    ppermute x2, starting transfers between devices, two_on(): return lax.ppermute(x, 'blk', [(b, (b + by) % blks) for b in range(blks)])  3.27 us
  transfers between devices with their start and end apart: 26, of which 9 were waited for; matrix products, arithmetic and copies ran while one was open for 3% of the time, Pallas kernels for 15%

profile of v9, /device:TPU:8, one launch (start us, length us, event | category | flops | bytes accessed | tf_op | source)
XLA Modules:
  0.0 110.3 jit_solution(16035295324280118418)
XLA Ops:
  0.6 4.0 %embed.1.p0.own_ref = bf16[272,768]{1,0:T(8,128)(2,1)} custom-call(bf16[256,2048]{1,0:T(8,128)(2,1)} %features_ref.1, bf16[2048,768]{1,0:T(8,128)(2,1)} %weight_ref.1, s32[1,256]{1,0:T(1,128)} %bitcast.22, s32[3,256]{1,0:T(4,128)} %bitcast.21, f32[1,256]{1,0:T(1,128)} %bitcast.23), custom_call_target="tpu_custom_call" | custom-call | flops 1073741824 | bytes 4194304 | tf_op jit(solution)/shard_map/embed/pallas_call | solution.py:75
  4.6 2.2 %collective-permute-start.1 = (bf16[272,768]{1,0:T(8,128)(2,1)}, bf16[272,768]{1,0:T(8,128)(2,1)S(1)}, u32[]{:S(2)}, u32[]{:S(2)}) collective-permute-start(bf16[272,768]{1,0:T(8,128)(2,1)} %embed.1.p0.own_ref), channel_id=1, source_target_pairs={{0,2},{1,3},{2,0},{3,1},{4,6},{5,7},{6,4},{7,5},{8,10},{9,11},{10,... | collective-permute-start | bytes 1253384 | tf_op jit(solution)/shard_map/ppermute | solution.py:309
  7.0 1.3 %copy.12 = bf16[256,2048]{0,1:T(8,128)(2,1)} copy(bf16[256,2048]{1,0:T(8,128)(2,1)S(1)} %copy-done.1) | data formatting | bytes 2097152 | tf_op jit(solution)/shard_map/optimization_barrier | solution.py:335
  8.3 2.0 %dynamic-slice_bitcast_fusion = (bf16[512,256]{1,0:T(8,128)(2,1)S(1)}, bf16[512,256]{1,0:T(8,128)(2,1)S(1)}, bf16[512,256]{1,0:T(8,128)(2,1)}, bf16[512,256]{1,0:T(8,128)(2,1)S(1)}) fusion(bf16[64,4,8,256]{3,2,1,0:T(8,128)(2,1)} %bitcast.20, s32[]{:T(128)S(6)} %select_n.24, s32[]{:T(128)S(6)} %select_n.23, s32[]{:T(128)S(6)} %select_n.22, s32[]{:T(128)S(6)} %select_n.21), kind=kLoop, calls=%fused_computation.1 | loop fusion | bytes 2097168 | tf_op jit(solution)/shard_map/reshape | solution.py:339
  10.3 5.9 %collective-permute-done.1.p2 = bf16[272,768]{1,0:T(8,128)(2,1)S(1)} collective-permute-done((bf16[272,768]{1,0:T(8,128)(2,1)}, bf16[272,768]{1,0:T(8,128)(2,1)S(1)}, u32[]{:S(2)}, u32[]{:S(2)}) %collective-permute-start.1) | collective-permute-done | bytes 417824 | tf_op jit(solution)/shard_map/ppermute | solution.py:309
  16.2 0.5 collective-permute-start.7
  16.7 0.3 collective-permute-start.8
  17.1 5.7 %collective-permute-done.3.n2.other_ref = bf16[272,768]{1,0:T(8,128)(2,1)S(1)} collective-permute-done((bf16[272,768]{1,0:T(8,128)(2,1)}, bf16[272,768]{1,0:T(8,128)(2,1)S(1)}, u32[]{:S(2)}, u32[]{:S(2)}) %collective-permute-start.3) | collective-permute-done | bytes 417824 | tf_op jit(solution)/shard_map/ppermute | solution.py:312
  22.7 1.6 %collective-permute-start.9 = (bf16[512,256]{1,0:T(8,128)(2,1)S(1)}, bf16[512,256]{1,0:T(8,128)(2,1)S(1)}, u32[]{:S(2)}, u32[]{:S(2)}) collective-permute-start(bf16[512,256]{1,0:T(8,128)(2,1)S(1)} %get-tuple-element.50), channel_id=1, source_target_pairs={{0,2},{1,3},{2,0},{3,1},{4,6},{5,7},{6,4},{7,5},{8,10},{9,11},{10,... | collective-permute-start | bytes 786440 | tf_op jit(solution)/shard_map/ppermute | solution.py:309
  24.4 0.6 row_choice.1
  25.0 1.8 %collective-permute-start.4 = (bf16[272,768]{1,0:T(8,128)(2,1)S(1)}, bf16[272,768]{1,0:T(8,128)(2,1)S(1)}, u32[]{:S(2)}, u32[]{:S(2)}) collective-permute-start(bf16[272,768]{1,0:T(8,128)(2,1)S(1)} %row_choice.1), channel_id=1, source_target_pairs={{0,6},{1,7},{2,4},{3,5},{4,2},{5,3},{6,0},{7,1},{8,14},{9,15},{10,... | collective-permute-start | bytes 1253384 | tf_op jit(solution)/shard_map/ppermute | solution.py:318
  26.8 8.7 %own_and_two_before.1 = (f32[8,1024]{1,0:T(8,128)S(1)}, bf16[256,1024]{1,0:T(8,128)(2,1)S(1)}, bf16[256,1024]{1,0:T(8,128)(2,1)S(1)}, f32[8,1024]{1,0:T(8,128)S(...) custom-call(s32[5]{0:T(128)S(1)} %pad_add_fusion.scal_ref, bf16[272,768]{1,0:T(8,128)(2,1)S(1)} %copy-done, ...), custom_call_target="tpu_custom_call" | custom-call | flops 1048576 | bytes 1024 | tf_op jit(solution)/shard_map/own_and_two_before/pallas_call | solution.py:25
  35.5 3.1 %collective-permute-start.10 = (bf16[256,768]{1,0:T(8,128)(2,1)S(1)}, bf16[256,768]{1,0:T(8,128)(2,1)S(1)}, u32[]{:S(2)}, u32[]{:S(2)}) collective-permute-start(bf16[256,768]{1,0:T(8,128)(2,1)S(1)} %get-tuple-element.51), channel_id=1, source_target_pairs={{0,248},{4,252},{8,0},{12,4},{16,8},{20,12},{24,16},{28,20},{32,24... | collective-permute-start | bytes 1179656 | tf_op jit(solution)/shard_map/ppermute | solution.py:312
  38.6 4.7 %block_before.1 = (f32[8,1024]{1,0:T(8,128)S(1)}, bf16[256,768]{1,0:T(8,128)(2,1)S(1)}, f32[256,768]{1,0:T(8,128)S(1)}, f32[256,768]{1,0:T(8,128)S(1)}, f32[64,7...) custom-call(s32[5]{0:T(128)S(1)} %pad_add_fusion.scal_ref, ...), custom_call_target="tpu_custom_call" | custom-call | flops 1048576 | bytes 1024 | tf_op jit(solution)/shard_map/block_before/pallas_call | solution.py:25
  43.4 0.5 collective-permute-start.14
  43.9 1.6 %collective-permute-start.6 = (f32[8,1024]{1,0:T(8,128)S(1)}, f32[8,1024]{1,0:T(8,128)S(1)}, u32[]{:S(2)}, u32[]{:S(2)}) collective-permute-start(f32[8,1024]{1,0:T(8,128)S(1)} %get-tuple-element.45.s0), channel_id=1, source_target_pairs={{0,2},{1,3},{2,0},{3,1},{4,6},{5,7},{6,4},{7,5},{8,10},{9,11},{10,... | collective-permute-start | bytes 98312 | tf_op jit(solution)/shard_map/ppermute | solution.py:309
  45.5 2.3 %collective-permute-done.6.s2 = f32[8,1024]{1,0:T(8,128)S(1)} collective-permute-done((f32[8,1024]{1,0:T(8,128)S(1)}, f32[8,1024]{1,0:T(8,128)S(1)}, u32[]{:S(2)}, u32[]{:S(2)}) %collective-permute-start.6) | collective-permute-done | bytes 32800 | tf_op jit(solution)/shard_map/ppermute | solution.py:309
  47.8 1.2 %collective-permute-done.5.s1 = f32[8,1024]{1,0:T(8,128)S(1)} collective-permute-done((f32[8,1024]{1,0:T(8,128)S(1)}, f32[8,1024]{1,0:T(8,128)S(1)}, u32[]{:S(2)}, u32[]{:S(2)}) %collective-permute-start.5) | collective-permute-done | bytes 32800 | tf_op jit(solution)/shard_map/ppermute | solution.py:309
  49.2 0.3 collective-permute-start.16
  49.7 3.4 %collective-permute-start.21 = (bf16[256,768]{1,0:T(8,128)(2,1)S(1)}, bf16[256,768]{1,0:T(8,128)(2,1)S(1)}, u32[]{:S(2)}, u32[]{:S(2)}) collective-permute-start(bf16[256,768]{1,0:T(8,128)(2,1)S(1)} %get-tuple-element.73), channel_id=1, source_target_pairs={{0,254},{1,255},{2,252},{3,253},{4,2},{5,3},{6,0},{7,1},{8,6},{9,7... | collective-permute-start | bytes 1179656 | tf_op jit(solution)/shard_map/ppermute | solution.py:326
  53.1 0.5 collective-permute-start.18
  53.7 0.4 collective-permute-start.20
  54.3 2.1 %collective-permute-start.22 = (bf16[256,768]{1,0:T(8,128)(2,1)S(1)}, bf16[256,768]{1,0:T(8,128)(2,1)S(1)}, u32[]{:S(2)}, u32[]{:S(2)}) collective-permute-start(bf16[256,768]{1,0:T(8,128)(2,1)S(1)} %half_sum.1), channel_id=1, source_target_pairs={{0,2},{1,3},{2,0},{3,1},{4,6},{5,7},{6,4},{7,5},{8,10},{9,11},{10,... | collective-permute-start | bytes 1179656 | tf_op jit(solution)/shard_map/ppermute | solution.py:309
  56.5 2.0 %listed.1 = (f32[256,768]{1,0:T(8,128)S(1)}, f32[1,256]{1,0:T(1,128)}) custom-call(f32[8,1024]{1,0:T(8,128)S(1)} %get-tuple-element.41.anchors_ref, f32[8,1024]{1,0:T(8,128)S(1)} %get-tuple-element.45.s0, f32[8,1024]{1,0:T(8,128)S(1)} %collective-permute-done.5.s1, f32[8,1024]{1,0:T(8,128)S(1)} %collective-permute-done.6.s2, ...), custom_call_target="tpu_custom_call" | custom-call | flops 1048576 | bytes 1024 | tf_op jit(solution)/shard_map/listed/pallas_call | solution.py:25
  58.5 2.6 %collective-permute-done.21.one_ref = bf16[256,768]{1,0:T(8,128)(2,1)S(1)} collective-permute-done((bf16[256,768]{1,0:T(8,128)(2,1)S(1)}, bf16[256,768]{1,0:T(8,128)(2,1)S(1)}, u32[]{:S(2)}, u32[]{:S(2)}) %collective-permute-start.21) | collective-permute-done | bytes 393248 | tf_op jit(solution)/shard_map/ppermute | solution.py:326
  61.2 4.7 %collective-permute-done.22.y_ref = bf16[256,768]{1,0:T(8,128)(2,1)S(1)} collective-permute-done((bf16[256,768]{1,0:T(8,128)(2,1)S(1)}, bf16[256,768]{1,0:T(8,128)(2,1)S(1)}, u32[]{:S(2)}, u32[]{:S(2)}) %collective-permute-start.22) | collective-permute-done | bytes 393248 | tf_op jit(solution)/shard_map/ppermute | solution.py:309
  65.9 1.8 %collective-permute-start.24 = (bf16[256,768]{1,0:T(8,128)(2,1)S(1)}, bf16[256,768]{1,0:T(8,128)(2,1)S(1)}, u32[]{:S(2)}, u32[]{:S(2)}) collective-permute-start(bf16[256,768]{1,0:T(8,128)(2,1)S(1)} %row_grad.1.g0), channel_id=1, source_target_pairs={{0,2},{1,3},{2,0},{3,1},{4,6},{5,7},{6,4},{7,5},{8,10},{9,11},{10,... | collective-permute-start | bytes 1179656 | tf_op jit(solution)/shard_map/ppermute | solution.py:309
  67.8 8.7 %collective-permute-done.24.g2 = bf16[256,768]{1,0:T(8,128)(2,1)S(1)} collective-permute-done((bf16[256,768]{1,0:T(8,128)(2,1)S(1)}, bf16[256,768]{1,0:T(8,128)(2,1)S(1)}, u32[]{:S(2)}, u32[]{:S(2)}) %collective-permute-start.24) | collective-permute-done | bytes 393248 | tf_op jit(solution)/shard_map/ppermute | solution.py:309
  76.5 1.7 %collective-permute-done.25.g3 = bf16[256,768]{1,0:T(8,128)(2,1)S(1)} collective-permute-done((bf16[256,768]{1,0:T(8,128)(2,1)S(1)}, bf16[256,768]{1,0:T(8,128)(2,1)S(1)}, u32[]{:S(2)}, u32[]{:S(2)}) %collective-permute-start.25) | collective-permute-done | bytes 393248 | tf_op jit(solution)/shard_map/ppermute | solution.py:309
  78.2 1.0 head_grad.1
  79.2 30.4 %all_to_all.9 = bf16[64,8,768]{2,1,0:T(8,128)(2,1)S(1)} all-to-all(bf16[64,8,768]{2,1,0:T(8,128)(2,1)S(1)} %bitcast.19), channel_id=1, replica_groups=mesh['blk'=64,'rows'=4] {'blk'}, dimensions={0} | all-to-all | bytes 1572864 | tf_op jit(solution)/shard_map/all_to_all | solution.py:403
  109.5 0.7 convert_reduce_fusion
  (40 shorter events, 1.2 us)
Async XLA Ops:
  0.6 6.4 %copy-start.1 = (bf16[256,2048]{1,0:T(8,128)(2,1)S(1)}, bf16[256,2048]{1,0:T(8,128)(2,1)}, u32[]{:S(2)}) copy-start(bf16[256,2048]{1,0:T(8,128)(2,1)} %features_ref.1) | copy-start | bytes 3145732
  4.6 19.7 %copy-start.2 = (s32[1,3]{1,0:T(1,128)S(1)}, s32[1,3]{1,0:T(1,128)}, u32[]{:S(2)}) copy-start(s32[1,3]{1,0:T(1,128)} %param.10) | copy-start | bytes 40
  4.6 19.8 %copy-start = (bf16[272,768]{1,0:T(8,128)(2,1)S(1)}, bf16[272,768]{1,0:T(8,128)(2,1)}, u32[]{:S(2)}) copy-start(bf16[272,768]{1,0:T(8,128)(2,1)} %embed.1.p0.own_ref) | copy-start | bytes 1253380
  4.6 11.6 %collective-permute-start.1 = (bf16[272,768]{1,0:T(8,128)(2,1)}, bf16[272,768]{1,0:T(8,128)(2,1)S(1)}, u32[]{:S(2)}, u32[]{:S(2)}) collective-permute-start(bf16[272,768]{1,0:T(8,128)(2,1)} %embed.1.p0.own_ref), channel_id=1, source_target_pairs={{0,2},{1,3},{2,0},{3,1},{4,6},{5,7},{6,4},{7,5},{8,10},{9,11},{10,... | collective-permute-start | bytes 1253384 | tf_op jit(solution)/shard_map/ppermute | solution.py:309
  6.8 15.9 %collective-permute-start.3 = (bf16[272,768]{1,0:T(8,128)(2,1)}, bf16[272,768]{1,0:T(8,128)(2,1)S(1)}, u32[]{:S(2)}, u32[]{:S(2)}) collective-permute-start(bf16[272,768]{1,0:T(8,128)(2,1)} %embed.1.p0.own_ref), channel_id=1, source_target_pairs={{0,8},{4,12},{8,16},{12,20},{16,24},{20,28},{24,32},{28,36},{32,40... | collective-permute-start | bytes 1253384 | tf_op jit(solution)/shard_map/ppermute | solution.py:312
  7.0 18.0 %collective-permute-start = (bf16[272,768]{1,0:T(8,128)(2,1)}, bf16[272,768]{1,0:T(8,128)(2,1)S(1)}, u32[]{:S(2)}, u32[]{:S(2)}) collective-permute-start(bf16[272,768]{1,0:T(8,128)(2,1)} %embed.1.p0.own_ref), channel_id=1, source_target_pairs={{0,1},{1,0},{2,3},{3,2},{4,5},{5,4},{6,7},{7,6},{8,9},{9,8},{10,11... | collective-permute-start | bytes 1253384 | tf_op jit(solution)/shard_map/ppermute | solution.py:309
  16.2 10.6 %collective-permute-start.2 = (bf16[272,768]{1,0:T(8,128)(2,1)S(1)}, bf16[272,768]{1,0:T(8,128)(2,1)S(1)}, u32[]{:S(2)}, u32[]{:S(2)}) collective-permute-start(bf16[272,768]{1,0:T(8,128)(2,1)S(1)} %collective-permute-done.1.p2), channel_id=1, source_target_pairs={{0,1},{1,0},{2,3},{3,2},{4,5},{5,4},{6,7},{7,6},{8,9},{9,8},{10,11... | collective-permute-start | bytes 1253384 | tf_op jit(solution)/shard_map/ppermute | solution.py:309
  16.2 19.3 %collective-permute-start.7 = (bf16[512,256]{1,0:T(8,128)(2,1)}, bf16[512,256]{1,0:T(8,128)(2,1)S(1)}, u32[]{:S(2)}, u32[]{:S(2)}) collective-permute-start(bf16[512,256]{1,0:T(8,128)(2,1)} %get-tuple-element.48), channel_id=1, source_target_pairs={{0,1},{1,0},{2,3},{3,2},{4,5},{5,4},{6,7},{7,6},{8,9},{9,8},{10,11... | collective-permute-start | bytes 786440 | tf_op jit(solution)/shard_map/ppermute | solution.py:309
  16.7 18.8 %collective-permute-start.8 = (bf16[512,256]{1,0:T(8,128)(2,1)S(1)}, bf16[512,256]{1,0:T(8,128)(2,1)S(1)}, u32[]{:S(2)}, u32[]{:S(2)}) collective-permute-start(bf16[512,256]{1,0:T(8,128)(2,1)S(1)} %get-tuple-element.49), channel_id=1, source_target_pairs={{0,2},{1,3},{2,0},{3,1},{4,6},{5,7},{6,4},{7,5},{8,10},{9,11},{10,... | collective-permute-start | bytes 786440 | tf_op jit(solution)/shard_map/ppermute | solution.py:309
  22.7 12.8 %collective-permute-start.9 = (bf16[512,256]{1,0:T(8,128)(2,1)S(1)}, bf16[512,256]{1,0:T(8,128)(2,1)S(1)}, u32[]{:S(2)}, u32[]{:S(2)}) collective-permute-start(bf16[512,256]{1,0:T(8,128)(2,1)S(1)} %get-tuple-element.50), channel_id=1, source_target_pairs={{0,2},{1,3},{2,0},{3,1},{4,6},{5,7},{6,4},{7,5},{8,10},{9,11},{10,... | collective-permute-start | bytes 786440 | tf_op jit(solution)/shard_map/ppermute | solution.py:309
  25.0 13.6 %collective-permute-start.4 = (bf16[272,768]{1,0:T(8,128)(2,1)S(1)}, bf16[272,768]{1,0:T(8,128)(2,1)S(1)}, u32[]{:S(2)}, u32[]{:S(2)}) collective-permute-start(bf16[272,768]{1,0:T(8,128)(2,1)S(1)} %row_choice.1), channel_id=1, source_target_pairs={{0,6},{1,7},{2,4},{3,5},{4,2},{5,3},{6,0},{7,1},{8,14},{9,15},{10,... | collective-permute-start | bytes 1253384 | tf_op jit(solution)/shard_map/ppermute | solution.py:318
  35.5 14.2 %collective-permute-start.10 = (bf16[256,768]{1,0:T(8,128)(2,1)S(1)}, bf16[256,768]{1,0:T(8,128)(2,1)S(1)}, u32[]{:S(2)}, u32[]{:S(2)}) collective-permute-start(bf16[256,768]{1,0:T(8,128)(2,1)S(1)} %get-tuple-element.51), channel_id=1, source_target_pairs={{0,248},{4,252},{8,0},{12,4},{16,8},{20,12},{24,16},{28,20},{32,24... | collective-permute-start | bytes 1179656 | tf_op jit(solution)/shard_map/ppermute | solution.py:312
  43.3 5.9 %collective-permute-start.13 = (f32[64,768]{1,0:T(8,128)S(1)}, f32[64,768]{1,0:T(8,128)S(1)}, u32[]{:S(2)}, u32[]{:S(2)}) collective-permute-start(f32[64,768]{1,0:T(8,128)S(1)} %get-tuple-element.59), channel_id=1, source_target_pairs={{0,1},{1,0},{2,3},{3,2},{4,5},{5,4},{6,7},{7,6},{8,9},{9,8},{10,11... | collective-permute-start | bytes 589832 | tf_op jit(solution)/shard_map/ppermute | solution.py:309
  43.4 6.1 %collective-permute-start.14 = (f32[64,768]{1,0:T(8,128)S(1)}, f32[64,768]{1,0:T(8,128)S(1)}, u32[]{:S(2)}, u32[]{:S(2)}) collective-permute-start(f32[64,768]{1,0:T(8,128)S(1)} %get-tuple-element.60), channel_id=1, source_target_pairs={{0,1},{1,0},{2,3},{3,2},{4,5},{5,4},{6,7},{7,6},{8,9},{9,8},{10,11... | collective-permute-start | bytes 589832 | tf_op jit(solution)/shard_map/ppermute | solution.py:309
  43.9 3.9 %collective-permute-start.6 = (f32[8,1024]{1,0:T(8,128)S(1)}, f32[8,1024]{1,0:T(8,128)S(1)}, u32[]{:S(2)}, u32[]{:S(2)}) collective-permute-start(f32[8,1024]{1,0:T(8,128)S(1)} %get-tuple-element.45.s0), channel_id=1, source_target_pairs={{0,2},{1,3},{2,0},{3,1},{4,6},{5,7},{6,4},{7,5},{8,10},{9,11},{10,... | collective-permute-start | bytes 98312 | tf_op jit(solution)/shard_map/ppermute | solution.py:309
  45.5 8.2 %collective-permute-start.12 = (bf16[512,256]{1,0:T(8,128)(2,1)S(1)}, bf16[512,256]{1,0:T(8,128)(2,1)S(1)}, u32[]{:S(2)}, u32[]{:S(2)}) collective-permute-start(bf16[512,256]{1,0:T(8,128)(2,1)S(1)} %collective-permute-done.9), channel_id=1, source_target_pairs={{0,1},{1,0},{2,3},{3,2},{4,5},{5,4},{6,7},{7,6},{8,9},{9,8},{10,11... | collective-permute-start | bytes 786440 | tf_op jit(solution)/shard_map/ppermute | solution.py:309
  47.8 1.2 %collective-permute-start.5 = (f32[8,1024]{1,0:T(8,128)S(1)}, f32[8,1024]{1,0:T(8,128)S(1)}, u32[]{:S(2)}, u32[]{:S(2)}) collective-permute-start(f32[8,1024]{1,0:T(8,128)S(1)} %get-tuple-element.45.s0), channel_id=1, source_target_pairs={{0,1},{1,0},{2,3},{3,2},{4,5},{5,4},{6,7},{7,6},{8,9},{9,8},{10,11... | collective-permute-start | bytes 98312 | tf_op jit(solution)/shard_map/ppermute | solution.py:309
  49.0 4.1 %collective-permute-start.15 = (f32[64,768]{1,0:T(8,128)S(1)}, f32[64,768]{1,0:T(8,128)S(1)}, u32[]{:S(2)}, u32[]{:S(2)}) collective-permute-start(f32[64,768]{1,0:T(8,128)S(1)} %get-tuple-element.61), channel_id=1, source_target_pairs={{0,1},{1,0},{2,3},{3,2},{4,5},{5,4},{6,7},{7,6},{8,9},{9,8},{10,11... | collective-permute-start | bytes 589832 | tf_op jit(solution)/shard_map/ppermute | solution.py:309
  49.2 3.9 %collective-permute-start.16 = (f32[64,768]{1,0:T(8,128)S(1)}, f32[64,768]{1,0:T(8,128)S(1)}, u32[]{:S(2)}, u32[]{:S(2)}) collective-permute-start(f32[64,768]{1,0:T(8,128)S(1)} %get-tuple-element.62), channel_id=1, source_target_pairs={{0,1},{1,0},{2,3},{3,2},{4,5},{5,4},{6,7},{7,6},{8,9},{9,8},{10,11... | collective-permute-start | bytes 589832 | tf_op jit(solution)/shard_map/ppermute | solution.py:309
  49.5 4.1 %collective-permute-start.17 = (f32[64,768]{1,0:T(8,128)S(1)}, f32[64,768]{1,0:T(8,128)S(1)}, u32[]{:S(2)}, u32[]{:S(2)}) collective-permute-start(f32[64,768]{1,0:T(8,128)S(1)} %get-tuple-element.64), channel_id=1, source_target_pairs={{0,1},{1,0},{2,3},{3,2},{4,5},{5,4},{6,7},{7,6},{8,9},{9,8},{10,11... | collective-permute-start | bytes 589832 | tf_op jit(solution)/shard_map/ppermute | solution.py:309
  49.7 11.4 %collective-permute-start.21 = (bf16[256,768]{1,0:T(8,128)(2,1)S(1)}, bf16[256,768]{1,0:T(8,128)(2,1)S(1)}, u32[]{:S(2)}, u32[]{:S(2)}) collective-permute-start(bf16[256,768]{1,0:T(8,128)(2,1)S(1)} %get-tuple-element.73), channel_id=1, source_target_pairs={{0,254},{1,255},{2,252},{3,253},{4,2},{5,3},{6,0},{7,1},{8,6},{9,7... | collective-permute-start | bytes 1179656 | tf_op jit(solution)/shard_map/ppermute | solution.py:326
  53.1 1.2 %collective-permute-start.11 = (f32[8,1024]{1,0:T(8,128)S(1)}, f32[8,1024]{1,0:T(8,128)S(1)}, u32[]{:S(2)}, u32[]{:S(2)}) collective-permute-start(f32[8,1024]{1,0:T(8,128)S(1)} %collective-permute-done.6.s2), channel_id=1, source_target_pairs={{0,1},{1,0},{2,3},{3,2},{4,5},{5,4},{6,7},{7,6},{8,9},{9,8},{10,11... | collective-permute-start | bytes 98312 | tf_op jit(solution)/shard_map/ppermute | solution.py:309
  53.1 3.3 %collective-permute-start.18 = (f32[64,768]{1,0:T(8,128)S(1)}, f32[64,768]{1,0:T(8,128)S(1)}, u32[]{:S(2)}, u32[]{:S(2)}) collective-permute-start(f32[64,768]{1,0:T(8,128)S(1)} %get-tuple-element.65), channel_id=1, source_target_pairs={{0,1},{1,0},{2,3},{3,2},{4,5},{5,4},{6,7},{7,6},{8,9},{9,8},{10,11... | collective-permute-start | bytes 589832 | tf_op jit(solution)/shard_map/ppermute | solution.py:309
  53.6 2.8 %collective-permute-start.19 = (f32[64,768]{1,0:T(8,128)S(1)}, f32[64,768]{1,0:T(8,128)S(1)}, u32[]{:S(2)}, u32[]{:S(2)}) collective-permute-start(f32[64,768]{1,0:T(8,128)S(1)} %get-tuple-element.66), channel_id=1, source_target_pairs={{0,1},{1,0},{2,3},{3,2},{4,5},{5,4},{6,7},{7,6},{8,9},{9,8},{10,11... | collective-permute-start | bytes 589832 | tf_op jit(solution)/shard_map/ppermute | solution.py:309
  53.7 2.7 %collective-permute-start.20 = (f32[64,768]{1,0:T(8,128)S(1)}, f32[64,768]{1,0:T(8,128)S(1)}, u32[]{:S(2)}, u32[]{:S(2)}) collective-permute-start(f32[64,768]{1,0:T(8,128)S(1)} %get-tuple-element.67), channel_id=1, source_target_pairs={{0,1},{1,0},{2,3},{3,2},{4,5},{5,4},{6,7},{7,6},{8,9},{9,8},{10,11... | collective-permute-start | bytes 589832 | tf_op jit(solution)/shard_map/ppermute | solution.py:309
  54.3 11.5 %collective-permute-start.22 = (bf16[256,768]{1,0:T(8,128)(2,1)S(1)}, bf16[256,768]{1,0:T(8,128)(2,1)S(1)}, u32[]{:S(2)}, u32[]{:S(2)}) collective-permute-start(bf16[256,768]{1,0:T(8,128)(2,1)S(1)} %half_sum.1), channel_id=1, source_target_pairs={{0,2},{1,3},{2,0},{3,1},{4,6},{5,7},{6,4},{7,5},{8,10},{9,11},{10,... | collective-permute-start | bytes 1179656 | tf_op jit(solution)/shard_map/ppermute | solution.py:309
  65.9 10.5 %collective-permute-start.24 = (bf16[256,768]{1,0:T(8,128)(2,1)S(1)}, bf16[256,768]{1,0:T(8,128)(2,1)S(1)}, u32[]{:S(2)}, u32[]{:S(2)}) collective-permute-start(bf16[256,768]{1,0:T(8,128)(2,1)S(1)} %row_grad.1.g0), channel_id=1, source_target_pairs={{0,2},{1,3},{2,0},{3,1},{4,6},{5,7},{6,4},{7,5},{8,10},{9,11},{10,... | collective-permute-start | bytes 1179656 | tf_op jit(solution)/shard_map/ppermute | solution.py:309
  67.8 8.7 %collective-permute-start.23 = (bf16[256,768]{1,0:T(8,128)(2,1)S(1)}, bf16[256,768]{1,0:T(8,128)(2,1)S(1)}, u32[]{:S(2)}, u32[]{:S(2)}) collective-permute-start(bf16[256,768]{1,0:T(8,128)(2,1)S(1)} %row_grad.1.g0), channel_id=1, source_target_pairs={{0,1},{1,0},{2,3},{3,2},{4,5},{5,4},{6,7},{7,6},{8,9},{9,8},{10,11... | collective-permute-start | bytes 1179656 | tf_op jit(solution)/shard_map/ppermute | solution.py:309
  76.4 1.7 %collective-permute-start.25 = (bf16[256,768]{1,0:T(8,128)(2,1)S(1)}, bf16[256,768]{1,0:T(8,128)(2,1)S(1)}, u32[]{:S(2)}, u32[]{:S(2)}) collective-permute-start(bf16[256,768]{1,0:T(8,128)(2,1)S(1)} %collective-permute-done.24.g2), channel_id=1, source_target_pairs={{0,1},{1,0},{2,3},{3,2},{4,5},{5,4},{6,7},{7,6},{8,9},{9,8},{10,11... | collective-permute-start | bytes 1179656 | tf_op jit(solution)/shard_map/ppermute | solution.py:309

commit v10 on v9

--- a/solution.py
+++ b/solution.py
@@ -367,7 +367,7 @@
     s0, grad1, keep0, keep2, *sends = call(
         last_kernel,
         (scal, n1, n2, *tile, c0, c2, anchors, sums),
-        [shape(8, 4 * n), low_grad] + [shape(n, wide)] * 2 + [shape(n // 4, wide)] * 8,
+        [shape(8, 4 * n), low_grad] + [shape(n, wide)] * 2 + [shape(n // 2, wide)] * 4,
         [pltpu.VMEM((n, 4 * n), bf16), *scratch],
         name="block_before",
     )
@@ -376,14 +376,14 @@
     s1 = over_rows(s0, 1)
     sends = [over_rows(x, 1) for x in sends]
     keep2, s2, grad2 = lax.optimization_barrier((keep2, s2, grad2))
-    (half,) = call(halved_kernel, (keep2, *sends[4:]), [low_grad], name="half_sum")
+    (half,) = call(halved_kernel, (keep2, *sends[2:]), [low_grad], name="half_sum")
     own_grad, half = lax.optimization_barrier((own_grad, half))
     from_y = over_rows(half, 2)
     f3, s3 = over_rows(f3, 1), over_rows(s2, 1)
     s1, s3, f3 = lax.optimization_barrier((s1, s3, f3))
     base, anchor_loss = call(
         listed_kernel,
-        (anchors, s0, s1, s2, s3, *tile, keep0, own_grad, *sends[:4]),
+        (anchors, s0, s1, s2, s3, *tile, keep0, own_grad, *sends[:2]),
         [shape(n, wide), shape(1, n)],
         name="listed",
     )

time: 110 us -> 113 us (1.027)
  waiting for transfers between devices: 33 us -> 38.1 us
  starting transfers between devices: 21 us -> 19.6 us
    ppermute x22 -> x18, waiting for transfers between devices: 24.7 us -> 31.6 us  [over_rows(): return lax.ppermute(x, 'rows', [(i, i ^ flip) for i in range(rows_n)])]
    ppermute x1, waiting for transfers between devices: 2.61 us -> 0.06 us  [one_back(): return lax.ppermute(x, ('blk', 'rows'), pairs)]
    ppermute x22 -> x18, starting transfers between devices: 12.4 us -> 10.9 us  [over_rows(): return lax.ppermute(x, 'rows', [(i, i ^ flip) for i in range(rows_n)])]
    ppermute x2, starting transfers between devices: 3.27 us -> 1.89 us  [two_on(): return lax.ppermute(x, 'blk', [(b, (b + by) % blks) for b in range(blks)])]
  transfers between devices with their start and end apart: 26 -> 22, of which waited for: 9 -> 10; matrix products, arithmetic and copies ran while one was open for 3% -> 2% of each run, Pallas kernels for 15% -> 14%
where the time goes in v10:
time: 113 us
  waiting for transfers between devices  38.1 us (34%)
  blocking collectives  29.8 us (26%)
  Pallas kernels  21.3 us (19%)
  starting transfers between devices  19.6 us (17%)
  local copies, waits for them, and re-layouts  2.59 us (2%)
    ppermute x18, waiting for transfers between devices, over_rows(): return lax.ppermute(x, 'rows', [(i, i ^ flip) for i in range(rows_n)])  31.6 us
    all_to_all x1, blocking collectives, local(): parts = lax.all_to_all(part, 'blk', split_axis=0, concat_axis=0, tiled=True)  29.8 us
    pallas_call x8, Pallas kernels, call(): pl.pallas_call(kernel, out_shape=outs, in_specs=[SMEM if x.ndim == 1 else...  17.3 us
    ppermute x18, starting transfers between devices, over_rows(): return lax.ppermute(x, 'rows', [(i, i ^ flip) for i in range(rows_n)])  10.9 us
    ppermute x2, waiting for transfers between devices, two_on(): return lax.ppermute(x, 'blk', [(b, (b + by) % blks) for b in range(blks)])  6.43 us
    ppermute x1, starting transfers between devices, one_back(): return lax.ppermute(x, ('blk', 'rows'), pairs)  4.28 us
    pallas_call x1, Pallas kernels, embed(): pl.pallas_call(embed_kernel, grid=(wide // step,), out_shape=shape(n + ME...  4 us
    ppermute x1, starting transfers between devices, swapped(): return lax.ppermute(x, ('blk', 'rows'), pairs)  2.5 us
  transfers between devices with their start and end apart: 22, of which 10 were waited for; matrix products, arithmetic and copies ran while one was open for 2% of the time, Pallas kernels for 14%

profile of v10, /device:TPU:8, one launch (start us, length us, event | category | flops | bytes accessed | tf_op | source)
XLA Modules:
  0.0 112.9 jit_solution(7633032570524990597)
XLA Ops:
  0.6 4.0 %embed.1.p0.own_ref = bf16[272,768]{1,0:T(8,128)(2,1)} custom-call(bf16[256,2048]{1,0:T(8,128)(2,1)} %features_ref.1, bf16[2048,768]{1,0:T(8,128)(2,1)} %weight_ref.1, s32[1,256]{1,0:T(1,128)} %bitcast.22, s32[3,256]{1,0:T(4,128)} %bitcast.21, f32[1,256]{1,0:T(1,128)} %bitcast.23), custom_call_target="tpu_custom_call" | custom-call | flops 1073741824 | bytes 4194304 | tf_op jit(solution)/shard_map/embed/pallas_call | solution.py:75
  4.6 2.2 %collective-permute-start.1 = (bf16[272,768]{1,0:T(8,128)(2,1)}, bf16[272,768]{1,0:T(8,128)(2,1)S(1)}, u32[]{:S(2)}, u32[]{:S(2)}) collective-permute-start(bf16[272,768]{1,0:T(8,128)(2,1)} %embed.1.p0.own_ref), channel_id=1, source_target_pairs={{0,2},{1,3},{2,0},{3,1},{4,6},{5,7},{6,4},{7,5},{8,10},{9,11},{10,... | collective-permute-start | bytes 1253384 | tf_op jit(solution)/shard_map/ppermute | solution.py:309
  6.8 0.2 collective-permute-start.3
  7.0 1.3 %copy.12 = bf16[256,2048]{0,1:T(8,128)(2,1)} copy(bf16[256,2048]{1,0:T(8,128)(2,1)S(1)} %copy-done.1) | data formatting | bytes 2097152 | tf_op jit(solution)/shard_map/optimization_barrier | solution.py:335
  8.3 1.3 %dynamic-slice_bitcast_fusion = (bf16[512,256]{1,0:T(8,128)(2,1)S(1)}, bf16[512,256]{1,0:T(8,128)(2,1)S(1)}, bf16[512,256]{1,0:T(8,128)(2,1)S(1)}, bf16[512,256]{1,0:T(8,128)(2,1)S(1)}) fusion(bf16[64,4,8,256]{3,2,1,0:T(8,128)(2,1)} %bitcast.20, s32[]{:T(128)S(6)} %select_n.24, s32[]{:T(128)S(6)} %select_n.23, s32[]{:T(128)S(6)} %select_n.22, s32[]{:T(128)S(6)} %select_n.21), kind=kLoop, calls=%fused_computation.1 | loop fusion | bytes 2097168 | tf_op jit(solution)/shard_map/reshape | solution.py:339
  9.6 6.6 %collective-permute-done.1.p2 = bf16[272,768]{1,0:T(8,128)(2,1)S(1)} collective-permute-done((bf16[272,768]{1,0:T(8,128)(2,1)}, bf16[272,768]{1,0:T(8,128)(2,1)S(1)}, u32[]{:S(2)}, u32[]{:S(2)}) %collective-permute-start.1) | collective-permute-done | bytes 417824 | tf_op jit(solution)/shard_map/ppermute | solution.py:309
  16.3 6.4 %collective-permute-done.3.n2.other_ref = bf16[272,768]{1,0:T(8,128)(2,1)S(1)} collective-permute-done((bf16[272,768]{1,0:T(8,128)(2,1)}, bf16[272,768]{1,0:T(8,128)(2,1)S(1)}, u32[]{:S(2)}, u32[]{:S(2)}) %collective-permute-start.3) | collective-permute-done | bytes 417824 | tf_op jit(solution)/shard_map/ppermute | solution.py:312
  22.7 0.6 row_choice.1
  23.3 2.5 %collective-permute-start.4 = (bf16[272,768]{1,0:T(8,128)(2,1)S(1)}, bf16[272,768]{1,0:T(8,128)(2,1)S(1)}, u32[]{:S(2)}, u32[]{:S(2)}) collective-permute-start(bf16[272,768]{1,0:T(8,128)(2,1)S(1)} %row_choice.1), channel_id=1, source_target_pairs={{0,6},{1,7},{2,4},{3,5},{4,2},{5,3},{6,0},{7,1},{8,14},{9,15},{10,... | collective-permute-start | bytes 1253384 | tf_op jit(solution)/shard_map/ppermute | solution.py:318
  25.8 1.3 %collective-permute-start.8 = (bf16[512,256]{1,0:T(8,128)(2,1)S(1)}, bf16[512,256]{1,0:T(8,128)(2,1)S(1)}, u32[]{:S(2)}, u32[]{:S(2)}) collective-permute-start(bf16[512,256]{1,0:T(8,128)(2,1)S(1)} %get-tuple-element.45), channel_id=1, source_target_pairs={{0,2},{1,3},{2,0},{3,1},{4,6},{5,7},{6,4},{7,5},{8,10},{9,11},{10,... | collective-permute-start | bytes 786440 | tf_op jit(solution)/shard_map/ppermute | solution.py:309
  27.2 0.7 collective-permute-start.9
  27.9 8.7 %own_and_two_before.1 = (f32[8,1024]{1,0:T(8,128)S(1)}, bf16[256,1024]{1,0:T(8,128)(2,1)S(1)}, bf16[256,1024]{1,0:T(8,128)(2,1)S(1)}, f32[8,1024]{1,0:T(8,128)S(...) custom-call(s32[5]{0:T(128)S(1)} %pad_add_fusion.scal_ref, bf16[272,768]{1,0:T(8,128)(2,1)S(1)} %copy-done, ...), custom_call_target="tpu_custom_call" | custom-call | flops 1048576 | bytes 1024 | tf_op jit(solution)/shard_map/own_and_two_before/pallas_call | solution.py:25
  36.6 3.6 %collective-permute-done.9 = bf16[512,256]{1,0:T(8,128)(2,1)S(1)} collective-permute-done((bf16[512,256]{1,0:T(8,128)(2,1)S(1)}, bf16[512,256]{1,0:T(8,128)(2,1)S(1)}, u32[]{:S(2)}, u32[]{:S(2)}) %collective-permute-start.9) | collective-permute-done | bytes 262176 | tf_op jit(solution)/shard_map/ppermute | solution.py:309
  40.2 1.7 %collective-permute-start.10 = (bf16[256,768]{1,0:T(8,128)(2,1)S(1)}, bf16[256,768]{1,0:T(8,128)(2,1)S(1)}, u32[]{:S(2)}, u32[]{:S(2)}) collective-permute-start(bf16[256,768]{1,0:T(8,128)(2,1)S(1)} %get-tuple-element.47), channel_id=1, source_target_pairs={{0,248},{4,252},{8,0},{12,4},{16,8},{20,12},{24,16},{28,20},{32,24... | collective-permute-start | bytes 1179656 | tf_op jit(solution)/shard_map/ppermute | solution.py:312
  41.9 4.7 %block_before.1 = (f32[8,1024]{1,0:T(8,128)S(1)}, bf16[256,768]{1,0:T(8,128)(2,1)S(1)}, f32[256,768]{1,0:T(8,128)S(1)}, f32[256,768]{1,0:T(8,128)S(1)}, f32[128,...) custom-call(s32[5]{0:T(128)S(1)} %pad_add_fusion.scal_ref, ...), custom_call_target="tpu_custom_call" | custom-call | flops 1048576 | bytes 1024 | tf_op jit(solution)/shard_map/block_before/pallas_call | solution.py:25
  46.7 0.5 collective-permute-start.14
  47.2 1.4 %collective-permute-start.6 = (f32[8,1024]{1,0:T(8,128)S(1)}, f32[8,1024]{1,0:T(8,128)S(1)}, u32[]{:S(2)}, u32[]{:S(2)}) collective-permute-start(f32[8,1024]{1,0:T(8,128)S(1)} %get-tuple-element.41.s0), channel_id=1, source_target_pairs={{0,2},{1,3},{2,0},{3,1},{4,6},{5,7},{6,4},{7,5},{8,10},{9,11},{10,... | collective-permute-start | bytes 98312 | tf_op jit(solution)/shard_map/ppermute | solution.py:309
  48.6 2.6 %collective-permute-done.6.s2 = f32[8,1024]{1,0:T(8,128)S(1)} collective-permute-done((f32[8,1024]{1,0:T(8,128)S(1)}, f32[8,1024]{1,0:T(8,128)S(1)}, u32[]{:S(2)}, u32[]{:S(2)}) %collective-permute-start.6) | collective-permute-done | bytes 32800 | tf_op jit(solution)/shard_map/ppermute | solution.py:309
  51.1 4.3 %collective-permute-start.17 = (bf16[256,768]{1,0:T(8,128)(2,1)S(1)}, bf16[256,768]{1,0:T(8,128)(2,1)S(1)}, u32[]{:S(2)}, u32[]{:S(2)}) collective-permute-start(bf16[256,768]{1,0:T(8,128)(2,1)S(1)} %get-tuple-element.65), channel_id=1, source_target_pairs={{0,254},{1,255},{2,252},{3,253},{4,2},{5,3},{6,0},{7,1},{8,6},{9,7... | collective-permute-start | bytes 1179656 | tf_op jit(solution)/shard_map/ppermute | solution.py:326
  55.4 0.5 collective-permute-start.5
  56.0 1.0 collective-permute-done.5.s1
  57.0 2.4 %collective-permute-start.18 = (bf16[256,768]{1,0:T(8,128)(2,1)S(1)}, bf16[256,768]{1,0:T(8,128)(2,1)S(1)}, u32[]{:S(2)}, u32[]{:S(2)}) collective-permute-start(bf16[256,768]{1,0:T(8,128)(2,1)S(1)} %half_sum.1), channel_id=1, source_target_pairs={{0,2},{1,3},{2,0},{3,1},{4,6},{5,7},{6,4},{7,5},{8,10},{9,11},{10,... | collective-permute-start | bytes 1179656 | tf_op jit(solution)/shard_map/ppermute | solution.py:309
  59.4 1.2 %collective-permute-done.11.s3 = f32[8,1024]{1,0:T(8,128)S(1)} collective-permute-done((f32[8,1024]{1,0:T(8,128)S(1)}, f32[8,1024]{1,0:T(8,128)S(1)}, u32[]{:S(2)}, u32[]{:S(2)}) %collective-permute-start.11) | collective-permute-done | bytes 32800 | tf_op jit(solution)/shard_map/ppermute | solution.py:309
  60.6 2.0 %listed.1 = (f32[256,768]{1,0:T(8,128)S(1)}, f32[1,256]{1,0:T(1,128)}) custom-call(f32[8,1024]{1,0:T(8,128)S(1)} %get-tuple-element.37.anchors_ref, f32[8,1024]{1,0:T(8,128)S(1)} %get-tuple-element.41.s0, f32[8,1024]{1,0:T(8,128)S(1)} %collective-permute-done.5.s1, f32[8,1024]{1,0:T(8,128)S(1)} %collective-permute-done.6.s2, ...), custom_call_target="tpu_custom_call" | custom-call | flops 1048576 | bytes 1024 | tf_op jit(solution)/shard_map/listed/pallas_call | solution.py:25
  62.7 0.1 joined.1.base_ref
  62.8 6.0 %collective-permute-done.18.y_ref = bf16[256,768]{1,0:T(8,128)(2,1)S(1)} collective-permute-done((bf16[256,768]{1,0:T(8,128)(2,1)S(1)}, bf16[256,768]{1,0:T(8,128)(2,1)S(1)}, u32[]{:S(2)}, u32[]{:S(2)}) %collective-permute-start.18) | collective-permute-done | bytes 393248 | tf_op jit(solution)/shard_map/ppermute | solution.py:309
  68.9 1.8 %collective-permute-start.20 = (bf16[256,768]{1,0:T(8,128)(2,1)S(1)}, bf16[256,768]{1,0:T(8,128)(2,1)S(1)}, u32[]{:S(2)}, u32[]{:S(2)}) collective-permute-start(bf16[256,768]{1,0:T(8,128)(2,1)S(1)} %row_grad.1.g0), channel_id=1, source_target_pairs={{0,2},{1,3},{2,0},{3,1},{4,6},{5,7},{6,4},{7,5},{8,10},{9,11},{10,... | collective-permute-start | bytes 1179656 | tf_op jit(solution)/shard_map/ppermute | solution.py:309
  70.7 8.9 %collective-permute-done.20.g2 = bf16[256,768]{1,0:T(8,128)(2,1)S(1)} collective-permute-done((bf16[256,768]{1,0:T(8,128)(2,1)S(1)}, bf16[256,768]{1,0:T(8,128)(2,1)S(1)}, u32[]{:S(2)}, u32[]{:S(2)}) %collective-permute-start.20) | collective-permute-done | bytes 393248 | tf_op jit(solution)/shard_map/ppermute | solution.py:309
  79.6 1.7 %collective-permute-done.21.g3 = bf16[256,768]{1,0:T(8,128)(2,1)S(1)} collective-permute-done((bf16[256,768]{1,0:T(8,128)(2,1)S(1)}, bf16[256,768]{1,0:T(8,128)(2,1)S(1)}, u32[]{:S(2)}, u32[]{:S(2)}) %collective-permute-start.21) | collective-permute-done | bytes 393248 | tf_op jit(solution)/shard_map/ppermute | solution.py:309
  81.3 1.0 head_grad.1
  82.3 29.8 %all_to_all.9 = bf16[64,8,768]{2,1,0:T(8,128)(2,1)S(1)} all-to-all(bf16[64,8,768]{2,1,0:T(8,128)(2,1)S(1)} %bitcast.19), channel_id=1, replica_groups=mesh['blk'=64,'rows'=4] {'blk'}, dimensions={0} | all-to-all | bytes 1572864 | tf_op jit(solution)/shard_map/all_to_all | solution.py:403
  112.1 0.7 convert_reduce_fusion
  (32 shorter events, 0.5 us)
Async XLA Ops:
  0.6 6.4 %copy-start.1 = (bf16[256,2048]{1,0:T(8,128)(2,1)S(1)}, bf16[256,2048]{1,0:T(8,128)(2,1)}, u32[]{:S(2)}) copy-start(bf16[256,2048]{1,0:T(8,128)(2,1)} %features_ref.1) | copy-start | bytes 3145732
  4.6 11.6 %copy-start.2 = (s32[1,3]{1,0:T(1,128)S(1)}, s32[1,3]{1,0:T(1,128)}, u32[]{:S(2)}) copy-start(s32[1,3]{1,0:T(1,128)} %param.10) | copy-start | bytes 40
  4.6 18.1 %copy-start = (bf16[272,768]{1,0:T(8,128)(2,1)S(1)}, bf16[272,768]{1,0:T(8,128)(2,1)}, u32[]{:S(2)}) copy-start(bf16[272,768]{1,0:T(8,128)(2,1)} %embed.1.p0.own_ref) | copy-start | bytes 1253380
  4.6 11.6 %collective-permute-start.1 = (bf16[272,768]{1,0:T(8,128)(2,1)}, bf16[272,768]{1,0:T(8,128)(2,1)S(1)}, u32[]{:S(2)}, u32[]{:S(2)}) collective-permute-start(bf16[272,768]{1,0:T(8,128)(2,1)} %embed.1.p0.own_ref), channel_id=1, source_target_pairs={{0,2},{1,3},{2,0},{3,1},{4,6},{5,7},{6,4},{7,5},{8,10},{9,11},{10,... | collective-permute-start | bytes 1253384 | tf_op jit(solution)/shard_map/ppermute | solution.py:309
  6.8 15.9 %collective-permute-start.3 = (bf16[272,768]{1,0:T(8,128)(2,1)}, bf16[272,768]{1,0:T(8,128)(2,1)S(1)}, u32[]{:S(2)}, u32[]{:S(2)}) collective-permute-start(bf16[272,768]{1,0:T(8,128)(2,1)} %embed.1.p0.own_ref), channel_id=1, source_target_pairs={{0,8},{4,12},{8,16},{12,20},{16,24},{20,28},{24,32},{28,36},{32,40... | collective-permute-start | bytes 1253384 | tf_op jit(solution)/shard_map/ppermute | solution.py:312
  7.0 20.2 %collective-permute-start = (bf16[272,768]{1,0:T(8,128)(2,1)}, bf16[272,768]{1,0:T(8,128)(2,1)S(1)}, u32[]{:S(2)}, u32[]{:S(2)}) collective-permute-start(bf16[272,768]{1,0:T(8,128)(2,1)} %embed.1.p0.own_ref), channel_id=1, source_target_pairs={{0,1},{1,0},{2,3},{3,2},{4,5},{5,4},{6,7},{7,6},{8,9},{9,8},{10,11... | collective-permute-start | bytes 1253384 | tf_op jit(solution)/shard_map/ppermute | solution.py:309
  16.2 11.6 %collective-permute-start.2 = (bf16[272,768]{1,0:T(8,128)(2,1)S(1)}, bf16[272,768]{1,0:T(8,128)(2,1)S(1)}, u32[]{:S(2)}, u32[]{:S(2)}) collective-permute-start(bf16[272,768]{1,0:T(8,128)(2,1)S(1)} %collective-permute-done.1.p2), channel_id=1, source_target_pairs={{0,1},{1,0},{2,3},{3,2},{4,5},{5,4},{6,7},{7,6},{8,9},{9,8},{10,11... | collective-permute-start | bytes 1253384 | tf_op jit(solution)/shard_map/ppermute | solution.py:309
  23.3 18.6 %collective-permute-start.4 = (bf16[272,768]{1,0:T(8,128)(2,1)S(1)}, bf16[272,768]{1,0:T(8,128)(2,1)S(1)}, u32[]{:S(2)}, u32[]{:S(2)}) collective-permute-start(bf16[272,768]{1,0:T(8,128)(2,1)S(1)} %row_choice.1), channel_id=1, source_target_pairs={{0,6},{1,7},{2,4},{3,5},{4,2},{5,3},{6,0},{7,1},{8,14},{9,15},{10,... | collective-permute-start | bytes 1253384 | tf_op jit(solution)/shard_map/ppermute | solution.py:318
  25.8 10.7 %collective-permute-start.7 = (bf16[512,256]{1,0:T(8,128)(2,1)S(1)}, bf16[512,256]{1,0:T(8,128)(2,1)S(1)}, u32[]{:S(2)}, u32[]{:S(2)}) collective-permute-start(bf16[512,256]{1,0:T(8,128)(2,1)S(1)} %get-tuple-element.44), channel_id=1, source_target_pairs={{0,1},{1,0},{2,3},{3,2},{4,5},{5,4},{6,7},{7,6},{8,9},{9,8},{10,11... | collective-permute-start | bytes 786440 | tf_op jit(solution)/shard_map/ppermute | solution.py:309
  25.8 10.8 %collective-permute-start.8 = (bf16[512,256]{1,0:T(8,128)(2,1)S(1)}, bf16[512,256]{1,0:T(8,128)(2,1)S(1)}, u32[]{:S(2)}, u32[]{:S(2)}) collective-permute-start(bf16[512,256]{1,0:T(8,128)(2,1)S(1)} %get-tuple-element.45), channel_id=1, source_target_pairs={{0,2},{1,3},{2,0},{3,1},{4,6},{5,7},{6,4},{7,5},{8,10},{9,11},{10,... | collective-permute-start | bytes 786440 | tf_op jit(solution)/shard_map/ppermute | solution.py:309
  27.2 13.0 %collective-permute-start.9 = (bf16[512,256]{1,0:T(8,128)(2,1)S(1)}, bf16[512,256]{1,0:T(8,128)(2,1)S(1)}, u32[]{:S(2)}, u32[]{:S(2)}) collective-permute-start(bf16[512,256]{1,0:T(8,128)(2,1)S(1)} %get-tuple-element.46), channel_id=1, source_target_pairs={{0,2},{1,3},{2,0},{3,1},{4,6},{5,7},{6,4},{7,5},{8,10},{9,11},{10,... | collective-permute-start | bytes 786440 | tf_op jit(solution)/shard_map/ppermute | solution.py:309
  40.2 11.0 %collective-permute-start.10 = (bf16[256,768]{1,0:T(8,128)(2,1)S(1)}, bf16[256,768]{1,0:T(8,128)(2,1)S(1)}, u32[]{:S(2)}, u32[]{:S(2)}) collective-permute-start(bf16[256,768]{1,0:T(8,128)(2,1)S(1)} %get-tuple-element.47), channel_id=1, source_target_pairs={{0,248},{4,252},{8,0},{12,4},{16,8},{20,12},{24,16},{28,20},{32,24... | collective-permute-start | bytes 1179656 | tf_op jit(solution)/shard_map/ppermute | solution.py:312
  46.6 8.8 %collective-permute-start.13 = (f32[128,768]{1,0:T(8,128)S(1)}, f32[128,768]{1,0:T(8,128)S(1)}, u32[]{:S(2)}, u32[]{:S(2)}) collective-permute-start(f32[128,768]{1,0:T(8,128)S(1)} %get-tuple-element.55), channel_id=1, source_target_pairs={{0,1},{1,0},{2,3},{3,2},{4,5},{5,4},{6,7},{7,6},{8,9},{9,8},{10,11... | collective-permute-start | bytes 1179656 | tf_op jit(solution)/shard_map/ppermute | solution.py:309
  46.7 8.7 %collective-permute-start.14 = (f32[128,768]{1,0:T(8,128)S(1)}, f32[128,768]{1,0:T(8,128)S(1)}, u32[]{:S(2)}, u32[]{:S(2)}) collective-permute-start(f32[128,768]{1,0:T(8,128)S(1)} %get-tuple-element.56), channel_id=1, source_target_pairs={{0,1},{1,0},{2,3},{3,2},{4,5},{5,4},{6,7},{7,6},{8,9},{9,8},{10,11... | collective-permute-start | bytes 1179656 | tf_op jit(solution)/shard_map/ppermute | solution.py:309
  47.2 3.9 %collective-permute-start.6 = (f32[8,1024]{1,0:T(8,128)S(1)}, f32[8,1024]{1,0:T(8,128)S(1)}, u32[]{:S(2)}, u32[]{:S(2)}) collective-permute-start(f32[8,1024]{1,0:T(8,128)S(1)} %get-tuple-element.41.s0), channel_id=1, source_target_pairs={{0,2},{1,3},{2,0},{3,1},{4,6},{5,7},{6,4},{7,5},{8,10},{9,11},{10,... | collective-permute-start | bytes 98312 | tf_op jit(solution)/shard_map/ppermute | solution.py:309
  48.6 12.0 %collective-permute-start.15 = (f32[128,768]{1,0:T(8,128)S(1)}, f32[128,768]{1,0:T(8,128)S(1)}, u32[]{:S(2)}, u32[]{:S(2)}) collective-permute-start(f32[128,768]{1,0:T(8,128)S(1)} %get-tuple-element.58), channel_id=1, source_target_pairs={{0,1},{1,0},{2,3},{3,2},{4,5},{5,4},{6,7},{7,6},{8,9},{9,8},{10,11... | collective-permute-start | bytes 1179656 | tf_op jit(solution)/shard_map/ppermute | solution.py:309
  51.1 9.5 %collective-permute-start.16 = (f32[128,768]{1,0:T(8,128)S(1)}, f32[128,768]{1,0:T(8,128)S(1)}, u32[]{:S(2)}, u32[]{:S(2)}) collective-permute-start(f32[128,768]{1,0:T(8,128)S(1)} %get-tuple-element.59), channel_id=1, source_target_pairs={{0,1},{1,0},{2,3},{3,2},{4,5},{5,4},{6,7},{7,6},{8,9},{9,8},{10,11... | collective-permute-start | bytes 1179656 | tf_op jit(solution)/shard_map/ppermute | solution.py:309
  51.1 11.6 %collective-permute-start.17 = (bf16[256,768]{1,0:T(8,128)(2,1)S(1)}, bf16[256,768]{1,0:T(8,128)(2,1)S(1)}, u32[]{:S(2)}, u32[]{:S(2)}) collective-permute-start(bf16[256,768]{1,0:T(8,128)(2,1)S(1)} %get-tuple-element.65), channel_id=1, source_target_pairs={{0,254},{1,255},{2,252},{3,253},{4,2},{5,3},{6,0},{7,1},{8,6},{9,7... | collective-permute-start | bytes 1179656 | tf_op jit(solution)/shard_map/ppermute | solution.py:326
  55.4 4.0 %collective-permute-start.12 = (bf16[512,256]{1,0:T(8,128)(2,1)S(1)}, bf16[512,256]{1,0:T(8,128)(2,1)S(1)}, u32[]{:S(2)}, u32[]{:S(2)}) collective-permute-start(bf16[512,256]{1,0:T(8,128)(2,1)S(1)} %collective-permute-done.9), channel_id=1, source_target_pairs={{0,1},{1,0},{2,3},{3,2},{4,5},{5,4},{6,7},{7,6},{8,9},{9,8},{10,11... | collective-permute-start | bytes 786440 | tf_op jit(solution)/shard_map/ppermute | solution.py:309
  55.4 1.6 %collective-permute-start.5 = (f32[8,1024]{1,0:T(8,128)S(1)}, f32[8,1024]{1,0:T(8,128)S(1)}, u32[]{:S(2)}, u32[]{:S(2)}) collective-permute-start(f32[8,1024]{1,0:T(8,128)S(1)} %get-tuple-element.41.s0), channel_id=1, source_target_pairs={{0,1},{1,0},{2,3},{3,2},{4,5},{5,4},{6,7},{7,6},{8,9},{9,8},{10,11... | collective-permute-start | bytes 98312 | tf_op jit(solution)/shard_map/ppermute | solution.py:309
  57.0 11.8 %collective-permute-start.18 = (bf16[256,768]{1,0:T(8,128)(2,1)S(1)}, bf16[256,768]{1,0:T(8,128)(2,1)S(1)}, u32[]{:S(2)}, u32[]{:S(2)}) collective-permute-start(bf16[256,768]{1,0:T(8,128)(2,1)S(1)} %half_sum.1), channel_id=1, source_target_pairs={{0,2},{1,3},{2,0},{3,1},{4,6},{5,7},{6,4},{7,5},{8,10},{9,11},{10,... | collective-permute-start | bytes 1179656 | tf_op jit(solution)/shard_map/ppermute | solution.py:309
  59.4 1.2 %collective-permute-start.11 = (f32[8,1024]{1,0:T(8,128)S(1)}, f32[8,1024]{1,0:T(8,128)S(1)}, u32[]{:S(2)}, u32[]{:S(2)}) collective-permute-start(f32[8,1024]{1,0:T(8,128)S(1)} %collective-permute-done.6.s2), channel_id=1, source_target_pairs={{0,1},{1,0},{2,3},{3,2},{4,5},{5,4},{6,7},{7,6},{8,9},{9,8},{10,11... | collective-permute-start | bytes 98312 | tf_op jit(solution)/shard_map/ppermute | solution.py:309
  68.9 10.7 %collective-permute-start.20 = (bf16[256,768]{1,0:T(8,128)(2,1)S(1)}, bf16[256,768]{1,0:T(8,128)(2,1)S(1)}, u32[]{:S(2)}, u32[]{:S(2)}) collective-permute-start(bf16[256,768]{1,0:T(8,128)(2,1)S(1)} %row_grad.1.g0), channel_id=1, source_target_pairs={{0,2},{1,3},{2,0},{3,1},{4,6},{5,7},{6,4},{7,5},{8,10},{9,11},{10,... | collective-permute-start | bytes 1179656 | tf_op jit(solution)/shard_map/ppermute | solution.py:309
  70.7 8.9 %collective-permute-start.19 = (bf16[256,768]{1,0:T(8,128)(2,1)S(1)}, bf16[256,768]{1,0:T(8,128)(2,1)S(1)}, u32[]{:S(2)}, u32[]{:S(2)}) collective-permute-start(bf16[256,768]{1,0:T(8,128)(2,1)S(1)} %row_grad.1.g0), channel_id=1, source_target_pairs={{0,1},{1,0},{2,3},{3,2},{4,5},{5,4},{6,7},{7,6},{8,9},{9,8},{10,11... | collective-permute-start | bytes 1179656 | tf_op jit(solution)/shard_map/ppermute | solution.py:309
  79.6 1.7 %collective-permute-start.21 = (bf16[256,768]{1,0:T(8,128)(2,1)S(1)}, bf16[256,768]{1,0:T(8,128)(2,1)S(1)}, u32[]{:S(2)}, u32[]{:S(2)}) collective-permute-start(bf16[256,768]{1,0:T(8,128)(2,1)S(1)} %collective-permute-done.20.g2), channel_id=1, source_target_pairs={{0,1},{1,0},{2,3},{3,2},{4,5},{5,4},{6,7},{7,6},{8,9},{9,8},{10,11... | collective-permute-start | bytes 1179656 | tf_op jit(solution)/shard_map/ppermute | solution.py:309
